TPU v7x, 512 devices: a whole 4x8x8 slice. The times are simulated.
512 devices in a mesh: grp: 4 (over x), comp: 32 (over y, z_lo, core), tp: 4 (over z_hi).
Axes of the slice: x: 4, y: 8, z: 8 (z_hi: 4, z_lo: 2; z = z_hi * 2 + z_lo), core: 2. Of those that a mesh axis runs over, the one named last changes fastest.
Arguments:
- queries: bfloat16 [65536, 2560], P(('grp', 'comp'), 'tp'), parts along dimension 0, may hold values from -7 to 7
- comp_keys: bfloat16 [65536, 512], P(('grp', 'comp'), 'tp'), parts along dimension 0, may hold values from -4 to 4
- comp_values: bfloat16 [65536, 512], P(('grp', 'comp'), 'tp'), parts along dimension 0, may hold values from -4 to 4
- out_grad: bfloat16 [65536, 2560], P(('grp', 'comp'), 'tp'), parts along dimension 0, may hold values from -24 to 24
- prompt_keys: bfloat16 [4096, 512], P(('grp', 'comp'), 'tp'), parts along dimension 0, may hold values from -4 to 4
- prompt_values: bfloat16 [4096, 512], P(('grp', 'comp'), 'tp'), parts along dimension 0, may hold values from -4 to 4
- lengths: int32 [128], P(('grp', 'comp')), parts along dimension 0, may hold values from 1 to 4, as said below
Outputs:
- grad_queries: float32 [65536, 2560], P(('grp', 'comp'), 'tp'), parts along dimension 0
- grad_prompt_keys: float32 [4096, 512], P(('grp', 'comp'), 'tp'), parts along dimension 0
- grad_prompt_values: float32 [4096, 512], P(('grp', 'comp'), 'tp'), parts along dimension 0
- grad_comp_keys: float32 [65536, 512], P(('grp', 'comp'), 'tp'), parts along dimension 0
- grad_comp_values: float32 [65536, 512], P(('grp', 'comp'), 'tp'), parts along dimension 0
There are 4 independent parts, one for each index of `grp`. A program takes and returns all parts, laid end to end along the dimension named above; each array names one. Nothing has to cross between parts.
Inputs may be any that keep to these rules, and one draw needn't show every extreme that they name: `lengths`: in every draw one completion has exactly 4 blocks.
All inputs are finite; a program needn't handle non-finite values.
Results may differ from a plain program's by a relative error of at most 0.011.
Values may be sent and summed in bfloat16 or wider, within the bound.
No kernel may reach another device: no remote copies, remote signals or barrier semaphores. Data moves between devices by JAX's collectives and lax.ppermute only.
A program may use at most 64 MiB of HBM per device.

v0:
```python
import jax
import jax.numpy as jnp
from jax import lax
from jax.sharding import PartitionSpec as P

HD = 128
BLK = 128
MAXLEN = 512


def per_device(queries, comp_keys, comp_values, out_grad, prompt_keys, prompt_values, lengths):
    keys_whole, values_whole = (
        lax.all_gather(prompt_keys, "comp", axis=0, tiled=True),
        lax.all_gather(prompt_values, "comp", axis=0, tiled=True),
    )
    seq_length = queries.shape[0]
    prompt_length = keys_whole.shape[0]
    kv_heads = comp_keys.shape[1] // HD
    group_size = queries.shape[1] // HD // kv_heads
    softmax_scale = HD ** (-0.5)
    live_rows = (jnp.arange(MAXLEN, dtype=jnp.int32)[None, :] < BLK * lengths[:, None]).reshape(
        seq_length
    )
    masked = out_grad * live_rows[:, None].astype(jnp.bfloat16)
    positions = jnp.arange(seq_length)
    same_member = positions[:, None] // MAXLEN == positions[None, :] // MAXLEN
    causal = jnp.logical_and(same_member, positions[:, None] >= positions[None, :])
    query_grads = []
    saved_stats = []
    prompt_kgrad = jnp.zeros((prompt_length, HD), jnp.float32)
    prompt_vgrad = jnp.zeros((prompt_length, HD), jnp.float32)
    own_kgrad = jnp.zeros((seq_length, HD), jnp.float32)
    own_vgrad = jnp.zeros((seq_length, HD), jnp.float32)
    for member in range(group_size):
        query_head = queries[:, member * HD : (member + 1) * HD]
        grad_head = masked[:, member * HD : (member + 1) * HD]
        prompt_scores = (
            jnp.dot(query_head, keys_whole.T, preferred_element_type=jnp.float32) * softmax_scale
        )
        own_scores = jnp.where(
            causal,
            jnp.dot(query_head, comp_keys.T, preferred_element_type=jnp.float32) * softmax_scale,
            -jnp.inf,
        )
        row_max = jnp.maximum(jnp.max(prompt_scores, 1), jnp.max(own_scores, 1))
        row_total = jnp.sum(jnp.exp(prompt_scores - row_max[:, None]), 1) + jnp.sum(
            jnp.exp(own_scores - row_max[:, None]), 1
        )
        log_total = row_max + jnp.log(row_total)
        prompt_prob = jnp.exp(prompt_scores - log_total[:, None])
        own_prob = jnp.exp(own_scores - log_total[:, None])
        prompt_half = prompt_prob.astype(jnp.bfloat16)
        own_half = own_prob.astype(jnp.bfloat16)
        attended = jnp.dot(prompt_half, values_whole, preferred_element_type=jnp.float32) + jnp.dot(
            own_half, comp_values, preferred_element_type=jnp.float32
        )
        row_delta = jnp.sum(grad_head.astype(jnp.float32) * attended, 1)
        prompt_dprob = jnp.dot(grad_head, values_whole.T, preferred_element_type=jnp.float32)
        own_dprob = jnp.dot(grad_head, comp_values.T, preferred_element_type=jnp.float32)
        prompt_dscore = (prompt_prob * (prompt_dprob - row_delta[:, None])).astype(jnp.bfloat16)
        own_dscore = (own_prob * (own_dprob - row_delta[:, None])).astype(jnp.bfloat16)
        query_grads.append(
            softmax_scale
            * (
                jnp.dot(prompt_dscore, keys_whole, preferred_element_type=jnp.float32)
                + jnp.dot(own_dscore, comp_keys, preferred_element_type=jnp.float32)
            )
        )
        prompt_kgrad = prompt_kgrad + softmax_scale * jnp.dot(
            prompt_dscore.T, query_head, preferred_element_type=jnp.float32
        )
        prompt_vgrad = prompt_vgrad + jnp.dot(
            prompt_half.T, grad_head, preferred_element_type=jnp.float32
        )
        own_kgrad = own_kgrad + softmax_scale * jnp.dot(
            own_dscore.T, query_head, preferred_element_type=jnp.float32
        )
        own_vgrad = own_vgrad + jnp.dot(own_half.T, grad_head, preferred_element_type=jnp.float32)
        saved_stats.append((log_total, row_delta))
    grad_queries = jnp.concatenate(query_grads, 1)
    grad_prompt_keys, grad_prompt_values = (
        lax.psum_scatter(prompt_kgrad, "comp", scatter_dimension=0, tiled=True),
        lax.psum_scatter(prompt_vgrad, "comp", scatter_dimension=0, tiled=True),
    )
    return (grad_queries, grad_prompt_keys, grad_prompt_values, own_kgrad, own_vgrad)


def solution(mesh):
    placed = (
        P(("grp", "comp"), "tp"),
        P(("grp", "comp"), "tp"),
        P(("grp", "comp"), "tp"),
        P(("grp", "comp"), "tp"),
        P(("grp", "comp"), "tp"),
        P(("grp", "comp"), "tp"),
        P(("grp", "comp")),
    )
    return jax.shard_map(
        per_device,
        mesh=mesh,
        in_specs=placed,
        out_specs=(
            P(("grp", "comp"), "tp"),
            P(("grp", "comp"), "tp"),
            P(("grp", "comp"), "tp"),
            P(("grp", "comp"), "tp"),
            P(("grp", "comp"), "tp"),
        ),
        check_vma=False,
    )
```

profile of v0, /device:TPU:6, one launch (start us, length us, event | category | flops | bytes accessed | tf_op | source)
XLA Modules:
  0.0 324.6 jit_solution(13259389224969478431)
XLA Ops:
  7.2 36.6 %all_gather.6 = bf16[1024,128]{1,0:T(8,128)(2,1)S(1)} all-gather(bf16[32,128]{1,0:T(8,128)(2,1)} %param.11), channel_id=1, replica_groups=mesh['grp'=4,'comp'=32,'tp'=4] {'comp'}, dimensions={0}, use_global_device_ids=true | all-gather | bytes 270336 | tf_op jit(solution)/shard_map/all_gather | solution.py:13
  43.8 1.4 multiply_reduce_fusion.4
  45.2 2.8 multiply_reduce_fusion.3
  48.0 1.2 fusion.126
  50.2 2.3 multiply_reduce_fusion.2
  52.5 1.9 fusion.128
  54.4 2.3 multiply_reduce_fusion.1
  56.7 2.0 fusion.129
  58.7 1.8 multiply_reduce_fusion
  60.5 1.9 fusion.130
  63.6 2.2 copy.12
  67.3 2.1 exponential_reduce_fusion.3
  77.0 1.5 convolution_add_fusion
  78.5 31.6 %all_gather.7 = bf16[1024,128]{1,0:T(8,128)(2,1)S(1)} all-gather(bf16[32,128]{1,0:T(8,128)(2,1)S(1)} %copy-done.63), channel_id=1, replica_groups=mesh['grp'=4,'comp'=32,'tp'=4] {'comp'}, dimensions={0}, use_global_device_ids=true | all-gather | bytes 270336 | tf_op jit(solution)/shard_map/all_gather | solution.py:14
  110.1 2.3 fusion.121
  126.4 1.3 fusion.20
  132.5 1.2 fusion.135
  133.8 1.4 fusion.134
  141.2 2.2 fusion.23
  143.4 2.1 fusion.26
  145.5 2.0 fusion.29
  149.5 2.8 copy.23
  154.9 42.8 %reduce-scatter.5.cloned.1.call-done = f32[32,128]{1,0:T(8,128)} async-done(((f32[1024,128]{1,0:T(8,128)}), f32[32,128]{1,0:T(8,128)}) %reduce-scatter.5.cloned.1.call-update) | async-done | bytes 16400 | tf_op jit(solution)/shard_map/reduce_scatter | solution.py:83
  197.7 120.1 %reduce-scatter.3.cloned.1.call-done = f32[32,128]{1,0:T(8,128)} async-done(((f32[1024,128]{1,0:T(8,128)}), f32[32,128]{1,0:T(8,128)}) %reduce-scatter.3.cloned.1.call-update) | async-done | bytes 16400 | tf_op jit(solution)/shard_map/reduce_scatter | solution.py:82
  (210 shorter events, 39.2 us)
Async XLA Ops:
  7.2 40.8 %copy-start = (bf16[512,128]{1,0:T(8,128)(2,1)S(1)}, bf16[512,128]{1,0:T(8,128)(2,1)}, u32[]{:S(2)}) copy-start(bf16[512,128]{1,0:T(8,128)(2,1)} %param.8) | copy-start | bytes 393220
  7.2 190.5 %reduce-scatter.5.cloned.1.call-start = ((), (), s32[]{:S(2)}) async-start(), calls=%async_computation.3 | async-start | bytes 540672 | tf_op jit(solution)/shard_map/reduce_scatter | solution.py:83
  45.2 4.0 %copy-start.38 = (bf16[512,640]{1,0:T(8,128)(2,1)S(1)}, bf16[512,640]{1,0:T(8,128)(2,1)}, u32[]{:S(2)}) copy-start(bf16[512,640]{1,0:T(8,128)(2,1)} %param.7) | copy-start | bytes 1966084
  49.2 14.2 %copy-start.23 = (f32[512,512]{0,1:T(8,128)}, f32[512,512]{0,1:T(8,128)S(1)}, u32[]{:S(2)}) copy-start(f32[512,512]{0,1:T(8,128)S(1)} %get-tuple-element.13) | copy-start | bytes 3145732
  50.2 19.3 %copy-start.9 = (f32[512,512]{0,1:T(8,128)}, f32[512,512]{0,1:T(8,128)S(1)}, u32[]{:S(2)}) copy-start(f32[512,512]{0,1:T(8,128)S(1)} %get-tuple-element.17) | copy-start | bytes 3145732
  65.8 3.8 %copy-start.65 = (f32[512]{0:T(512)S(1)}, f32[512]{0:T(512)}, u32[]{:S(2)}) copy-start(f32[512]{0:T(512)} %get-tuple-element.18) | copy-start | bytes 6148
  65.8 3.8 %copy-start.69 = (f32[512]{0:T(512)S(1)}, f32[512]{0:T(512)}, u32[]{:S(2)}) copy-start(f32[512]{0:T(512)} %get-tuple-element.20) | copy-start | bytes 6148
  65.8 3.9 %copy-start.3 = (f32[512,1024]{1,0:T(8,128)S(1)}, f32[512,1024]{1,0:T(8,128)}, u32[]{:S(2)}) copy-start(f32[512,1024]{1,0:T(8,128)} %get-tuple-element.19) | copy-start | bytes 6291460
  73.6 47.8 %copy-start.52 = (f32[512]{0:T(512)}, f32[512]{0:T(512)S(1)}, u32[]{:S(2)}) copy-start(f32[512]{0:T(512)S(1)} %log_add_fusion.1) | copy-start | bytes 6148
  78.5 239.3 %reduce-scatter.3.cloned.1.call-start = ((), (), s32[]{:S(2)}) async-start(), calls=%async_computation.2 | async-start | bytes 540672 | tf_op jit(solution)/shard_map/reduce_scatter | solution.py:82
  118.7 3.5 %copy-start.30 = (bf16[512,1024]{1,0:T(8,128)(2,1)}, bf16[512,1024]{1,0:T(8,128)(2,1)S(1)}, u32[]{:S(2)}) copy-start(bf16[512,1024]{1,0:T(8,128)(2,1)S(1)} %multiply_convert_fusion.3) | copy-start | bytes 3145732
  129.2 9.8 %copy-start.43 = (bf16[512,512]{0,1:T(8,128)(2,1)}, bf16[512,512]{0,1:T(8,128)(2,1)S(1)}, u32[]{:S(2)}) copy-start(bf16[512,512]{0,1:T(8,128)(2,1)S(1)} %fusion.18) | copy-start | bytes 1572868
  130.4 8.3 %copy-start.47 = (bf16[512,512]{0,1:T(8,128)(2,1)}, bf16[512,512]{0,1:T(8,128)(2,1)S(1)}, u32[]{:S(2)}) copy-start(bf16[512,512]{0,1:T(8,128)(2,1)S(1)} %fusion.19) | copy-start | bytes 1572868
  130.8 8.6 %copy-start.46 = (bf16[512,512]{0,1:T(8,128)(2,1)}, bf16[512,512]{0,1:T(8,128)(2,1)S(1)}, u32[]{:S(2)}) copy-start(bf16[512,512]{0,1:T(8,128)(2,1)S(1)} %fusion.17) | copy-start | bytes 1572868
  132.1 7.6 %copy-start.44 = (bf16[512,512]{0,1:T(8,128)(2,1)}, bf16[512,512]{0,1:T(8,128)(2,1)S(1)}, u32[]{:S(2)}) copy-start(bf16[512,512]{0,1:T(8,128)(2,1)S(1)} %fusion.16) | copy-start | bytes 1572868
  132.4 7.6 %copy-start.41 = (bf16[512,512]{0,1:T(8,128)(2,1)}, bf16[512,512]{0,1:T(8,128)(2,1)S(1)}, u32[]{:S(2)}) copy-start(bf16[512,512]{0,1:T(8,128)(2,1)S(1)} %fusion.15) | copy-start | bytes 1572868
  132.5 3.9 %copy-start.31 = (bf16[512,1024]{1,0:T(8,128)(2,1)S(1)}, bf16[512,1024]{1,0:T(8,128)(2,1)}, u32[]{:S(2)}) copy-start(bf16[512,1024]{1,0:T(8,128)(2,1)} %copy-done.30) | copy-start | bytes 3145732
  133.8 3.8 %copy-start.29 = (bf16[512,1024]{1,0:T(8,128)(2,1)S(1)}, bf16[512,1024]{1,0:T(8,128)(2,1)}, u32[]{:S(2)}) copy-start(bf16[512,1024]{1,0:T(8,128)(2,1)} %copy-done.28) | copy-start | bytes 3145732
  135.2 3.6 %copy-start.40 = (bf16[512,640]{1,0:T(8,128)(2,1)S(1)}, bf16[512,640]{1,0:T(8,128)(2,1)}, u32[]{:S(2)}) copy-start(bf16[512,640]{1,0:T(8,128)(2,1)} %param.7) | copy-start | bytes 1966084
  141.2 4.3 %copy-start.51 = (f32[512,128]{0,1:T(8,128)S(1)}, f32[512,128]{0,1:T(8,128)}, u32[]{:S(2)}) copy-start(f32[512,128]{0,1:T(8,128)} %fusion.133) | copy-start | bytes 786436
  141.2 6.3 %copy-start.45 = (bf16[512,512]{0,1:T(8,128)(2,1)S(1)}, bf16[512,512]{0,1:T(8,128)(2,1)}, u32[]{:S(2)}) copy-start(bf16[512,512]{0,1:T(8,128)(2,1)} %copy-done.44) | copy-start | bytes 1572868
  141.2 6.3 %copy-start.50 = (f32[512,128]{0,1:T(8,128)S(1)}, f32[512,128]{0,1:T(8,128)}, u32[]{:S(2)}) copy-start(f32[512,128]{0,1:T(8,128)} %fusion.134) | copy-start | bytes 786436
  141.2 7.3 %copy-start.42 = (bf16[512,512]{0,1:T(8,128)(2,1)S(1)}, bf16[512,512]{0,1:T(8,128)(2,1)}, u32[]{:S(2)}) copy-start(bf16[512,512]{0,1:T(8,128)(2,1)} %copy-done.41) | copy-start | bytes 1572868
  141.2 7.3 %copy-start.49 = (f32[512,128]{0,1:T(8,128)S(1)}, f32[512,128]{0,1:T(8,128)}, u32[]{:S(2)}) copy-start(f32[512,128]{0,1:T(8,128)} %fusion.135) | copy-start | bytes 786436
  (48 other events, 80.9 us)
Sparse Core Ops, SparseCore 0:
  78.6 119.0 reduce-scatter.4
  201.3 116.4 reduce-scatter.2
where the time goes:
time: 325 us
  waiting for transfers between devices  163 us (50%)
  blocking collectives  68.2 us (21%)
  matrix products  57.1 us (18%)
  between operations  15.8 us (5%)
  local copies, waits for them, and re-layouts  14.2 us (4%)
  other arithmetic  6.46 us (2%)
    reduce_scatter x1, waiting for transfers between devices, per_device(): lax.psum_scatter(prompt_kgrad, 'comp', scatter_dimension=0, tiled=True)  120 us
    reduce_scatter x1, waiting for transfers between devices, per_device(): lax.psum_scatter(prompt_vgrad, 'comp', scatter_dimension=0, tiled=True)  42.8 us
    all_gather x1, blocking collectives, per_device(): lax.all_gather(prompt_keys, 'comp', axis=0, tiled=True)  36.6 us
    all_gather x1, blocking collectives, per_device(): lax.all_gather(prompt_values, 'comp', axis=0, tiled=True)  31.6 us
    unnamed x143, local copies, waits for them, and re-layouts  14.2 us
    dot_general x5, matrix products, per_device(): jnp.dot(query_head, keys_whole.T, preferred_element_type=jnp.float32)  10.6 us
    dot_general x5, matrix products, per_device(): jnp.dot(own_dscore, comp_keys, preferred_element_type=jnp.float32)  8.25 us
    dot_general x5, matrix products, per_device(): jnp.dot(query_head, comp_keys.T, preferred_element_type=jnp.float32)  7.87 us
  transfers between devices with their start and end apart: 2, of which 2 were waited for; matrix products, arithmetic and copies ran while one was open for 12% of the time, Pallas kernels for 0%

commit v1 on v0

v1 whole, which is shorter than its diff:
```python
import jax
import jax.numpy as jnp
from jax import lax
from jax.experimental import pallas as pl
from jax.experimental.pallas import tpu as pltpu
from jax.sharding import PartitionSpec as P

HD = 128
BLK = 128
MAXLEN = 512
GROUP = 5
QB = 256
SCALE = HD ** (-0.5)
LOG2E = 1.4426950408889634
C2 = SCALE * LOG2E
F32 = jnp.float32
BF16 = jnp.bfloat16
VMEM_LIMIT = 40 * 1024 * 1024

NT = (((1,), (1,)), ((), ()))


def dot(a, b):
    return jnp.dot(a, b, preferred_element_type=F32)


def dot_nt(a, b):
    return lax.dot_general(a, b, NT, preferred_element_type=F32)


def causal_keep(rows, first_row):
    u = lax.broadcasted_iota(jnp.int32, (rows, QB), 0)
    i = lax.broadcasted_iota(jnp.int32, (rows, QB), 1)
    return u <= i


def lanes(head):
    return pl.ds(pl.multiple_of(head * HD, HD), HD)


def own_stats_kernel(
    len_ref, q_ref, g_ref, k_ref, v_ref, copy_ref, masked_ref, max_ref, sum_ref, del_ref
):
    live = lax.broadcasted_iota(jnp.int32, (MAXLEN, 1), 0) < BLK * len_ref[0]
    g = jnp.where(live, g_ref[...], jnp.zeros((), BF16))
    masked_ref[...] = g
    copy_ref[...] = q_ref[...]
    keep = causal_keep(QB, 0)
    for block in range(MAXLEN // QB):
        lo = block * QB
        hi = lo + QB
        q = q_ref[lo:hi, :]
        gb = g[lo:hi, :]
        diag = jnp.where(keep, dot_nt(k_ref[lo:hi, :], q), -jnp.inf)
        top = jnp.max(diag, axis=0, keepdims=True)
        if block:
            past = dot_nt(k_ref[0:lo, :], q)
            top = jnp.maximum(top, jnp.max(past, axis=0, keepdims=True))
        top = top * C2
        e = jnp.exp2(diag * C2 - top)
        total = jnp.sum(e, axis=0, keepdims=True)
        delta = jnp.sum(e * dot_nt(v_ref[lo:hi, :], gb), axis=0, keepdims=True)
        if block:
            e = jnp.exp2(past * C2 - top)
            total = total + jnp.sum(e, axis=0, keepdims=True)
            delta = delta + jnp.sum(e * dot_nt(v_ref[0:lo, :], gb), axis=0, keepdims=True)
        max_ref[0, :, lo:hi] = top
        sum_ref[0, :, lo:hi] = total
        del_ref[0, :, lo:hi] = delta


def prompt_kernel(
    core_ref, q_ref, g_ref, kv_ref, max_ref, sum_ref, del_ref,
    ds_ref, keep_ref, send_ref, lse_ref, delta_ref,
    grad_ref, *scratch,
):
    tokens = kv_ref.shape[0]
    tile = 64
    sets = (scratch[0:5], scratch[5:10])

    def rows(block):
        return slice(block * QB, (block + 1) * QB)

    def scores(head, block):
        s_ref, dp_ref, _, _, top_ref = sets[block]
        s = dot_nt(kv_ref[:, 0:HD], q_ref[rows(block), lanes(head)])
        s_ref[...] = s
        top_ref[...] = jnp.max(s.reshape(tokens // 8, 8, QB), axis=0)
        dp_ref[...] = dot_nt(kv_ref[:, HD:], g_ref[rows(block), lanes(head)])

    def softmax(head, block):
        s_ref, dp_ref, p_ref, d_ref, top_ref = sets[block]
        own_top = max_ref[head, :, rows(block)]
        top = jnp.max(top_ref[...], axis=0, keepdims=True) * C2
        top = jnp.maximum(top, own_top)
        own = jnp.exp2(own_top - top)
        total = jnp.zeros((8, QB), F32)
        delta = jnp.zeros((8, QB), F32)
        for t in range(0, tokens, tile):
            e = jnp.exp2(s_ref[t : t + tile, :] * C2 - top)
            s_ref[t : t + tile, :] = e
            total = total + jnp.sum(e.reshape(tile // 8, 8, QB), axis=0)
            ed = e * dp_ref[t : t + tile, :]
            delta = delta + jnp.sum(ed.reshape(tile // 8, 8, QB), axis=0)
        total = jnp.sum(total, axis=0, keepdims=True) + own * sum_ref[head, :, rows(block)]
        inverse = 1.0 / total
        delta = jnp.sum(delta, axis=0, keepdims=True) + own * del_ref[head, :, rows(block)]
        delta = delta * inverse
        lse_ref[head, :, rows(block)] = top + jnp.log2(total)
        delta_ref[head, :, rows(block)] = delta
        for t in range(0, tokens, tile):
            p = s_ref[t : t + tile, :] * inverse
            p_ref[t : t + tile, :] = p.astype(BF16)
            ds = (p * (dp_ref[t : t + tile, :] - delta)).astype(BF16)
            d_ref[t : t + tile, :] = ds
            ds_ref[head, t : t + tile, rows(block)] = ds

    def grads(head, block):
        _, _, p_ref, d_ref, _ = sets[block]
        grad_ref[:, 0:HD] += dot(d_ref[...], q_ref[rows(block), lanes(head)])
        grad_ref[:, HD:] += dot(p_ref[...], g_ref[rows(block), lanes(head)])

    grad_ref[...] = jnp.zeros_like(grad_ref)
    scores(0, 0)
    scores(0, 1)
    softmax(0, 0)

    def body(head, carry):
        scores(head, 0)
        softmax(head - 1, 1)
        grads(head - 1, 0)
        scores(head, 1)
        softmax(head, 0)
        grads(head - 1, 1)
        return carry

    lax.fori_loop(1, GROUP, body, 0)
    softmax(GROUP - 1, 1)
    grads(GROUP - 1, 0)
    grads(GROUP - 1, 1)

    half = tokens // 2
    core = core_ref[0]
    for out, side in ((keep_ref, core), (send_ref, 1 - core)):
        part = grad_ref[pl.ds(pl.multiple_of(side * half, half), half), :]
        out[:, 0:HD] = part[:, 0:HD] * SCALE
        out[:, HD:] = part[:, HD:]


def tail_kernel(
    q_ref, g_ref, k_ref, v_ref, lse_ref, delta_ref, ds_ref, kv_ref, dq_ref, dk_ref, dv_ref
):
    head = pl.program_id(0)

    @pl.when(head == 0)
    def _():
        dk_ref[...] = jnp.zeros_like(dk_ref)
        dv_ref[...] = jnp.zeros_like(dv_ref)

    keep = causal_keep(QB, 0)
    keys_t = k_ref[...].T
    grad = dot(kv_ref[:, 0:HD].T, ds_ref[head])
    for block in range(MAXLEN // QB):
        lo = block * QB
        hi = lo + QB
        q = q_ref[lo:hi, lanes(head)]
        gb = g_ref[lo:hi, lanes(head)]
        lse = lse_ref[head, :, lo:hi]
        delta = delta_ref[head, :, lo:hi]
        p = jnp.exp2(dot_nt(k_ref[0:hi, :], q) * C2 - lse)
        last = jnp.where(keep, p[lo:hi], 0.0)
        p = jnp.concatenate([p[0:lo], last], axis=0) if block else last
        ds = (p * (dot_nt(v_ref[0:hi, :], gb) - delta)).astype(BF16)
        dv_ref[0:hi, :] += dot(p.astype(BF16), gb)
        dk_ref[0:hi, :] += dot(ds, q)
        part = grad[:, lo:hi] + dot(keys_t[:, 0:hi], ds)
        dq_ref[lo:hi, :] = part.T * SCALE

    @pl.when(head == GROUP - 1)
    def _():
        dk_ref[...] = dk_ref[...] * SCALE


def whole(shape):
    return pl.BlockSpec(shape, lambda h: (0,) * len(shape))


HEAD = pl.BlockSpec((MAXLEN, HD), lambda h: (0, h))
ROW = pl.BlockSpec((1, 1, MAXLEN), lambda h: (h, 0, 0))


def params():
    return pltpu.CompilerParams(
        dimension_semantics=("arbitrary",), vmem_limit_bytes=VMEM_LIMIT
    )


def cost(flops, exps, moved):
    return pl.CostEstimate(flops=flops, transcendentals=exps, bytes_accessed=moved)


def struct(shape, dtype):
    return jax.ShapeDtypeStruct(shape, dtype)


def vmem_struct(shape, dtype):
    return pltpu.VMEM(shape, dtype)


def vmem(x):
    return pltpu.with_memory_space_constraint(x, pltpu.VMEM)


def hbm(x):
    return pltpu.with_memory_space_constraint(x, pltpu.HBM)


SMEM = pl.BlockSpec(memory_space=pltpu.SMEM)
VMEM = pl.BlockSpec(memory_space=pltpu.VMEM)


def per_device(queries, comp_keys, comp_values, out_grad, prompt_keys, prompt_values, lengths):
    shard = prompt_keys.shape[0]
    devices = lax.axis_size("comp")
    chips = devices // 2
    ring = devices // 4
    tokens = devices * shard
    half = tokens // 2
    width = GROUP * HD

    own = jnp.concatenate([prompt_keys, prompt_values], axis=1)
    along_y = [[y * 4 + rest for y in range(ring)] for rest in range(4)]
    rest_of = [[y * 4 + z * 2 + core for core in range(2) for z in range(2)] for y in range(ring)]
    gathered = lax.all_gather(own, "comp", axis=0, tiled=True, axis_index_groups=along_y)
    prompt = lax.all_gather(gathered, "comp", axis=0, tiled=True, axis_index_groups=rest_of)
    core = (lax.axis_index("comp") % 2).reshape(1).astype(jnp.int32)

    stat = struct((GROUP, 1, MAXLEN), F32)
    copied, masked, own_max, own_sum, own_del = pl.pallas_call(
        own_stats_kernel,
        grid=(GROUP,),
        in_specs=[SMEM, HEAD, HEAD, whole((MAXLEN, HD)), whole((MAXLEN, HD))],
        out_specs=[HEAD, HEAD, ROW, ROW, ROW],
        out_shape=[
            vmem_struct((MAXLEN, width), BF16), vmem_struct((MAXLEN, width), BF16),
            stat, stat, stat,
        ],
        compiler_params=params(),
        cost_estimate=cost(GROUP * 4 * 384 * 512 * HD, GROUP * 384 * 512, 2**21),
        name="own_stats",
    )(lengths, hbm(queries), hbm(out_grad), hbm(comp_keys), hbm(comp_values))

    dscore, grad_keep, grad_send, lse, delta = pl.pallas_call(
        prompt_kernel,
        in_specs=[SMEM] + [VMEM] * 6,
        out_specs=[VMEM] * 5,
        out_shape=[
            vmem_struct((GROUP, tokens, MAXLEN), BF16),
            struct((half, 2 * HD), F32), struct((half, 2 * HD), F32), stat, stat,
        ],
        scratch_shapes=[pltpu.VMEM((tokens, 2 * HD), F32)]
        + [
            pltpu.VMEM((tokens, QB), F32),
            pltpu.VMEM((tokens, QB), F32),
            pltpu.VMEM((tokens, QB), BF16),
            pltpu.VMEM((tokens, QB), BF16),
            pltpu.VMEM((8, QB), F32),
        ]
        * 2,
        compiler_params=pltpu.CompilerParams(vmem_limit_bytes=VMEM_LIMIT),
        cost_estimate=cost(GROUP * 8 * 1024 * 512 * HD, GROUP * 1024 * 512, 2**23),
        name="prompt",
    )(core, vmem(copied), vmem(masked), prompt, own_max, own_sum, own_del)

    swap = [(d, d ^ 1) for d in range(devices)]
    received = lax.ppermute(grad_send, "comp", swap)
    chip_sum = (grad_keep + received).astype(BF16).reshape(chips, shard, 2 * HD)
    same_core = [
        [y * 4 + z * 2 + side for z in range(2) for y in range(ring)] for side in range(2)
    ]
    arrived = lax.all_to_all(chip_sum, "comp", 0, 0, axis_index_groups=same_core, tiled=True)
    grad_prompt = jnp.sum(arrived.astype(F32), axis=0)

    grad_queries, grad_comp_keys, grad_comp_values = pl.pallas_call(
        tail_kernel,
        grid=(GROUP,),
        in_specs=[VMEM, VMEM, whole((MAXLEN, HD)), whole((MAXLEN, HD)), VMEM, VMEM, VMEM, VMEM],
        out_specs=[HEAD, whole((MAXLEN, HD)), whole((MAXLEN, HD))],
        out_shape=[
            struct((MAXLEN, width), F32),
            struct((MAXLEN, HD), F32), struct((MAXLEN, HD), F32),
        ],
        compiler_params=params(),
        cost_estimate=cost(GROUP * 4 * 1024 * 512 * HD, GROUP * 384 * 512, 2**23),
        name="tail",
    )(
        vmem(copied), vmem(masked), hbm(comp_keys), hbm(comp_values), lse, delta,
        vmem(dscore), prompt,
    )

    return (
        grad_queries,
        grad_prompt[:, 0:HD],
        grad_prompt[:, HD:],
        grad_comp_keys,
        grad_comp_values,
    )


def solution(mesh):
    rows = P(("grp", "comp"), "tp")
    return jax.shard_map(
        per_device,
        mesh=mesh,
        in_specs=(rows,) * 6 + (P(("grp", "comp")),),
        out_specs=(rows,) * 5,
        check_vma=False,
    )
```

time: 325 us -> 80.8 us (0.25)
  waiting for transfers between devices: 163 us -> 2.81 us
  matrix products: 57.1 us -> 0 us
  blocking collectives: 68.2 us -> 40 us
  Pallas kernels: 0 us -> 20.9 us
  between operations: 15.8 us -> 1.34 us
  local copies, waits for them, and re-layouts: 14.2 us -> 5.39 us
  starting transfers between devices: 0.08 us -> 7.99 us
  other arithmetic: 6.46 us -> 1.52 us
    reduce_scatter x2 -> x0, waiting for transfers between devices: 163 us -> none  [the longest x1 120 us: per_device(): lax.psum_scatter(prompt_kgrad, 'comp', scatter_dimension=0, tiled=True)]
    dot_general x60 -> x0, matrix products: 57.1 us -> none  [the longest x5 10.6 us: per_device(): jnp.dot(query_head, keys_whole.T, preferred_element_type=jnp.float32)]
    all_gather x2, blocking collectives: 68.2 us -> 40 us  [the longest x1 26.1 us: per_device(): lax.all_gather(own, 'comp', axis=0, tiled=True, axis_index_groups=along_y)]
    pallas_call x0 -> x3, Pallas kernels: none -> 20.9 us  [the longest x1 9.36 us: per_device(): pl.pallas_call(prompt_kernel, in_specs=[SMEM] + [VMEM] * 6, out_specs=[VM...]
    unnamed x143 -> x4, local copies, waits for them, and re-layouts: 14.2 us -> 4.78 us
    all_to_all x0 -> x1, starting transfers between devices: none -> 6.08 us  [per_device(): lax.all_to_all(chip_sum, 'comp', 0, 0, axis_index_groups=same_core, tiled...]
    reduce_sum x10 -> x1, other arithmetic: 5.66 us -> 0.04 us  [per_device(): grad_prompt = jnp.sum(arrived.astype(F32), axis=0)]
  transfers between devices with their start and end apart: 2 -> 2, of which waited for: 2 -> 2; matrix products, arithmetic and copies ran while one was open for 12% -> 0% of each run, Pallas kernels for 0% -> 9%
where the time goes in v1:
time: 80.8 us; the launch traced here: 79.9 us
  blocking collectives  40 us (50%)
  Pallas kernels  20.9 us (26%)
  starting transfers between devices  7.99 us (10%)
  local copies, waits for them, and re-layouts  5.39 us (7%)
  waiting for transfers between devices  2.81 us (3%)
  other arithmetic  1.52 us (2%)
  between operations  1.34 us (2%)
    all_gather x1, blocking collectives, per_device(): lax.all_gather(own, 'comp', axis=0, tiled=True, axis_index_groups=along_y)  26.1 us
    all_gather x1, blocking collectives, per_device(): lax.all_gather(gathered, 'comp', axis=0, tiled=True, axis_index_groups=re...  13.8 us
    pallas_call x1, Pallas kernels, per_device(): pl.pallas_call(prompt_kernel, in_specs=[SMEM] + [VMEM] * 6, out_specs=[VM...  9.36 us
    pallas_call x1, Pallas kernels, per_device(): pl.pallas_call(tail_kernel, grid=(GROUP,), in_specs=[VMEM, VMEM, whole((M...  7.02 us
    all_to_all x1, starting transfers between devices, per_device(): lax.all_to_all(chip_sum, 'comp', 0, 0, axis_index_groups=same_core, tiled...  6.08 us
    unnamed x4, local copies, waits for them, and re-layouts  4.78 us
    pallas_call x1, Pallas kernels, per_device(): pl.pallas_call(own_stats_kernel, grid=(GROUP,), in_specs=[SMEM, HEAD, HEA...  4.53 us
    ppermute x1, starting transfers between devices, per_device(): received = lax.ppermute(grad_send, 'comp', swap)  1.91 us
  transfers between devices with their start and end apart: 2, of which 2 were waited for; matrix products, arithmetic and copies ran while one was open for 0% of the time, Pallas kernels for 9%

profile of v1, /device:TPU:6, one launch (start us, length us, event | category | flops | bytes accessed | tf_op | source)
XLA Modules:
  0.0 79.9 jit_solution(10443234571409805426)
XLA Ops:
  1.3 0.7 pad_maximum_fusion
  2.0 26.1 %all_gather.6 = bf16[256,256]{1,0:T(8,128)(2,1)S(1)} all-gather(bf16[32,256]{1,0:T(8,128)(2,1)S(1)} %pad_maximum_fusion), channel_id=1, replica_groups={{0,16,32,48,64,80,96,112},{4,20,36,52,68,84,100,116},{8,24,40,56,72,88,..., dimensions={0}, use_global_device_ids=true | all-gather | bytes 147456 | tf_op jit(solution)/shard_map/all_gather | solution.py:234
  28.1 13.8 %all_gather.7.kv_ref = bf16[1024,256]{1,0:T(8,128)(2,1)S(1)} all-gather(bf16[256,256]{1,0:T(8,128)(2,1)S(1)} %all_gather.6), channel_id=1, replica_groups={{0,8,4,12},{16,24,20,28},{32,40,36,44},{48,56,52,60},{64,72,68,76},{80,..., dimensions={0}, use_global_device_ids=true | all-gather | bytes 655360 | tf_op jit(solution)/shard_map/all_gather | solution.py:235
  42.0 4.5 %own_stats.1 = (bf16[512,640]{1,0:T(8,128)(2,1)S(1)}, bf16[512,640]{1,0:T(8,128)(2,1)S(1)}, f32[5,1,512]{2,1,0:T(1,128)S(1)}, f32[5,1,512]{2,1,0:T(1,128)S(1)}, f32[5,1,512]{2,1,0:T(1,128)S(1)}) custom-call(s32[1]{0:T(128)S(6)} %copy.12.len_ref, bf16[512,640]{1,0:T(8,128)(2,1)} %q_ref.1, bf16[512,640]{1,0:T(8,128)(2,1)} %g_ref.1, bf16[512,128]{1,0:T(8,128)(2,1)} %k_ref.3, ...), custom_call_target="tpu_custom_call" | custom-call | flops 503316480 | bytes 2097152 | tf_op jit(solution)/shard_map/own_stats/pallas_call | solution.py:239
  46.5 9.4 %prompt.1 = (bf16[5,1024,512]{2,1,0:T(8,128)(2,1)S(1)}, f32[512,256]{1,0:T(8,128)S(1)}, f32[512,256]{1,0:T(8,128)S(1)}, f32[5,1,512]{2,1,0:T(1,128)S(1)}, f32[5,1,512]{2,1,0:T(1,128)S(1)}) custom-call(s32[1]{0:T(128)} %bitcast.core_ref, bf16[512,640]{1,0:T(8,128)(2,1)S(1)} %get-tuple-element.18.q_ref, bf16[512,640]{1,0:T(8,128)(2,1)S(1)} %get-tuple-element.19.g_ref, ...), custom_call_target="tpu_custom_call" | custom-call | flops 2684354560 | bytes 8388608 | tf_op jit(solution)/shard_map/prompt/pallas_call | solution.py:253
  55.9 0.0 copy-start
  55.9 2.3 %copy-done = bf16[5,1024,512]{2,1,0:T(8,128)(2,1)} copy-done((bf16[5,1024,512]{2,1,0:T(8,128)(2,1)}, bf16[5,1024,512]{2,1,0:T(8,128)(2,1)S(1)}, u32[]{:S(2)}) %copy-start) | copy-done | bytes 5242904
  58.2 1.9 %collective-permute-start = (f32[512,256]{1,0:T(8,128)S(1)}, f32[512,256]{1,0:T(8,128)S(1)}, u32[]{:S(2)}, u32[]{:S(2)}) collective-permute-start(f32[512,256]{1,0:T(8,128)S(1)} %get-tuple-element.28), channel_id=1, source_target_pairs={{0,4},{4,0},{8,12},{12,8},{16,20},{20,16},{24,28},{28,24},{32,36},... | collective-permute-start | bytes 1572872 | tf_op jit(solution)/shard_map/ppermute | solution.py:276
  60.1 1.9 %collective-permute-done = f32[512,256]{1,0:T(8,128)S(1)} collective-permute-done((f32[512,256]{1,0:T(8,128)S(1)}, f32[512,256]{1,0:T(8,128)S(1)}, u32[]{:S(2)}, u32[]{:S(2)}) %collective-permute-start) | collective-permute-done | bytes 524320 | tf_op jit(solution)/shard_map/ppermute | solution.py:276
  62.0 0.8 add_convert_fusion
  62.7 6.1 %all-to-all-start = ((bf16[16,32,256]{2,1,0:T(8,128)(2,1)}), bf16[16,32,256]{2,1,0:T(8,128)(2,1)S(1)}, u32[]{:S(2)}, u32[]{:S(2)}) async-start(bf16[16,32,256]{2,1,0:T(8,128)(2,1)} %bitcast.1), calls=%async_computation | async-start | bytes 524288 | tf_op jit(solution)/shard_map/all_to_all | solution.py:281
  68.8 0.0 copy-start.1
  68.8 2.5 %copy-done.1 = bf16[5,1024,512]{2,1,0:T(8,128)(2,1)S(1)} copy-done((bf16[5,1024,512]{2,1,0:T(8,128)(2,1)S(1)}, bf16[5,1024,512]{2,1,0:T(8,128)(2,1)}, u32[]{:S(2)}) %copy-start.1) | copy-done | bytes 5242904
  71.3 7.0 %tail.1 = (f32[512,640]{1,0:T(8,128)}, f32[512,128]{1,0:T(8,128)}, f32[512,128]{1,0:T(8,128)}) custom-call(bf16[512,640]{1,0:T(8,128)(2,1)S(1)} %get-tuple-element.18.q_ref, bf16[512,640]{1,0:T(8,128)(2,1)S(1)} %get-tuple-element.19.g_ref, bf16[512,128]{1,0:T(8,128)(2,1)} %k_ref.3, bf16[512,128]{1,0:T(8,128)(2,1)} %v_ref.3, ...), custom_call_target="tpu_custom_call" | custom-call | flops 1342177280 | bytes 8388608 | tf_op jit(solution)/shard_map/tail/pallas_call | solution.py:284
  78.3 0.9 %all-to-all-done = bf16[16,32,256]{2,1,0:T(8,128)(2,1)S(1)} async-done(((bf16[16,32,256]{2,1,0:T(8,128)(2,1)}), bf16[16,32,256]{2,1,0:T(8,128)(2,1)S(1)}, u32[]{:S(2)}, u32[]{:S(2)}) %all-to-all-start) | async-done | bytes 262176 | tf_op jit(solution)/shard_map/all_to_all | solution.py:281
  79.3 0.6 fusion
  (1 shorter events, 0.0 us)
Async XLA Ops:
  55.9 2.3 %copy-start = (bf16[5,1024,512]{2,1,0:T(8,128)(2,1)}, bf16[5,1024,512]{2,1,0:T(8,128)(2,1)S(1)}, u32[]{:S(2)}) copy-start(bf16[5,1024,512]{2,1,0:T(8,128)(2,1)S(1)} %get-tuple-element.25.ds_ref) | copy-start | bytes 15728644
  58.2 3.8 %collective-permute-start = (f32[512,256]{1,0:T(8,128)S(1)}, f32[512,256]{1,0:T(8,128)S(1)}, u32[]{:S(2)}, u32[]{:S(2)}) collective-permute-start(f32[512,256]{1,0:T(8,128)S(1)} %get-tuple-element.28), channel_id=1, source_target_pairs={{0,4},{4,0},{8,12},{12,8},{16,20},{20,16},{24,28},{28,24},{32,36},... | collective-permute-start | bytes 1572872 | tf_op jit(solution)/shard_map/ppermute | solution.py:276
  62.7 16.5 %all-to-all-start = ((bf16[16,32,256]{2,1,0:T(8,128)(2,1)}), bf16[16,32,256]{2,1,0:T(8,128)(2,1)S(1)}, u32[]{:S(2)}, u32[]{:S(2)}) async-start(bf16[16,32,256]{2,1,0:T(8,128)(2,1)} %bitcast.1), calls=%async_computation | async-start | bytes 524288 | tf_op jit(solution)/shard_map/all_to_all | solution.py:281
  68.8 2.5 %copy-start.1 = (bf16[5,1024,512]{2,1,0:T(8,128)(2,1)S(1)}, bf16[5,1024,512]{2,1,0:T(8,128)(2,1)}, u32[]{:S(2)}) copy-start(bf16[5,1024,512]{2,1,0:T(8,128)(2,1)} %copy-done) | copy-start | bytes 15728644

commit v2 on v1

--- a/solution.py
+++ b/solution.py
@@ -10,6 +10,7 @@
 MAXLEN = 512
 GROUP = 5
 QB = 256
+SHARD = 32
 SCALE = HD ** (-0.5)
 LOG2E = 1.4426950408889634
 C2 = SCALE * LOG2E
@@ -36,6 +37,12 @@
 
 def lanes(head):
     return pl.ds(pl.multiple_of(head * HD, HD), HD)
+
+
+def spread_kernel(k_ref, v_ref, out_ref):
+    for chip in range(out_ref.shape[0]):
+        out_ref[chip, :, 0:HD] = k_ref[...]
+        out_ref[chip, :, HD:] = v_ref[...]
 
 
 def own_stats_kernel(
@@ -70,11 +77,12 @@
 
 
 def prompt_kernel(
-    core_ref, q_ref, g_ref, kv_ref, max_ref, sum_ref, del_ref,
-    ds_ref, keep_ref, send_ref, lse_ref, delta_ref,
-    grad_ref, *scratch,
+    q_ref, g_ref, mine_ref, other_ref, max_ref, sum_ref, del_ref,
+    dq_ref, keep_ref, send_ref, lse_ref, delta_ref,
+    grad_ref, kt_ref, kv_ref, *scratch,
 ):
-    tokens = kv_ref.shape[0]
+    half = mine_ref.shape[0]
+    tokens = 2 * half
     tile = 64
     sets = (scratch[0:5], scratch[5:10])
 
@@ -98,28 +106,29 @@
         delta = jnp.zeros((8, QB), F32)
         for t in range(0, tokens, tile):
             e = jnp.exp2(s_ref[t : t + tile, :] * C2 - top)
-            s_ref[t : t + tile, :] = e
             total = total + jnp.sum(e.reshape(tile // 8, 8, QB), axis=0)
             ed = e * dp_ref[t : t + tile, :]
             delta = delta + jnp.sum(ed.reshape(tile // 8, 8, QB), axis=0)
         total = jnp.sum(total, axis=0, keepdims=True) + own * sum_ref[head, :, rows(block)]
-        inverse = 1.0 / total
         delta = jnp.sum(delta, axis=0, keepdims=True) + own * del_ref[head, :, rows(block)]
-        delta = delta * inverse
-        lse_ref[head, :, rows(block)] = top + jnp.log2(total)
+        delta = delta * (1.0 / total)
+        lse = top + jnp.log2(total)
+        lse_ref[head, :, rows(block)] = lse
         delta_ref[head, :, rows(block)] = delta
         for t in range(0, tokens, tile):
-            p = s_ref[t : t + tile, :] * inverse
+            p = jnp.exp2(s_ref[t : t + tile, :] * C2 - lse)
             p_ref[t : t + tile, :] = p.astype(BF16)
-            ds = (p * (dp_ref[t : t + tile, :] - delta)).astype(BF16)
-            d_ref[t : t + tile, :] = ds
-            ds_ref[head, t : t + tile, rows(block)] = ds
+            d_ref[t : t + tile, :] = (p * (dp_ref[t : t + tile, :] - delta)).astype(BF16)
 
     def grads(head, block):
         _, _, p_ref, d_ref, _ = sets[block]
-        grad_ref[:, 0:HD] += dot(d_ref[...], q_ref[rows(block), lanes(head)])
-        grad_ref[:, HD:] += dot(p_ref[...], g_ref[rows(block), lanes(head)])
-
+        grad_ref[0:HD, :] += dot_nt(q_ref[rows(block), lanes(head)].T, d_ref[...])
+        grad_ref[HD:, :] += dot_nt(g_ref[rows(block), lanes(head)].T, p_ref[...])
+        dq_ref[head, :, rows(block)] = dot(kt_ref[...], d_ref[...])
+
+    kv_ref[0:half, :] = mine_ref[...]
+    kv_ref[half:, :] = other_ref[...]
+    kt_ref[...] = kv_ref[:, 0:HD].T
     grad_ref[...] = jnp.zeros_like(grad_ref)
     scores(0, 0)
     scores(0, 1)
@@ -139,16 +148,15 @@
     grads(GROUP - 1, 0)
     grads(GROUP - 1, 1)
 
-    half = tokens // 2
-    core = core_ref[0]
-    for out, side in ((keep_ref, core), (send_ref, 1 - core)):
-        part = grad_ref[pl.ds(pl.multiple_of(side * half, half), half), :]
-        out[:, 0:HD] = part[:, 0:HD] * SCALE
-        out[:, HD:] = part[:, HD:]
-
-
-def tail_kernel(
-    q_ref, g_ref, k_ref, v_ref, lse_ref, delta_ref, ds_ref, kv_ref, dq_ref, dk_ref, dv_ref
+    for base, out in ((0, keep_ref), (half, send_ref)):
+        for t in range(0, half, HD):
+            take = slice(base + t, base + t + HD)
+            out[t : t + HD, 0:HD] = grad_ref[0:HD, take].T * SCALE
+            out[t : t + HD, HD:] = grad_ref[HD:, take].T
+
+
+def own_grad_kernel(
+    q_ref, g_ref, k_ref, v_ref, lse_ref, delta_ref, past_ref, dq_ref, dk_ref, dv_ref
 ):
     head = pl.program_id(0)
 
@@ -159,7 +167,6 @@
 
     keep = causal_keep(QB, 0)
     keys_t = k_ref[...].T
-    grad = dot(kv_ref[:, 0:HD].T, ds_ref[head])
     for block in range(MAXLEN // QB):
         lo = block * QB
         hi = lo + QB
@@ -173,7 +180,7 @@
         ds = (p * (dot_nt(v_ref[0:hi, :], gb) - delta)).astype(BF16)
         dv_ref[0:hi, :] += dot(p.astype(BF16), gb)
         dk_ref[0:hi, :] += dot(ds, q)
-        part = grad[:, lo:hi] + dot(keys_t[:, 0:hi], ds)
+        part = past_ref[head, :, lo:hi] + dot(keys_t[:, 0:hi], ds)
         dq_ref[lo:hi, :] = part.T * SCALE
 
     @pl.when(head == GROUP - 1)
@@ -220,20 +227,23 @@
 
 
 def per_device(queries, comp_keys, comp_values, out_grad, prompt_keys, prompt_values, lengths):
-    shard = prompt_keys.shape[0]
     devices = lax.axis_size("comp")
+    half = devices * SHARD // 2
+    tokens = 2 * half
+    width = GROUP * HD
+
     chips = devices // 2
-    ring = devices // 4
-    tokens = devices * shard
-    half = tokens // 2
-    width = GROUP * HD
-
-    own = jnp.concatenate([prompt_keys, prompt_values], axis=1)
-    along_y = [[y * 4 + rest for y in range(ring)] for rest in range(4)]
-    rest_of = [[y * 4 + z * 2 + core for core in range(2) for z in range(2)] for y in range(ring)]
-    gathered = lax.all_gather(own, "comp", axis=0, tiled=True, axis_index_groups=along_y)
-    prompt = lax.all_gather(gathered, "comp", axis=0, tiled=True, axis_index_groups=rest_of)
-    core = (lax.axis_index("comp") % 2).reshape(1).astype(jnp.int32)
+    swap = [(d, d ^ 1) for d in range(devices)]
+    same_core = [[2 * chip + core for chip in range(chips)] for core in range(2)]
+    spread = pl.pallas_call(
+        spread_kernel,
+        in_specs=[VMEM, VMEM],
+        out_specs=VMEM,
+        out_shape=struct((chips, SHARD, 2 * HD), BF16),
+        name="spread",
+    )(hbm(prompt_keys), hbm(prompt_values))
+    mine = lax.all_to_all(spread, "comp", 0, 0, axis_index_groups=same_core, tiled=True)
+    mine = mine.reshape(half, 2 * HD)
 
     stat = struct((GROUP, 1, MAXLEN), F32)
     copied, masked, own_max, own_sum, own_del = pl.pallas_call(
@@ -250,15 +260,22 @@
         name="own_stats",
     )(lengths, hbm(queries), hbm(out_grad), hbm(comp_keys), hbm(comp_values))
 
-    dscore, grad_keep, grad_send, lse, delta = pl.pallas_call(
+    mine, masked = lax.optimization_barrier((mine, masked))
+    other = lax.ppermute(mine, "comp", swap)
+
+    past, grad_keep, grad_send, lse, delta = pl.pallas_call(
         prompt_kernel,
-        in_specs=[SMEM] + [VMEM] * 6,
+        in_specs=[VMEM] * 7,
         out_specs=[VMEM] * 5,
         out_shape=[
-            vmem_struct((GROUP, tokens, MAXLEN), BF16),
+            struct((GROUP, HD, MAXLEN), F32),
             struct((half, 2 * HD), F32), struct((half, 2 * HD), F32), stat, stat,
         ],
-        scratch_shapes=[pltpu.VMEM((tokens, 2 * HD), F32)]
+        scratch_shapes=[
+            pltpu.VMEM((2 * HD, tokens), F32),
+            pltpu.VMEM((HD, tokens), BF16),
+            pltpu.VMEM((tokens, 2 * HD), BF16),
+        ]
         + [
             pltpu.VMEM((tokens, QB), F32),
             pltpu.VMEM((tokens, QB), F32),
@@ -268,34 +285,29 @@
         ]
         * 2,
         compiler_params=pltpu.CompilerParams(vmem_limit_bytes=VMEM_LIMIT),
-        cost_estimate=cost(GROUP * 8 * 1024 * 512 * HD, GROUP * 1024 * 512, 2**23),
+        cost_estimate=cost(GROUP * 10 * 1024 * 512 * HD, GROUP * 2048 * 512, 2**22),
         name="prompt",
-    )(core, vmem(copied), vmem(masked), prompt, own_max, own_sum, own_del)
-
-    swap = [(d, d ^ 1) for d in range(devices)]
+    )(vmem(copied), vmem(masked), mine, other, own_max, own_sum, own_del)
+
     received = lax.ppermute(grad_send, "comp", swap)
-    chip_sum = (grad_keep + received).astype(BF16).reshape(chips, shard, 2 * HD)
-    same_core = [
-        [y * 4 + z * 2 + side for z in range(2) for y in range(ring)] for side in range(2)
-    ]
-    arrived = lax.all_to_all(chip_sum, "comp", 0, 0, axis_index_groups=same_core, tiled=True)
+    total = (grad_keep + received).astype(BF16).reshape(chips, SHARD, 2 * HD)
+    arrived = lax.all_to_all(total, "comp", 0, 0, axis_index_groups=same_core, tiled=True)
     grad_prompt = jnp.sum(arrived.astype(F32), axis=0)
 
     grad_queries, grad_comp_keys, grad_comp_values = pl.pallas_call(
-        tail_kernel,
+        own_grad_kernel,
         grid=(GROUP,),
-        in_specs=[VMEM, VMEM, whole((MAXLEN, HD)), whole((MAXLEN, HD)), VMEM, VMEM, VMEM, VMEM],
+        in_specs=[VMEM, VMEM, whole((MAXLEN, HD)), whole((MAXLEN, HD)), VMEM, VMEM, VMEM],
         out_specs=[HEAD, whole((MAXLEN, HD)), whole((MAXLEN, HD))],
         out_shape=[
             struct((MAXLEN, width), F32),
             struct((MAXLEN, HD), F32), struct((MAXLEN, HD), F32),
         ],
         compiler_params=params(),
-        cost_estimate=cost(GROUP * 4 * 1024 * 512 * HD, GROUP * 384 * 512, 2**23),
-        name="tail",
+        cost_estimate=cost(GROUP * 10 * 384 * 512 * HD, GROUP * 384 * 512, 2**22),
+        name="own_grad",
     )(
-        vmem(copied), vmem(masked), hbm(comp_keys), hbm(comp_values), lse, delta,
-        vmem(dscore), prompt,
+        vmem(copied), vmem(masked), hbm(comp_keys), hbm(comp_values), lse, delta, past,
     )
 
     return (

time: 80.8 us -> 59.2 us (0.73)
  blocking collectives: 40 us -> 0 us
  waiting for transfers between devices: 2.81 us -> 16.9 us
  starting transfers between devices: 7.99 us -> 16.5 us
  local copies, waits for them, and re-layouts: 5.39 us -> 0.61 us
  Pallas kernels: 20.9 us -> 22.6 us
    all_gather x2 -> x0, blocking collectives: 40 us -> none  [the longest x1 26.1 us: per_device(): lax.all_gather(own, 'comp', axis=0, tiled=True, axis_index_groups=along_y)]
    all_to_all x1 -> x2, waiting for transfers between devices: 0.94 us -> 13.6 us  [the longest x1 6.83 us: per_device(): lax.all_to_all(spread, 'comp', 0, 0, axis_index_groups=same_core, tiled=T...]
    all_to_all x1 -> x2, starting transfers between devices: 6.08 us -> 12.5 us  [the longest x1 9.01 us: per_device(): lax.all_to_all(spread, 'comp', 0, 0, axis_index_groups=same_core, tiled=T...]
    unnamed x4 -> x0, local copies, waits for them, and re-layouts: 4.78 us -> none
    ppermute x0 -> x1, starting transfers between devices: none -> 1.91 us  [per_device(): other = lax.ppermute(mine, 'comp', swap)]
    pallas_call x2 -> x3, Pallas kernels: 16.4 us -> 18 us  [the longest x1 10.3 us: per_device(): pl.pallas_call(prompt_kernel, in_specs=[VMEM] * 7, out_specs=[VMEM] * 5,...]
    ppermute x0 -> x1, waiting for transfers between devices: none -> 1.5 us  [per_device(): other = lax.ppermute(mine, 'comp', swap)]
  transfers between devices with their start and end apart: 2 -> 4, of which waited for: 2 -> 4; matrix products, arithmetic and copies ran while one was open for 0% -> 0% of each run, Pallas kernels for 9% -> 18%
where the time goes in v2:
time: 59.2 us; the launch traced here: 58.7 us
  Pallas kernels  22.6 us (38%)
  waiting for transfers between devices  16.9 us (29%)
  starting transfers between devices  16.5 us (28%)
  between operations  1.32 us (2%)
  other arithmetic  0.79 us (1%)
  local copies, waits for them, and re-layouts  0.61 us (1%)
    pallas_call x1, Pallas kernels, per_device(): pl.pallas_call(prompt_kernel, in_specs=[VMEM] * 7, out_specs=[VMEM] * 5,...  10.3 us
    all_to_all x1, starting transfers between devices, per_device(): lax.all_to_all(spread, 'comp', 0, 0, axis_index_groups=same_core, tiled=T...  9.01 us
    all_to_all x1, waiting for transfers between devices, per_device(): lax.all_to_all(spread, 'comp', 0, 0, axis_index_groups=same_core, tiled=T...  6.83 us
    all_to_all x1, waiting for transfers between devices, per_device(): lax.all_to_all(total, 'comp', 0, 0, axis_index_groups=same_core, tiled=True)  6.79 us
    pallas_call x1, Pallas kernels, per_device(): pl.pallas_call(own_grad_kernel, grid=(GROUP,), in_specs=[VMEM, VMEM, whol...  6.23 us
    pallas_call x1, Pallas kernels, per_device(): pl.pallas_call(own_stats_kernel, grid=(GROUP,), in_specs=[SMEM, HEAD, HEA...  4.56 us
    all_to_all x1, starting transfers between devices, per_device(): lax.all_to_all(total, 'comp', 0, 0, axis_index_groups=same_core, tiled=True)  3.53 us
    ppermute x1, starting transfers between devices, per_device(): received = lax.ppermute(grad_send, 'comp', swap)  2.04 us
  transfers between devices with their start and end apart: 4, of which 4 were waited for; matrix products, arithmetic and copies ran while one was open for 0% of the time, Pallas kernels for 18%

profile of v2, /device:TPU:6, one launch (start us, length us, event | category | flops | bytes accessed | tf_op | source)
XLA Modules:
  0.0 58.7 jit_solution(9013083002532239879)
XLA Ops:
  0.6 1.5 %spread.1 = bf16[16,32,256]{2,1,0:T(8,128)(2,1)} custom-call(bf16[32,128]{1,0:T(8,128)(2,1)} %k_ref.4, bf16[32,128]{1,0:T(8,128)(2,1)} %v_ref.4), custom_call_target="tpu_custom_call" | custom-call | tf_op jit(solution)/shard_map/spread/pallas_call | solution.py:238
  2.1 9.0 %all-to-all-start = ((bf16[16,32,256]{2,1,0:T(8,128)(2,1)}), bf16[16,32,256]{2,1,0:T(8,128)(2,1)S(1)}, u32[]{:S(2)}, u32[]{:S(2)}) async-start(bf16[16,32,256]{2,1,0:T(8,128)(2,1)} %spread.1), calls=%async_computation | async-start | bytes 524288 | tf_op jit(solution)/shard_map/all_to_all | solution.py:245
  11.8 4.6 %own_stats.1 = (bf16[512,640]{1,0:T(8,128)(2,1)S(1)}, bf16[512,640]{1,0:T(8,128)(2,1)S(1)}, f32[5,1,512]{2,1,0:T(1,128)S(1)}, f32[5,1,512]{2,1,0:T(1,128)S(1)}, f32[5,1,512]{2,1,0:T(1,128)S(1)}) custom-call(s32[1]{0:T(128)S(6)} %copy.12.len_ref, bf16[512,640]{1,0:T(8,128)(2,1)} %q_ref.1, bf16[512,640]{1,0:T(8,128)(2,1)} %g_ref.1, bf16[512,128]{1,0:T(8,128)(2,1)} %k_ref.5, ...), custom_call_target="tpu_custom_call" | custom-call | flops 503316480 | bytes 2097152 | tf_op jit(solution)/shard_map/own_stats/pallas_call | solution.py:249
  16.3 6.8 %all-to-all-done = bf16[16,32,256]{2,1,0:T(8,128)(2,1)S(1)} async-done(((bf16[16,32,256]{2,1,0:T(8,128)(2,1)}), bf16[16,32,256]{2,1,0:T(8,128)(2,1)S(1)}, u32[]{:S(2)}, u32[]{:S(2)}) %all-to-all-start) | async-done | bytes 262176 | tf_op jit(solution)/shard_map/all_to_all | solution.py:245
  23.1 1.9 %collective-permute-start = (bf16[512,256]{1,0:T(8,128)(2,1)S(1)}, bf16[512,256]{1,0:T(8,128)(2,1)S(1)}, u32[]{:S(2)}, u32[]{:S(2)}) collective-permute-start(bf16[512,256]{1,0:T(8,128)(2,1)S(1)} %bitcast.2), channel_id=1, source_target_pairs={{0,4},{4,0},{8,12},{12,8},{16,20},{20,16},{24,28},{28,24},{32,36},... | collective-permute-start | bytes 786440 | tf_op jit(solution)/shard_map/ppermute | solution.py:264
  25.1 1.5 %collective-permute-done.other_ref = bf16[512,256]{1,0:T(8,128)(2,1)S(1)} collective-permute-done((bf16[512,256]{1,0:T(8,128)(2,1)S(1)}, bf16[512,256]{1,0:T(8,128)(2,1)S(1)}, u32[]{:S(2)}, u32[]{:S(2)}) %collective-permute-start) | collective-permute-done | bytes 262176 | tf_op jit(solution)/shard_map/ppermute | solution.py:264
  26.6 10.3 %prompt.1 = (f32[5,128,512]{2,1,0:T(8,128)S(1)}, f32[512,256]{1,0:T(8,128)S(1)}, f32[512,256]{1,0:T(8,128)S(1)}, f32[5,1,512]{2,1,0:T(1,128)S(1)}, f32[5,1,512]{2,1,0:T(1,128)S(1)}) custom-call(bf16[512,640]{1,0:T(8,128)(2,1)S(1)} %get-tuple-element.20.q_ref, bf16[512,640]{1,0:T(8,128)(2,1)S(1)} %get-tuple-element.22.g_ref, bf16[512,256]{1,0:T(8,128)(2,1)S(1)} %bitcast.3, ...), custom_call_target="tpu_custom_call" | custom-call | flops 3355443200 | bytes 4194304 | tf_op jit(solution)/shard_map/prompt/pallas_call | solution.py:266
  36.9 2.0 %collective-permute-start.1 = (f32[512,256]{1,0:T(8,128)S(1)}, f32[512,256]{1,0:T(8,128)S(1)}, u32[]{:S(2)}, u32[]{:S(2)}) collective-permute-start(f32[512,256]{1,0:T(8,128)S(1)} %get-tuple-element.32), channel_id=1, source_target_pairs={{0,4},{4,0},{8,12},{12,8},{16,20},{20,16},{24,28},{28,24},{32,36},... | collective-permute-start | bytes 1572872 | tf_op jit(solution)/shard_map/ppermute | solution.py:292
  38.9 1.8 %collective-permute-done.1 = f32[512,256]{1,0:T(8,128)S(1)} collective-permute-done((f32[512,256]{1,0:T(8,128)S(1)}, f32[512,256]{1,0:T(8,128)S(1)}, u32[]{:S(2)}, u32[]{:S(2)}) %collective-permute-start.1) | collective-permute-done | bytes 524320 | tf_op jit(solution)/shard_map/ppermute | solution.py:292
  40.7 0.7 %add_convert_fusion = bf16[512,256]{1,0:T(8,128)(2,1)} fusion(f32[512,256]{1,0:T(8,128)S(1)} %get-tuple-element.31, f32[512,256]{1,0:T(8,128)S(1)} %collective-permute-done.1), kind=kLoop, calls=%fused_computation.1 | loop fusion | flops 262144 | bytes 1310720 | tf_op jit(solution)/shard_map/convert_element_type | solution.py:293
  41.4 3.5 %all-to-all-start.1 = ((bf16[16,32,256]{2,1,0:T(8,128)(2,1)}), bf16[16,32,256]{2,1,0:T(8,128)(2,1)S(1)}, u32[]{:S(2)}, u32[]{:S(2)}) async-start(bf16[16,32,256]{2,1,0:T(8,128)(2,1)} %bitcast.1), calls=%async_computation.1 | async-start | bytes 524288 | tf_op jit(solution)/shard_map/all_to_all | solution.py:294
  45.0 6.2 %own_grad.1 = (f32[512,640]{1,0:T(8,128)}, f32[512,128]{1,0:T(8,128)}, f32[512,128]{1,0:T(8,128)}) custom-call(bf16[512,640]{1,0:T(8,128)(2,1)S(1)} %get-tuple-element.20.q_ref, bf16[512,640]{1,0:T(8,128)(2,1)S(1)} %get-tuple-element.22.g_ref, bf16[512,128]{1,0:T(8,128)(2,1)} %k_ref.5, bf16[512,128]{1,0:T(8,128)(2,1)} %v_ref.5, ...), custom_call_target="tpu_custom_call" | custom-call | flops 1258291200 | bytes 4194304 | tf_op jit(solution)/shard_map/own_grad/pallas_call | solution.py:297
  51.2 6.8 %all-to-all-done.1 = bf16[16,32,256]{2,1,0:T(8,128)(2,1)S(1)} async-done(((bf16[16,32,256]{2,1,0:T(8,128)(2,1)}), bf16[16,32,256]{2,1,0:T(8,128)(2,1)S(1)}, u32[]{:S(2)}, u32[]{:S(2)}) %all-to-all-start.1) | async-done | bytes 262176 | tf_op jit(solution)/shard_map/all_to_all | solution.py:294
  58.0 0.6 %fusion = (f32[32,128]{1,0:T(8,128)}, f32[32,128]{1,0:T(8,128)}) fusion(f32[32,256]{1,0:T(8,128)S(1)} %convert_reduce_fusion), kind=kLoop, calls=%fused_computation.2 | loop fusion | bytes 65536 | tf_op jit(solution)/shard_map/slice | solution.py:316
  (1 shorter events, 0.0 us)
Async XLA Ops:
  2.1 21.1 %all-to-all-start = ((bf16[16,32,256]{2,1,0:T(8,128)(2,1)}), bf16[16,32,256]{2,1,0:T(8,128)(2,1)S(1)}, u32[]{:S(2)}, u32[]{:S(2)}) async-start(bf16[16,32,256]{2,1,0:T(8,128)(2,1)} %spread.1), calls=%async_computation | async-start | bytes 524288 | tf_op jit(solution)/shard_map/all_to_all | solution.py:245
  23.1 3.4 %collective-permute-start = (bf16[512,256]{1,0:T(8,128)(2,1)S(1)}, bf16[512,256]{1,0:T(8,128)(2,1)S(1)}, u32[]{:S(2)}, u32[]{:S(2)}) collective-permute-start(bf16[512,256]{1,0:T(8,128)(2,1)S(1)} %bitcast.2), channel_id=1, source_target_pairs={{0,4},{4,0},{8,12},{12,8},{16,20},{20,16},{24,28},{28,24},{32,36},... | collective-permute-start | bytes 786440 | tf_op jit(solution)/shard_map/ppermute | solution.py:264
  36.9 3.8 %collective-permute-start.1 = (f32[512,256]{1,0:T(8,128)S(1)}, f32[512,256]{1,0:T(8,128)S(1)}, u32[]{:S(2)}, u32[]{:S(2)}) collective-permute-start(f32[512,256]{1,0:T(8,128)S(1)} %get-tuple-element.32), channel_id=1, source_target_pairs={{0,4},{4,0},{8,12},{12,8},{16,20},{20,16},{24,28},{28,24},{32,36},... | collective-permute-start | bytes 1572872 | tf_op jit(solution)/shard_map/ppermute | solution.py:292
  41.4 16.6 %all-to-all-start.1 = ((bf16[16,32,256]{2,1,0:T(8,128)(2,1)}), bf16[16,32,256]{2,1,0:T(8,128)(2,1)S(1)}, u32[]{:S(2)}, u32[]{:S(2)}) async-start(bf16[16,32,256]{2,1,0:T(8,128)(2,1)} %bitcast.1), calls=%async_computation.1 | async-start | bytes 524288 | tf_op jit(solution)/shard_map/all_to_all | solution.py:294

commit v3 on v2

--- a/solution.py
+++ b/solution.py
@@ -39,10 +39,18 @@
     return pl.ds(pl.multiple_of(head * HD, HD), HD)
 
 
-def spread_kernel(k_ref, v_ref, out_ref):
+def spread_kernel(k_ref, v_ref, out_ref, held_ref, sems):
+    copies = [
+        pltpu.make_async_copy(src, held_ref.at[i], sems.at[i])
+        for i, src in enumerate((k_ref, v_ref))
+    ]
+    for copy in copies:
+        copy.start()
+    for copy in copies:
+        copy.wait()
     for chip in range(out_ref.shape[0]):
-        out_ref[chip, :, 0:HD] = k_ref[...]
-        out_ref[chip, :, HD:] = v_ref[...]
+        out_ref[chip, :, 0:HD] = held_ref[0]
+        out_ref[chip, :, HD:] = held_ref[1]
 
 
 def own_stats_kernel(
@@ -79,7 +87,7 @@
 def prompt_kernel(
     q_ref, g_ref, mine_ref, other_ref, max_ref, sum_ref, del_ref,
     dq_ref, keep_ref, send_ref, lse_ref, delta_ref,
-    grad_ref, kt_ref, kv_ref, *scratch,
+    grad_ref, kt_ref, vt_ref, ks_ref, v_ref, *scratch,
 ):
     half = mine_ref.shape[0]
     tokens = 2 * half
@@ -90,46 +98,58 @@
         return slice(block * QB, (block + 1) * QB)
 
     def scores(head, block):
-        s_ref, dp_ref, _, _, top_ref = sets[block]
-        s = dot_nt(kv_ref[:, 0:HD], q_ref[rows(block), lanes(head)])
+        s_ref, _, _, _, top_ref = sets[block]
+        q = q_ref[rows(block), lanes(head)]
+        s = dot_nt(ks_ref[...], jnp.concatenate([q, q], axis=1))
         s_ref[...] = s
         top_ref[...] = jnp.max(s.reshape(tokens // 8, 8, QB), axis=0)
-        dp_ref[...] = dot_nt(kv_ref[:, HD:], g_ref[rows(block), lanes(head)])
 
     def softmax(head, block):
-        s_ref, dp_ref, p_ref, d_ref, top_ref = sets[block]
+        s_ref, prob_ref, p_ref, _, top_ref = sets[block]
         own_top = max_ref[head, :, rows(block)]
-        top = jnp.max(top_ref[...], axis=0, keepdims=True) * C2
-        top = jnp.maximum(top, own_top)
+        top = jnp.maximum(jnp.max(top_ref[...], axis=0, keepdims=True), own_top)
         own = jnp.exp2(own_top - top)
         total = jnp.zeros((8, QB), F32)
-        delta = jnp.zeros((8, QB), F32)
         for t in range(0, tokens, tile):
-            e = jnp.exp2(s_ref[t : t + tile, :] * C2 - top)
+            e = jnp.exp2(s_ref[t : t + tile, :] - top)
+            s_ref[t : t + tile, :] = e
             total = total + jnp.sum(e.reshape(tile // 8, 8, QB), axis=0)
-            ed = e * dp_ref[t : t + tile, :]
-            delta = delta + jnp.sum(ed.reshape(tile // 8, 8, QB), axis=0)
         total = jnp.sum(total, axis=0, keepdims=True) + own * sum_ref[head, :, rows(block)]
-        delta = jnp.sum(delta, axis=0, keepdims=True) + own * del_ref[head, :, rows(block)]
-        delta = delta * (1.0 / total)
-        lse = top + jnp.log2(total)
-        lse_ref[head, :, rows(block)] = lse
-        delta_ref[head, :, rows(block)] = delta
+        inverse = 1.0 / total
+        lse_ref[head, :, rows(block)] = top + jnp.log2(total)
         for t in range(0, tokens, tile):
-            p = jnp.exp2(s_ref[t : t + tile, :] * C2 - lse)
+            p = s_ref[t : t + tile, :] * inverse
+            prob_ref[t : t + tile, :] = p
             p_ref[t : t + tile, :] = p.astype(BF16)
-            d_ref[t : t + tile, :] = (p * (dp_ref[t : t + tile, :] - delta)).astype(BF16)
+        attended = dot(vt_ref[...], p_ref[...])
+        g = g_ref[rows(block), lanes(head)].T.astype(F32)
+        delta = jnp.sum(attended * g, axis=0, keepdims=True)
+        delta_ref[head, :, rows(block)] = delta + own * inverse * del_ref[head, :, rows(block)]
 
     def grads(head, block):
-        _, _, p_ref, d_ref, _ = sets[block]
-        grad_ref[0:HD, :] += dot_nt(q_ref[rows(block), lanes(head)].T, d_ref[...])
-        grad_ref[HD:, :] += dot_nt(g_ref[rows(block), lanes(head)].T, p_ref[...])
+        _, prob_ref, p_ref, d_ref, _ = sets[block]
+        q = q_ref[rows(block), lanes(head)]
+        g = g_ref[rows(block), lanes(head)]
+        delta = delta_ref[head, :, rows(block)]
+        ds = prob_ref[...] * (dot_nt(v_ref[...], g) - delta)
+        d_ref[...] = ds.astype(BF16)
+        grad_ref[HD:, :] += dot_nt(g.T, p_ref[...])
+        grad_ref[0:HD, :] += dot_nt(q.T, d_ref[...])
         dq_ref[head, :, rows(block)] = dot(kt_ref[...], d_ref[...])
 
-    kv_ref[0:half, :] = mine_ref[...]
-    kv_ref[half:, :] = other_ref[...]
-    kt_ref[...] = kv_ref[:, 0:HD].T
+    for first, side_ref in ((0, mine_ref), (half, other_ref)):
+        part = slice(first, first + half)
+        keys = side_ref[:, 0:HD]
+        values = side_ref[:, HD:]
+        kt_ref[:, part] = keys.T
+        vt_ref[:, part] = values.T
+        v_ref[part, :] = values
+        scaled = keys.astype(F32) * C2
+        high = scaled.astype(BF16)
+        ks_ref[part, 0:HD] = high
+        ks_ref[part, HD:] = (scaled - high.astype(F32)).astype(BF16)
     grad_ref[...] = jnp.zeros_like(grad_ref)
+
     scores(0, 0)
     scores(0, 1)
     softmax(0, 0)
@@ -237,11 +257,12 @@
     same_core = [[2 * chip + core for chip in range(chips)] for core in range(2)]
     spread = pl.pallas_call(
         spread_kernel,
-        in_specs=[VMEM, VMEM],
+        in_specs=[pl.BlockSpec(memory_space=pltpu.HBM)] * 2,
         out_specs=VMEM,
         out_shape=struct((chips, SHARD, 2 * HD), BF16),
+        scratch_shapes=[pltpu.VMEM((2, SHARD, HD), BF16), pltpu.SemaphoreType.DMA((2,))],
         name="spread",
-    )(hbm(prompt_keys), hbm(prompt_values))
+    )(prompt_keys, prompt_values)
     mine = lax.all_to_all(spread, "comp", 0, 0, axis_index_groups=same_core, tiled=True)
     mine = mine.reshape(half, 2 * HD)
 
@@ -274,7 +295,9 @@
         scratch_shapes=[
             pltpu.VMEM((2 * HD, tokens), F32),
             pltpu.VMEM((HD, tokens), BF16),
+            pltpu.VMEM((HD, tokens), BF16),
             pltpu.VMEM((tokens, 2 * HD), BF16),
+            pltpu.VMEM((tokens, HD), BF16),
         ]
         + [
             pltpu.VMEM((tokens, QB), F32),

time: 59.2 us -> 59.4 us (level)
  no operation moved by 1% of the time
where the time goes in v3:
time: 59.4 us; the launch traced here: 58.9 us
  Pallas kernels  22.7 us (38%)
  waiting for transfers between devices  16.9 us (28%)
  starting transfers between devices  16.5 us (28%)
  between operations  1.34 us (2%)
  other arithmetic  0.79 us (1%)
  local copies, waits for them, and re-layouts  0.61 us (1%)
    pallas_call x1, Pallas kernels, per_device(): pl.pallas_call(prompt_kernel, in_specs=[VMEM] * 7, out_specs=[VMEM] * 5,...  10.5 us
    all_to_all x1, starting transfers between devices, per_device(): lax.all_to_all(spread, 'comp', 0, 0, axis_index_groups=same_core, tiled=T...  9.03 us
    all_to_all x1, waiting for transfers between devices, per_device(): lax.all_to_all(spread, 'comp', 0, 0, axis_index_groups=same_core, tiled=T...  6.83 us
    all_to_all x1, waiting for transfers between devices, per_device(): lax.all_to_all(total, 'comp', 0, 0, axis_index_groups=same_core, tiled=True)  6.79 us
    pallas_call x1, Pallas kernels, per_device(): pl.pallas_call(own_grad_kernel, grid=(GROUP,), in_specs=[VMEM, VMEM, whol...  6.22 us
    pallas_call x1, Pallas kernels, per_device(): pl.pallas_call(own_stats_kernel, grid=(GROUP,), in_specs=[SMEM, HEAD, HEA...  4.55 us
    all_to_all x1, starting transfers between devices, per_device(): lax.all_to_all(total, 'comp', 0, 0, axis_index_groups=same_core, tiled=True)  3.53 us
    ppermute x1, starting transfers between devices, per_device(): received = lax.ppermute(grad_send, 'comp', swap)  2.04 us
  transfers between devices with their start and end apart: 4, of which 4 were waited for; matrix products, arithmetic and copies ran while one was open for 0% of the time, Pallas kernels for 18%

profile of v3, /device:TPU:6, one launch (start us, length us, event | category | flops | bytes accessed | tf_op | source)
XLA Modules:
  0.0 58.9 jit_solution(931158961283507572)
XLA Ops:
  0.6 1.5 %spread.1 = bf16[16,32,256]{2,1,0:T(8,128)(2,1)} custom-call(bf16[32,128]{1,0:T(8,128)(2,1)} %k_ref.4, bf16[32,128]{1,0:T(8,128)(2,1)} %v_ref.4), custom_call_target="tpu_custom_call" | custom-call | tf_op jit(solution)/shard_map/spread/pallas_call | solution.py:258
  2.1 9.0 %all-to-all-start = ((bf16[16,32,256]{2,1,0:T(8,128)(2,1)}), bf16[16,32,256]{2,1,0:T(8,128)(2,1)S(1)}, u32[]{:S(2)}, u32[]{:S(2)}) async-start(bf16[16,32,256]{2,1,0:T(8,128)(2,1)} %spread.1), calls=%async_computation | async-start | bytes 524288 | tf_op jit(solution)/shard_map/all_to_all | solution.py:266
  11.8 4.5 %own_stats.1 = (bf16[512,640]{1,0:T(8,128)(2,1)S(1)}, bf16[512,640]{1,0:T(8,128)(2,1)S(1)}, f32[5,1,512]{2,1,0:T(1,128)S(1)}, f32[5,1,512]{2,1,0:T(1,128)S(1)}, f32[5,1,512]{2,1,0:T(1,128)S(1)}) custom-call(s32[1]{0:T(128)S(6)} %copy.12.len_ref, bf16[512,640]{1,0:T(8,128)(2,1)} %q_ref.1, bf16[512,640]{1,0:T(8,128)(2,1)} %g_ref.1, bf16[512,128]{1,0:T(8,128)(2,1)} %k_ref.5, ...), custom_call_target="tpu_custom_call" | custom-call | flops 503316480 | bytes 2097152 | tf_op jit(solution)/shard_map/own_stats/pallas_call | solution.py:270
  16.3 6.8 %all-to-all-done = bf16[16,32,256]{2,1,0:T(8,128)(2,1)S(1)} async-done(((bf16[16,32,256]{2,1,0:T(8,128)(2,1)}), bf16[16,32,256]{2,1,0:T(8,128)(2,1)S(1)}, u32[]{:S(2)}, u32[]{:S(2)}) %all-to-all-start) | async-done | bytes 262176 | tf_op jit(solution)/shard_map/all_to_all | solution.py:266
  23.2 1.9 %collective-permute-start = (bf16[512,256]{1,0:T(8,128)(2,1)S(1)}, bf16[512,256]{1,0:T(8,128)(2,1)S(1)}, u32[]{:S(2)}, u32[]{:S(2)}) collective-permute-start(bf16[512,256]{1,0:T(8,128)(2,1)S(1)} %bitcast.2), channel_id=1, source_target_pairs={{0,4},{4,0},{8,12},{12,8},{16,20},{20,16},{24,28},{28,24},{32,36},... | collective-permute-start | bytes 786440 | tf_op jit(solution)/shard_map/ppermute | solution.py:285
  25.1 1.5 %collective-permute-done.other_ref = bf16[512,256]{1,0:T(8,128)(2,1)S(1)} collective-permute-done((bf16[512,256]{1,0:T(8,128)(2,1)S(1)}, bf16[512,256]{1,0:T(8,128)(2,1)S(1)}, u32[]{:S(2)}, u32[]{:S(2)}) %collective-permute-start) | collective-permute-done | bytes 262176 | tf_op jit(solution)/shard_map/ppermute | solution.py:285
  26.6 10.5 %prompt.1 = (f32[5,128,512]{2,1,0:T(8,128)S(1)}, f32[512,256]{1,0:T(8,128)S(1)}, f32[512,256]{1,0:T(8,128)S(1)}, f32[5,1,512]{2,1,0:T(1,128)S(1)}, f32[5,1,512]{2,1,0:T(1,128)S(1)}) custom-call(bf16[512,640]{1,0:T(8,128)(2,1)S(1)} %get-tuple-element.20.q_ref, bf16[512,640]{1,0:T(8,128)(2,1)S(1)} %get-tuple-element.22.g_ref, bf16[512,256]{1,0:T(8,128)(2,1)S(1)} %bitcast.3, ...), custom_call_target="tpu_custom_call" | custom-call | flops 3355443200 | bytes 4194304 | tf_op jit(solution)/shard_map/prompt/pallas_call | solution.py:287
  37.1 2.0 %collective-permute-start.1 = (f32[512,256]{1,0:T(8,128)S(1)}, f32[512,256]{1,0:T(8,128)S(1)}, u32[]{:S(2)}, u32[]{:S(2)}) collective-permute-start(f32[512,256]{1,0:T(8,128)S(1)} %get-tuple-element.32), channel_id=1, source_target_pairs={{0,4},{4,0},{8,12},{12,8},{16,20},{20,16},{24,28},{28,24},{32,36},... | collective-permute-start | bytes 1572872 | tf_op jit(solution)/shard_map/ppermute | solution.py:315
  39.2 1.8 %collective-permute-done.1 = f32[512,256]{1,0:T(8,128)S(1)} collective-permute-done((f32[512,256]{1,0:T(8,128)S(1)}, f32[512,256]{1,0:T(8,128)S(1)}, u32[]{:S(2)}, u32[]{:S(2)}) %collective-permute-start.1) | collective-permute-done | bytes 524320 | tf_op jit(solution)/shard_map/ppermute | solution.py:315
  40.9 0.7 %add_convert_fusion = bf16[512,256]{1,0:T(8,128)(2,1)} fusion(f32[512,256]{1,0:T(8,128)S(1)} %get-tuple-element.31, f32[512,256]{1,0:T(8,128)S(1)} %collective-permute-done.1), kind=kLoop, calls=%fused_computation.1 | loop fusion | flops 262144 | bytes 1310720 | tf_op jit(solution)/shard_map/convert_element_type | solution.py:316
  41.7 3.5 %all-to-all-start.1 = ((bf16[16,32,256]{2,1,0:T(8,128)(2,1)}), bf16[16,32,256]{2,1,0:T(8,128)(2,1)S(1)}, u32[]{:S(2)}, u32[]{:S(2)}) async-start(bf16[16,32,256]{2,1,0:T(8,128)(2,1)} %bitcast.1), calls=%async_computation.1 | async-start | bytes 524288 | tf_op jit(solution)/shard_map/all_to_all | solution.py:317
  45.2 6.2 %own_grad.1 = (f32[512,640]{1,0:T(8,128)}, f32[512,128]{1,0:T(8,128)}, f32[512,128]{1,0:T(8,128)}) custom-call(bf16[512,640]{1,0:T(8,128)(2,1)S(1)} %get-tuple-element.20.q_ref, bf16[512,640]{1,0:T(8,128)(2,1)S(1)} %get-tuple-element.22.g_ref, bf16[512,128]{1,0:T(8,128)(2,1)} %k_ref.5, bf16[512,128]{1,0:T(8,128)(2,1)} %v_ref.5, ...), custom_call_target="tpu_custom_call" | custom-call | flops 1258291200 | bytes 4194304 | tf_op jit(solution)/shard_map/own_grad/pallas_call | solution.py:320
  51.4 6.8 %all-to-all-done.1 = bf16[16,32,256]{2,1,0:T(8,128)(2,1)S(1)} async-done(((bf16[16,32,256]{2,1,0:T(8,128)(2,1)}), bf16[16,32,256]{2,1,0:T(8,128)(2,1)S(1)}, u32[]{:S(2)}, u32[]{:S(2)}) %all-to-all-start.1) | async-done | bytes 262176 | tf_op jit(solution)/shard_map/all_to_all | solution.py:317
  58.3 0.6 %fusion = (f32[32,128]{1,0:T(8,128)}, f32[32,128]{1,0:T(8,128)}) fusion(f32[32,256]{1,0:T(8,128)S(1)} %convert_reduce_fusion), kind=kLoop, calls=%fused_computation.2 | loop fusion | bytes 65536 | tf_op jit(solution)/shard_map/slice | solution.py:339
  (1 shorter events, 0.0 us)
Async XLA Ops:
  2.1 21.1 %all-to-all-start = ((bf16[16,32,256]{2,1,0:T(8,128)(2,1)}), bf16[16,32,256]{2,1,0:T(8,128)(2,1)S(1)}, u32[]{:S(2)}, u32[]{:S(2)}) async-start(bf16[16,32,256]{2,1,0:T(8,128)(2,1)} %spread.1), calls=%async_computation | async-start | bytes 524288 | tf_op jit(solution)/shard_map/all_to_all | solution.py:266
  23.2 3.4 %collective-permute-start = (bf16[512,256]{1,0:T(8,128)(2,1)S(1)}, bf16[512,256]{1,0:T(8,128)(2,1)S(1)}, u32[]{:S(2)}, u32[]{:S(2)}) collective-permute-start(bf16[512,256]{1,0:T(8,128)(2,1)S(1)} %bitcast.2), channel_id=1, source_target_pairs={{0,4},{4,0},{8,12},{12,8},{16,20},{20,16},{24,28},{28,24},{32,36},... | collective-permute-start | bytes 786440 | tf_op jit(solution)/shard_map/ppermute | solution.py:285
  37.1 3.8 %collective-permute-start.1 = (f32[512,256]{1,0:T(8,128)S(1)}, f32[512,256]{1,0:T(8,128)S(1)}, u32[]{:S(2)}, u32[]{:S(2)}) collective-permute-start(f32[512,256]{1,0:T(8,128)S(1)} %get-tuple-element.32), channel_id=1, source_target_pairs={{0,4},{4,0},{8,12},{12,8},{16,20},{20,16},{24,28},{28,24},{32,36},... | collective-permute-start | bytes 1572872 | tf_op jit(solution)/shard_map/ppermute | solution.py:315
  41.7 16.6 %all-to-all-start.1 = ((bf16[16,32,256]{2,1,0:T(8,128)(2,1)}), bf16[16,32,256]{2,1,0:T(8,128)(2,1)S(1)}, u32[]{:S(2)}, u32[]{:S(2)}) async-start(bf16[16,32,256]{2,1,0:T(8,128)(2,1)} %bitcast.1), calls=%async_computation.1 | async-start | bytes 524288 | tf_op jit(solution)/shard_map/all_to_all | solution.py:317

commit v4 on v3

--- a/solution.py
+++ b/solution.py
@@ -48,9 +48,9 @@
         copy.start()
     for copy in copies:
         copy.wait()
-    for chip in range(out_ref.shape[0]):
-        out_ref[chip, :, 0:HD] = held_ref[0]
-        out_ref[chip, :, HD:] = held_ref[1]
+    for device in range(out_ref.shape[0]):
+        out_ref[device, :, 0:HD] = held_ref[0]
+        out_ref[device, :, HD:] = held_ref[1]
 
 
 def own_stats_kernel(
@@ -85,94 +85,81 @@
 
 
 def prompt_kernel(
-    q_ref, g_ref, mine_ref, other_ref, max_ref, sum_ref, del_ref,
-    dq_ref, keep_ref, send_ref, lse_ref, delta_ref,
-    grad_ref, kt_ref, vt_ref, ks_ref, v_ref, *scratch,
+    q_ref, g_ref, kv_ref, max_ref, sum_ref, del_ref,
+    dq_ref, grad_ref, lse_ref, delta_ref,
+    total_ref, kt_ref, ks_ref, *scratch,
 ):
-    half = mine_ref.shape[0]
-    tokens = 2 * half
+    tokens = kv_ref.shape[0]
     tile = 64
-    sets = (scratch[0:5], scratch[5:10])
-
-    def rows(block):
-        return slice(block * QB, (block + 1) * QB)
-
-    def scores(head, block):
-        s_ref, _, _, _, top_ref = sets[block]
-        q = q_ref[rows(block), lanes(head)]
+    blocks = MAXLEN // QB
+    items = GROUP * blocks
+
+    def place(item):
+        head, block = divmod(item, blocks)
+        return head, slice(block * QB, (block + 1) * QB), slice(head * HD, (head + 1) * HD)
+
+    def buffers(item):
+        return scratch[item % 2 * 5 : item % 2 * 5 + 5]
+
+    def scores(item):
+        _, rows, cols = place(item)
+        s_ref, dp_ref, _, _, top_ref = buffers(item)
+        q = q_ref[rows, cols]
         s = dot_nt(ks_ref[...], jnp.concatenate([q, q], axis=1))
         s_ref[...] = s
         top_ref[...] = jnp.max(s.reshape(tokens // 8, 8, QB), axis=0)
-
-    def softmax(head, block):
-        s_ref, prob_ref, p_ref, _, top_ref = sets[block]
-        own_top = max_ref[head, :, rows(block)]
+        dp_ref[...] = dot_nt(kv_ref[:, HD:], g_ref[rows, cols])
+
+    def softmax(item):
+        head, rows, _ = place(item)
+        s_ref, dp_ref, p_ref, d_ref, top_ref = buffers(item)
+        own_top = max_ref[head, :, rows]
         top = jnp.maximum(jnp.max(top_ref[...], axis=0, keepdims=True), own_top)
         own = jnp.exp2(own_top - top)
         total = jnp.zeros((8, QB), F32)
+        delta = jnp.zeros((8, QB), F32)
         for t in range(0, tokens, tile):
             e = jnp.exp2(s_ref[t : t + tile, :] - top)
             s_ref[t : t + tile, :] = e
             total = total + jnp.sum(e.reshape(tile // 8, 8, QB), axis=0)
-        total = jnp.sum(total, axis=0, keepdims=True) + own * sum_ref[head, :, rows(block)]
+            ed = e * dp_ref[t : t + tile, :]
+            delta = delta + jnp.sum(ed.reshape(tile // 8, 8, QB), axis=0)
+        total = jnp.sum(total, axis=0, keepdims=True) + own * sum_ref[head, :, rows]
+        delta = jnp.sum(delta, axis=0, keepdims=True) + own * del_ref[head, :, rows]
         inverse = 1.0 / total
-        lse_ref[head, :, rows(block)] = top + jnp.log2(total)
+        delta = delta * inverse
+        lse_ref[head, :, rows] = top + jnp.log2(total)
+        delta_ref[head, :, rows] = delta
         for t in range(0, tokens, tile):
             p = s_ref[t : t + tile, :] * inverse
-            prob_ref[t : t + tile, :] = p
             p_ref[t : t + tile, :] = p.astype(BF16)
-        attended = dot(vt_ref[...], p_ref[...])
-        g = g_ref[rows(block), lanes(head)].T.astype(F32)
-        delta = jnp.sum(attended * g, axis=0, keepdims=True)
-        delta_ref[head, :, rows(block)] = delta + own * inverse * del_ref[head, :, rows(block)]
-
-    def grads(head, block):
-        _, prob_ref, p_ref, d_ref, _ = sets[block]
-        q = q_ref[rows(block), lanes(head)]
-        g = g_ref[rows(block), lanes(head)]
-        delta = delta_ref[head, :, rows(block)]
-        ds = prob_ref[...] * (dot_nt(v_ref[...], g) - delta)
-        d_ref[...] = ds.astype(BF16)
-        grad_ref[HD:, :] += dot_nt(g.T, p_ref[...])
-        grad_ref[0:HD, :] += dot_nt(q.T, d_ref[...])
-        dq_ref[head, :, rows(block)] = dot(kt_ref[...], d_ref[...])
-
-    for first, side_ref in ((0, mine_ref), (half, other_ref)):
-        part = slice(first, first + half)
-        keys = side_ref[:, 0:HD]
-        values = side_ref[:, HD:]
-        kt_ref[:, part] = keys.T
-        vt_ref[:, part] = values.T
-        v_ref[part, :] = values
-        scaled = keys.astype(F32) * C2
-        high = scaled.astype(BF16)
-        ks_ref[part, 0:HD] = high
-        ks_ref[part, HD:] = (scaled - high.astype(F32)).astype(BF16)
-    grad_ref[...] = jnp.zeros_like(grad_ref)
-
-    scores(0, 0)
-    scores(0, 1)
-    softmax(0, 0)
-
-    def body(head, carry):
-        scores(head, 0)
-        softmax(head - 1, 1)
-        grads(head - 1, 0)
-        scores(head, 1)
-        softmax(head, 0)
-        grads(head - 1, 1)
-        return carry
-
-    lax.fori_loop(1, GROUP, body, 0)
-    softmax(GROUP - 1, 1)
-    grads(GROUP - 1, 0)
-    grads(GROUP - 1, 1)
-
-    for base, out in ((0, keep_ref), (half, send_ref)):
-        for t in range(0, half, HD):
-            take = slice(base + t, base + t + HD)
-            out[t : t + HD, 0:HD] = grad_ref[0:HD, take].T * SCALE
-            out[t : t + HD, HD:] = grad_ref[HD:, take].T
+            d_ref[t : t + tile, :] = (p * (dp_ref[t : t + tile, :] - delta)).astype(BF16)
+
+    def grads(item):
+        head, rows, cols = place(item)
+        _, _, p_ref, d_ref, _ = buffers(item)
+        total_ref[:, HD:] += dot(p_ref[...], g_ref[rows, cols])
+        total_ref[:, 0:HD] += dot(d_ref[...], q_ref[rows, cols])
+        dq_ref[head, :, rows] = dot(kt_ref[...], d_ref[...])
+
+    keys = kv_ref[:, 0:HD]
+    kt_ref[...] = keys.T
+    scaled = keys.astype(F32) * C2
+    high = scaled.astype(BF16)
+    ks_ref[:, 0:HD] = high
+    ks_ref[:, HD:] = (scaled - high.astype(F32)).astype(BF16)
+    total_ref[...] = jnp.zeros_like(total_ref)
+
+    for step in range(-1, items + 1):
+        if step + 1 < items:
+            scores(step + 1)
+        if 0 <= step < items:
+            softmax(step)
+        if step >= 1:
+            grads(step - 1)
+
+    grad_ref[:, 0:HD] = (total_ref[:, 0:HD] * SCALE).astype(BF16)
+    grad_ref[:, HD:] = total_ref[:, HD:].astype(BF16)
 
 
 def own_grad_kernel(
@@ -248,23 +235,18 @@
 
 def per_device(queries, comp_keys, comp_values, out_grad, prompt_keys, prompt_values, lengths):
     devices = lax.axis_size("comp")
-    half = devices * SHARD // 2
-    tokens = 2 * half
+    tokens = devices * SHARD
     width = GROUP * HD
 
-    chips = devices // 2
-    swap = [(d, d ^ 1) for d in range(devices)]
-    same_core = [[2 * chip + core for chip in range(chips)] for core in range(2)]
     spread = pl.pallas_call(
         spread_kernel,
         in_specs=[pl.BlockSpec(memory_space=pltpu.HBM)] * 2,
         out_specs=VMEM,
-        out_shape=struct((chips, SHARD, 2 * HD), BF16),
+        out_shape=struct((devices, SHARD, 2 * HD), BF16),
         scratch_shapes=[pltpu.VMEM((2, SHARD, HD), BF16), pltpu.SemaphoreType.DMA((2,))],
         name="spread",
     )(prompt_keys, prompt_values)
-    mine = lax.all_to_all(spread, "comp", 0, 0, axis_index_groups=same_core, tiled=True)
-    mine = mine.reshape(half, 2 * HD)
+    prompt = lax.all_to_all(spread, "comp", 0, 0, tiled=True)
 
     stat = struct((GROUP, 1, MAXLEN), F32)
     copied, masked, own_max, own_sum, own_del = pl.pallas_call(
@@ -281,23 +263,19 @@
         name="own_stats",
     )(lengths, hbm(queries), hbm(out_grad), hbm(comp_keys), hbm(comp_values))
 
-    mine, masked = lax.optimization_barrier((mine, masked))
-    other = lax.ppermute(mine, "comp", swap)
-
-    past, grad_keep, grad_send, lse, delta = pl.pallas_call(
+    prompt, masked = lax.optimization_barrier((prompt, masked))
+
+    past, grad_part, lse, delta = pl.pallas_call(
         prompt_kernel,
-        in_specs=[VMEM] * 7,
-        out_specs=[VMEM] * 5,
+        in_specs=[VMEM] * 6,
+        out_specs=[VMEM] * 4,
         out_shape=[
-            struct((GROUP, HD, MAXLEN), F32),
-            struct((half, 2 * HD), F32), struct((half, 2 * HD), F32), stat, stat,
+            struct((GROUP, HD, MAXLEN), F32), struct((tokens, 2 * HD), BF16), stat, stat,
         ],
         scratch_shapes=[
-            pltpu.VMEM((2 * HD, tokens), F32),
-            pltpu.VMEM((HD, tokens), BF16),
+            pltpu.VMEM((tokens, 2 * HD), F32),
             pltpu.VMEM((HD, tokens), BF16),
             pltpu.VMEM((tokens, 2 * HD), BF16),
-            pltpu.VMEM((tokens, HD), BF16),
         ]
         + [
             pltpu.VMEM((tokens, QB), F32),
@@ -308,13 +286,14 @@
         ]
         * 2,
         compiler_params=pltpu.CompilerParams(vmem_limit_bytes=VMEM_LIMIT),
-        cost_estimate=cost(GROUP * 10 * 1024 * 512 * HD, GROUP * 2048 * 512, 2**22),
+        cost_estimate=cost(GROUP * 10 * 1024 * 512 * HD, GROUP * 1024 * 512, 2**22),
         name="prompt",
-    )(vmem(copied), vmem(masked), mine, other, own_max, own_sum, own_del)
-
-    received = lax.ppermute(grad_send, "comp", swap)
-    total = (grad_keep + received).astype(BF16).reshape(chips, SHARD, 2 * HD)
-    arrived = lax.all_to_all(total, "comp", 0, 0, axis_index_groups=same_core, tiled=True)
+    )(
+        vmem(copied), vmem(masked), prompt.reshape(tokens, 2 * HD), own_max, own_sum, own_del,
+    )
+
+    parts = grad_part.reshape(devices, SHARD, 2 * HD)
+    arrived = lax.all_to_all(parts, "comp", 0, 0, tiled=True)
     grad_prompt = jnp.sum(arrived.astype(F32), axis=0)
 
     grad_queries, grad_comp_keys, grad_comp_values = pl.pallas_call(

time: 59.4 us -> 62.4 us (1.051)
  waiting for transfers between devices: 16.9 us -> 24.6 us
  starting transfers between devices: 16.5 us -> 13.2 us
  Pallas kernels: 22.7 us -> 21.9 us
  other arithmetic: 0.79 us -> 0.08 us
    all_to_all x2, waiting for transfers between devices: 13.6 us -> 24.6 us  [the longest x1 12.8 us: per_device(): prompt = lax.all_to_all(spread, 'comp', 0, 0, tiled=True)]
    ppermute x2 -> x0, starting transfers between devices: 3.95 us -> none  [the longest x1 2.04 us: per_device(): received = lax.ppermute(grad_send, 'comp', swap)]
    ppermute x2 -> x0, waiting for transfers between devices: 3.26 us -> none  [the longest x1 1.76 us: per_device(): received = lax.ppermute(grad_send, 'comp', swap)]
    pallas_call x1, Pallas kernels: 10.5 us -> 9.5 us  [per_device(): pl.pallas_call(prompt_kernel, in_specs=[VMEM] * 6, out_specs=[VMEM] * 4,...]
    convert_element_type x1 -> x0, other arithmetic: 0.75 us -> none  [per_device(): total = (grad_keep + received).astype(BF16).reshape(chips, SHARD, 2 * HD)]
    all_to_all x2, starting transfers between devices: 12.6 us -> 13.2 us  [the longest x1 9.31 us: per_device(): prompt = lax.all_to_all(spread, 'comp', 0, 0, tiled=True)]
  transfers between devices with their start and end apart: 4 -> 2, of which waited for: 4 -> 2; matrix products, arithmetic and copies ran while one was open for 0% -> 0% of each run, Pallas kernels for 18% -> 17%
where the time goes in v4:
time: 62.4 us; the launch traced here: 61.7 us
  waiting for transfers between devices  24.6 us (39%)
  Pallas kernels  21.9 us (35%)
  starting transfers between devices  13.2 us (21%)
  between operations  1.31 us (2%)
    all_to_all x1, waiting for transfers between devices, per_device(): prompt = lax.all_to_all(spread, 'comp', 0, 0, tiled=True)  12.8 us
    all_to_all x1, waiting for transfers between devices, per_device(): arrived = lax.all_to_all(parts, 'comp', 0, 0, tiled=True)  11.8 us
    pallas_call x1, Pallas kernels, per_device(): pl.pallas_call(prompt_kernel, in_specs=[VMEM] * 6, out_specs=[VMEM] * 4,...  9.5 us
    all_to_all x1, starting transfers between devices, per_device(): prompt = lax.all_to_all(spread, 'comp', 0, 0, tiled=True)  9.31 us
    pallas_call x1, Pallas kernels, per_device(): pl.pallas_call(own_grad_kernel, grid=(GROUP,), in_specs=[VMEM, VMEM, whol...  6.22 us
    pallas_call x1, Pallas kernels, per_device(): pl.pallas_call(own_stats_kernel, grid=(GROUP,), in_specs=[SMEM, HEAD, HEA...  4.56 us
    all_to_all x1, starting transfers between devices, per_device(): arrived = lax.all_to_all(parts, 'comp', 0, 0, tiled=True)  3.89 us
    pallas_call x1, Pallas kernels, per_device(): pl.pallas_call(spread_kernel, in_specs=[pl.BlockSpec(memory_space=pltpu.H...  1.59 us
  transfers between devices with their start and end apart: 2, of which 2 were waited for; matrix products, arithmetic and copies ran while one was open for 0% of the time, Pallas kernels for 17%

profile of v4, /device:TPU:6, one launch (start us, length us, event | category | flops | bytes accessed | tf_op | source)
XLA Modules:
  0.0 61.7 jit_solution(11025629460273565009)
XLA Ops:
  0.6 1.6 %spread.1 = bf16[32,32,256]{2,1,0:T(8,128)(2,1)} custom-call(bf16[32,128]{1,0:T(8,128)(2,1)} %k_ref.4, bf16[32,128]{1,0:T(8,128)(2,1)} %v_ref.4), custom_call_target="tpu_custom_call" | custom-call | tf_op jit(solution)/shard_map/spread/pallas_call | solution.py:241
  2.2 9.3 %all-to-all-start = ((bf16[32,32,256]{2,1,0:T(8,128)(2,1)}), bf16[32,32,256]{2,1,0:T(8,128)(2,1)S(1)}, u32[]{:S(2)}, u32[]{:S(2)}) async-start(bf16[32,32,256]{2,1,0:T(8,128)(2,1)} %spread.1), calls=%async_computation | async-start | bytes 1048576 | tf_op jit(solution)/shard_map/all_to_all | solution.py:249
  12.2 4.6 %own_stats.1 = (bf16[512,640]{1,0:T(8,128)(2,1)S(1)}, bf16[512,640]{1,0:T(8,128)(2,1)S(1)}, f32[5,1,512]{2,1,0:T(1,128)S(1)}, f32[5,1,512]{2,1,0:T(1,128)S(1)}, f32[5,1,512]{2,1,0:T(1,128)S(1)}) custom-call(s32[1]{0:T(128)S(6)} %copy.12.len_ref, bf16[512,640]{1,0:T(8,128)(2,1)} %q_ref.1, bf16[512,640]{1,0:T(8,128)(2,1)} %g_ref.1, bf16[512,128]{1,0:T(8,128)(2,1)} %k_ref.5, ...), custom_call_target="tpu_custom_call" | custom-call | flops 503316480 | bytes 2097152 | tf_op jit(solution)/shard_map/own_stats/pallas_call | solution.py:252
  16.8 12.8 %all-to-all-done = bf16[32,32,256]{2,1,0:T(8,128)(2,1)S(1)} async-done(((bf16[32,32,256]{2,1,0:T(8,128)(2,1)}), bf16[32,32,256]{2,1,0:T(8,128)(2,1)S(1)}, u32[]{:S(2)}, u32[]{:S(2)}) %all-to-all-start) | async-done | bytes 524320 | tf_op jit(solution)/shard_map/all_to_all | solution.py:249
  29.6 9.5 %prompt.1 = (f32[5,128,512]{2,1,0:T(8,128)S(1)}, bf16[1024,256]{1,0:T(8,128)(2,1)}, f32[5,1,512]{2,1,0:T(1,128)S(1)}, f32[5,1,512]{2,1,0:T(1,128)S(1)}) custom-call(bf16[512,640]{1,0:T(8,128)(2,1)S(1)} %get-tuple-element.19.q_ref, bf16[512,640]{1,0:T(8,128)(2,1)S(1)} %get-tuple-element.21.g_ref, bf16[1024,256]{1,0:T(8,128)(2,1)S(1)} %bitcast.2, ...), custom_call_target="tpu_custom_call" | custom-call | flops 3355443200 | bytes 4194304 | tf_op jit(solution)/shard_map/prompt/pallas_call | solution.py:268
  39.1 3.9 %all-to-all-start.1 = ((bf16[32,32,256]{2,1,0:T(8,128)(2,1)}), bf16[32,32,256]{2,1,0:T(8,128)(2,1)S(1)}, u32[]{:S(2)}, u32[]{:S(2)}) async-start(bf16[32,32,256]{2,1,0:T(8,128)(2,1)} %bitcast.1), calls=%async_computation.1 | async-start | bytes 1048576 | tf_op jit(solution)/shard_map/all_to_all | solution.py:296
  43.0 6.2 %own_grad.1 = (f32[512,640]{1,0:T(8,128)}, f32[512,128]{1,0:T(8,128)}, f32[512,128]{1,0:T(8,128)}) custom-call(bf16[512,640]{1,0:T(8,128)(2,1)S(1)} %get-tuple-element.19.q_ref, bf16[512,640]{1,0:T(8,128)(2,1)S(1)} %get-tuple-element.21.g_ref, bf16[512,128]{1,0:T(8,128)(2,1)} %k_ref.5, bf16[512,128]{1,0:T(8,128)(2,1)} %v_ref.5, ...), custom_call_target="tpu_custom_call" | custom-call | flops 1258291200 | bytes 4194304 | tf_op jit(solution)/shard_map/own_grad/pallas_call | solution.py:299
  49.2 11.8 %all-to-all-done.1 = bf16[32,32,256]{2,1,0:T(8,128)(2,1)S(1)} async-done(((bf16[32,32,256]{2,1,0:T(8,128)(2,1)}), bf16[32,32,256]{2,1,0:T(8,128)(2,1)S(1)}, u32[]{:S(2)}, u32[]{:S(2)}) %all-to-all-start.1) | async-done | bytes 524320 | tf_op jit(solution)/shard_map/all_to_all | solution.py:296
  61.0 0.1 convert_reduce_fusion
  61.1 0.6 fusion
Async XLA Ops:
  2.2 27.4 %all-to-all-start = ((bf16[32,32,256]{2,1,0:T(8,128)(2,1)}), bf16[32,32,256]{2,1,0:T(8,128)(2,1)S(1)}, u32[]{:S(2)}, u32[]{:S(2)}) async-start(bf16[32,32,256]{2,1,0:T(8,128)(2,1)} %spread.1), calls=%async_computation | async-start | bytes 1048576 | tf_op jit(solution)/shard_map/all_to_all | solution.py:249
  39.1 21.9 %all-to-all-start.1 = ((bf16[32,32,256]{2,1,0:T(8,128)(2,1)}), bf16[32,32,256]{2,1,0:T(8,128)(2,1)S(1)}, u32[]{:S(2)}, u32[]{:S(2)}) async-start(bf16[32,32,256]{2,1,0:T(8,128)(2,1)} %bitcast.1), calls=%async_computation.1 | async-start | bytes 1048576 | tf_op jit(solution)/shard_map/all_to_all | solution.py:296

commit v5 on v4

--- a/solution.py
+++ b/solution.py
@@ -48,9 +48,9 @@
         copy.start()
     for copy in copies:
         copy.wait()
-    for device in range(out_ref.shape[0]):
-        out_ref[device, :, 0:HD] = held_ref[0]
-        out_ref[device, :, HD:] = held_ref[1]
+    for chip in range(out_ref.shape[0]):
+        out_ref[chip, :, 0:HD] = held_ref[0]
+        out_ref[chip, :, HD:] = held_ref[1]
 
 
 def own_stats_kernel(
@@ -85,11 +85,12 @@
 
 
 def prompt_kernel(
-    q_ref, g_ref, kv_ref, max_ref, sum_ref, del_ref,
-    dq_ref, grad_ref, lse_ref, delta_ref,
-    total_ref, kt_ref, ks_ref, *scratch,
+    q_ref, g_ref, mine_ref, other_ref, max_ref, sum_ref, del_ref,
+    ds_ref, keep_ref, send_ref, lse_ref, delta_ref,
+    total_ref, ks_ref, v_ref, d_ref, prob_ref, sems, *scratch,
 ):
-    tokens = kv_ref.shape[0]
+    half = mine_ref.shape[0]
+    tokens = 2 * half
     tile = 64
     blocks = MAXLEN // QB
     items = GROUP * blocks
@@ -99,20 +100,20 @@
         return head, slice(block * QB, (block + 1) * QB), slice(head * HD, (head + 1) * HD)
 
     def buffers(item):
-        return scratch[item % 2 * 5 : item % 2 * 5 + 5]
+        return scratch[item % 2 * 3 : item % 2 * 3 + 3]
 
     def scores(item):
         _, rows, cols = place(item)
-        s_ref, dp_ref, _, _, top_ref = buffers(item)
+        s_ref, dp_ref, top_ref = buffers(item)
         q = q_ref[rows, cols]
         s = dot_nt(ks_ref[...], jnp.concatenate([q, q], axis=1))
         s_ref[...] = s
         top_ref[...] = jnp.max(s.reshape(tokens // 8, 8, QB), axis=0)
-        dp_ref[...] = dot_nt(kv_ref[:, HD:], g_ref[rows, cols])
+        dp_ref[...] = dot_nt(v_ref[...], g_ref[rows, cols])
 
     def softmax(item):
         head, rows, _ = place(item)
-        s_ref, dp_ref, p_ref, d_ref, top_ref = buffers(item)
+        s_ref, dp_ref, top_ref = buffers(item)
         own_top = max_ref[head, :, rows]
         top = jnp.maximum(jnp.max(top_ref[...], axis=0, keepdims=True), own_top)
         own = jnp.exp2(own_top - top)
@@ -120,55 +121,73 @@
         delta = jnp.zeros((8, QB), F32)
         for t in range(0, tokens, tile):
             e = jnp.exp2(s_ref[t : t + tile, :] - top)
-            s_ref[t : t + tile, :] = e
             total = total + jnp.sum(e.reshape(tile // 8, 8, QB), axis=0)
             ed = e * dp_ref[t : t + tile, :]
             delta = delta + jnp.sum(ed.reshape(tile // 8, 8, QB), axis=0)
         total = jnp.sum(total, axis=0, keepdims=True) + own * sum_ref[head, :, rows]
         delta = jnp.sum(delta, axis=0, keepdims=True) + own * del_ref[head, :, rows]
-        inverse = 1.0 / total
-        delta = delta * inverse
-        lse_ref[head, :, rows] = top + jnp.log2(total)
+        delta = delta * (1.0 / total)
+        lse = top + jnp.log2(total)
+        lse_ref[head, :, rows] = lse
         delta_ref[head, :, rows] = delta
         for t in range(0, tokens, tile):
-            p = s_ref[t : t + tile, :] * inverse
-            p_ref[t : t + tile, :] = p.astype(BF16)
-            d_ref[t : t + tile, :] = (p * (dp_ref[t : t + tile, :] - delta)).astype(BF16)
-
-    def grads(item):
-        head, rows, cols = place(item)
-        _, _, p_ref, d_ref, _ = buffers(item)
-        total_ref[:, HD:] += dot(p_ref[...], g_ref[rows, cols])
-        total_ref[:, 0:HD] += dot(d_ref[...], q_ref[rows, cols])
-        dq_ref[head, :, rows] = dot(kt_ref[...], d_ref[...])
-
-    keys = kv_ref[:, 0:HD]
-    kt_ref[...] = keys.T
-    scaled = keys.astype(F32) * C2
-    high = scaled.astype(BF16)
-    ks_ref[:, 0:HD] = high
-    ks_ref[:, HD:] = (scaled - high.astype(F32)).astype(BF16)
-    total_ref[...] = jnp.zeros_like(total_ref)
-
-    for step in range(-1, items + 1):
-        if step + 1 < items:
-            scores(step + 1)
-        if 0 <= step < items:
-            softmax(step)
-        if step >= 1:
-            grads(step - 1)
-
-    grad_ref[:, 0:HD] = (total_ref[:, 0:HD] * SCALE).astype(BF16)
-    grad_ref[:, HD:] = total_ref[:, HD:].astype(BF16)
-
-
-def own_grad_kernel(
-    q_ref, g_ref, k_ref, v_ref, lse_ref, delta_ref, past_ref, dq_ref, dk_ref, dv_ref
+            p = jnp.exp2(s_ref[t : t + tile, :] - lse)
+            prob_ref[head % 2, t : t + tile, rows] = p.astype(BF16)
+            ds = p * (dp_ref[t : t + tile, :] - delta)
+            d_ref[head, t : t + tile, rows] = ds.astype(BF16)
+
+    def save(head):
+        return pltpu.make_async_copy(d_ref.at[head], ds_ref.at[head], sems.at[head])
+
+    def grads(head):
+        cols = slice(head * HD, (head + 1) * HD)
+        dv = dot(prob_ref[head % 2], g_ref[:, cols])
+        dk = dot(d_ref[head], q_ref[:, cols])
+        if head:
+            dv = total_ref[:, HD:] + dv
+            dk = total_ref[:, 0:HD] + dk
+        if head < GROUP - 1:
+            total_ref[:, HD:] = dv
+            total_ref[:, 0:HD] = dk
+            return
+        for part, out in ((slice(0, half), keep_ref), (slice(half, tokens), send_ref)):
+            out[:, 0:HD] = (dk[part] * SCALE).astype(out.dtype)
+            out[:, HD:] = dv[part].astype(out.dtype)
+
+    for first, side_ref in ((0, mine_ref), (half, other_ref)):
+        part = slice(first, first + half)
+        v_ref[part, :] = side_ref[:, HD:]
+        scaled = side_ref[:, 0:HD].astype(F32) * C2
+        high = scaled.astype(BF16)
+        ks_ref[part, 0:HD] = high
+        ks_ref[part, HD:] = (scaled - high.astype(F32)).astype(BF16)
+
+    scores(0)
+    for item in range(items):
+        head, block = divmod(item, blocks)
+        if item + 1 < items:
+            scores(item + 1)
+        softmax(item)
+        if block == 0 and head:
+            grads(head - 1)
+        if block == blocks - 1:
+            save(head).start()
+    grads(GROUP - 1)
+    for head in range(GROUP):
+        save(head).wait()
+
+
+def grads_kernel(
+    q_ref, g_ref, k_ref, v_ref, lse_ref, delta_ref, mine_ref, other_ref, ds_ref,
+    dq_ref, dk_ref, dv_ref, kt_ref,
 ):
     head = pl.program_id(0)
+    half = mine_ref.shape[0]
 
     @pl.when(head == 0)
     def _():
+        kt_ref[:, 0:half] = mine_ref[:, 0:HD].T
+        kt_ref[:, half:] = other_ref[:, 0:HD].T
         dk_ref[...] = jnp.zeros_like(dk_ref)
         dv_ref[...] = jnp.zeros_like(dv_ref)
 
@@ -187,7 +206,7 @@
         ds = (p * (dot_nt(v_ref[0:hi, :], gb) - delta)).astype(BF16)
         dv_ref[0:hi, :] += dot(p.astype(BF16), gb)
         dk_ref[0:hi, :] += dot(ds, q)
-        part = past_ref[head, :, lo:hi] + dot(keys_t[:, 0:hi], ds)
+        part = dot(kt_ref[...], ds_ref[0, :, lo:hi]) + dot(keys_t[:, 0:hi], ds)
         dq_ref[lo:hi, :] = part.T * SCALE
 
     @pl.when(head == GROUP - 1)
@@ -221,6 +240,10 @@
     return pltpu.VMEM(shape, dtype)
 
 
+def hbm_struct(shape, dtype):
+    return pltpu.HBM(shape, dtype)
+
+
 def vmem(x):
     return pltpu.with_memory_space_constraint(x, pltpu.VMEM)
 
@@ -235,18 +258,23 @@
 
 def per_device(queries, comp_keys, comp_values, out_grad, prompt_keys, prompt_values, lengths):
     devices = lax.axis_size("comp")
-    tokens = devices * SHARD
+    half = devices * SHARD // 2
+    tokens = 2 * half
     width = GROUP * HD
 
+    chips = devices // 2
+    swap = [(d, d ^ 1) for d in range(devices)]
+    same_core = [[2 * chip + core for chip in range(chips)] for core in range(2)]
     spread = pl.pallas_call(
         spread_kernel,
         in_specs=[pl.BlockSpec(memory_space=pltpu.HBM)] * 2,
         out_specs=VMEM,
-        out_shape=struct((devices, SHARD, 2 * HD), BF16),
+        out_shape=struct((chips, SHARD, 2 * HD), BF16),
         scratch_shapes=[pltpu.VMEM((2, SHARD, HD), BF16), pltpu.SemaphoreType.DMA((2,))],
         name="spread",
     )(prompt_keys, prompt_values)
-    prompt = lax.all_to_all(spread, "comp", 0, 0, tiled=True)
+    mine = lax.all_to_all(spread, "comp", 0, 0, axis_index_groups=same_core, tiled=True)
+    mine = mine.reshape(half, 2 * HD)
 
     stat = struct((GROUP, 1, MAXLEN), F32)
     copied, masked, own_max, own_sum, own_del = pl.pallas_call(
@@ -263,53 +291,59 @@
         name="own_stats",
     )(lengths, hbm(queries), hbm(out_grad), hbm(comp_keys), hbm(comp_values))
 
-    prompt, masked = lax.optimization_barrier((prompt, masked))
-
-    past, grad_part, lse, delta = pl.pallas_call(
+    mine, masked = lax.optimization_barrier((mine, masked))
+    other = lax.ppermute(mine, "comp", swap)
+
+    dscore, grad_keep, grad_send, lse, delta = pl.pallas_call(
         prompt_kernel,
-        in_specs=[VMEM] * 6,
-        out_specs=[VMEM] * 4,
+        in_specs=[VMEM] * 7,
+        out_specs=[pl.BlockSpec(memory_space=pltpu.HBM)] + [VMEM] * 4,
         out_shape=[
-            struct((GROUP, HD, MAXLEN), F32), struct((tokens, 2 * HD), BF16), stat, stat,
+            hbm_struct((GROUP, tokens, MAXLEN), BF16),
+            struct((half, 2 * HD), F32), struct((half, 2 * HD), BF16), stat, stat,
         ],
         scratch_shapes=[
             pltpu.VMEM((tokens, 2 * HD), F32),
-            pltpu.VMEM((HD, tokens), BF16),
             pltpu.VMEM((tokens, 2 * HD), BF16),
+            pltpu.VMEM((tokens, HD), BF16),
+            pltpu.VMEM((GROUP, tokens, MAXLEN), BF16),
+            pltpu.VMEM((2, tokens, MAXLEN), BF16),
+            pltpu.SemaphoreType.DMA((GROUP,)),
         ]
         + [
             pltpu.VMEM((tokens, QB), F32),
             pltpu.VMEM((tokens, QB), F32),
-            pltpu.VMEM((tokens, QB), BF16),
-            pltpu.VMEM((tokens, QB), BF16),
             pltpu.VMEM((8, QB), F32),
         ]
         * 2,
         compiler_params=pltpu.CompilerParams(vmem_limit_bytes=VMEM_LIMIT),
-        cost_estimate=cost(GROUP * 10 * 1024 * 512 * HD, GROUP * 1024 * 512, 2**22),
+        cost_estimate=cost(GROUP * 8 * 1024 * 512 * HD, GROUP * 2048 * 512, 2**23),
         name="prompt",
-    )(
-        vmem(copied), vmem(masked), prompt.reshape(tokens, 2 * HD), own_max, own_sum, own_del,
-    )
-
-    parts = grad_part.reshape(devices, SHARD, 2 * HD)
-    arrived = lax.all_to_all(parts, "comp", 0, 0, tiled=True)
+    )(vmem(copied), vmem(masked), mine, other, own_max, own_sum, own_del)
+
+    received = lax.ppermute(grad_send, "comp", swap)
+    total = (grad_keep + received.astype(F32)).astype(BF16).reshape(chips, SHARD, 2 * HD)
+    arrived = lax.all_to_all(total, "comp", 0, 0, axis_index_groups=same_core, tiled=True)
     grad_prompt = jnp.sum(arrived.astype(F32), axis=0)
 
     grad_queries, grad_comp_keys, grad_comp_values = pl.pallas_call(
-        own_grad_kernel,
+        grads_kernel,
         grid=(GROUP,),
-        in_specs=[VMEM, VMEM, whole((MAXLEN, HD)), whole((MAXLEN, HD)), VMEM, VMEM, VMEM],
+        in_specs=[VMEM, VMEM, whole((MAXLEN, HD)), whole((MAXLEN, HD))]
+        + [VMEM] * 4
+        + [pl.BlockSpec((1, tokens, MAXLEN), lambda h: (h, 0, 0))],
         out_specs=[HEAD, whole((MAXLEN, HD)), whole((MAXLEN, HD))],
         out_shape=[
             struct((MAXLEN, width), F32),
             struct((MAXLEN, HD), F32), struct((MAXLEN, HD), F32),
         ],
+        scratch_shapes=[pltpu.VMEM((HD, tokens), BF16)],
         compiler_params=params(),
-        cost_estimate=cost(GROUP * 10 * 384 * 512 * HD, GROUP * 384 * 512, 2**22),
-        name="own_grad",
+        cost_estimate=cost(GROUP * 4 * 1024 * 512 * HD, GROUP * 384 * 512, 2**23),
+        name="grads",
     )(
-        vmem(copied), vmem(masked), hbm(comp_keys), hbm(comp_values), lse, delta, past,
+        vmem(copied), vmem(masked), hbm(comp_keys), hbm(comp_values), lse, delta,
+        mine, other, hbm(dscore),
     )
 
     return (

time: 62.4 us -> 58.7 us (0.941)
  waiting for transfers between devices: 24.6 us -> 14.6 us
  starting transfers between devices: 13.2 us -> 16.5 us
  Pallas kernels: 21.9 us -> 24.2 us
  other arithmetic: 0.08 us -> 0.8 us
    all_to_all x2, waiting for transfers between devices: 24.6 us -> 11.8 us  [the longest x1 6.83 us: per_device(): lax.all_to_all(spread, 'comp', 0, 0, axis_index_groups=same_core, tiled=T...]
    ppermute x0 -> x2, starting transfers between devices: none -> 3.96 us  [the longest x1 2.05 us: per_device(): received = lax.ppermute(grad_send, 'comp', swap)]
    ppermute x0 -> x2, waiting for transfers between devices: none -> 2.87 us  [the longest x1 1.5 us: per_device(): other = lax.ppermute(mine, 'comp', swap)]
    pallas_call x2, Pallas kernels: 15.7 us -> 18.2 us  [the longest x1 10.1 us: per_device(): pl.pallas_call(prompt_kernel, in_specs=[VMEM] * 7, out_specs=[pl.BlockSpe...]
    convert_element_type x0 -> x1, other arithmetic: none -> 0.76 us  [per_device(): (grad_keep + received.astype(F32)).astype(BF16)]
    all_to_all x2, starting transfers between devices: 13.2 us -> 12.6 us  [the longest x1 9.03 us: per_device(): lax.all_to_all(spread, 'comp', 0, 0, axis_index_groups=same_core, tiled=T...]
  transfers between devices with their start and end apart: 2 -> 4, of which waited for: 2 -> 4; matrix products, arithmetic and copies ran while one was open for 0% -> 0% of each run, Pallas kernels for 17% -> 22%
where the time goes in v5:
time: 58.7 us; the launch traced here: 58.1 us
  Pallas kernels  24.2 us (41%)
  starting transfers between devices  16.5 us (28%)
  waiting for transfers between devices  14.6 us (25%)
  between operations  1.34 us (2%)
  other arithmetic  0.8 us (1%)
  local copies, waits for them, and re-layouts  0.61 us (1%)
    pallas_call x1, Pallas kernels, per_device(): pl.pallas_call(prompt_kernel, in_specs=[VMEM] * 7, out_specs=[pl.BlockSpe...  10.1 us
    all_to_all x1, starting transfers between devices, per_device(): lax.all_to_all(spread, 'comp', 0, 0, axis_index_groups=same_core, tiled=T...  9.03 us
    pallas_call x1, Pallas kernels, per_device(): pl.pallas_call(grads_kernel, grid=(GROUP,), in_specs=[VMEM, VMEM, whole((...  8.09 us
    all_to_all x1, waiting for transfers between devices, per_device(): lax.all_to_all(spread, 'comp', 0, 0, axis_index_groups=same_core, tiled=T...  6.83 us
    all_to_all x1, waiting for transfers between devices, per_device(): lax.all_to_all(total, 'comp', 0, 0, axis_index_groups=same_core, tiled=True)  4.92 us
    pallas_call x1, Pallas kernels, per_device(): pl.pallas_call(own_stats_kernel, grid=(GROUP,), in_specs=[SMEM, HEAD, HEA...  4.55 us
    all_to_all x1, starting transfers between devices, per_device(): lax.all_to_all(total, 'comp', 0, 0, axis_index_groups=same_core, tiled=True)  3.53 us
    ppermute x1, starting transfers between devices, per_device(): received = lax.ppermute(grad_send, 'comp', swap)  2.05 us
  transfers between devices with their start and end apart: 4, of which 4 were waited for; matrix products, arithmetic and copies ran while one was open for 0% of the time, Pallas kernels for 22%

profile of v5, /device:TPU:6, one launch (start us, length us, event | category | flops | bytes accessed | tf_op | source)
XLA Modules:
  0.0 58.1 jit_solution(12487865175091336775)
XLA Ops:
  0.6 1.5 %spread.1 = bf16[16,32,256]{2,1,0:T(8,128)(2,1)} custom-call(bf16[32,128]{1,0:T(8,128)(2,1)} %k_ref.4, bf16[32,128]{1,0:T(8,128)(2,1)} %v_ref.4), custom_call_target="tpu_custom_call" | custom-call | tf_op jit(solution)/shard_map/spread/pallas_call | solution.py:268
  2.1 9.0 %all-to-all-start = ((bf16[16,32,256]{2,1,0:T(8,128)(2,1)}), bf16[16,32,256]{2,1,0:T(8,128)(2,1)S(1)}, u32[]{:S(2)}, u32[]{:S(2)}) async-start(bf16[16,32,256]{2,1,0:T(8,128)(2,1)} %spread.1), calls=%async_computation | async-start | bytes 524288 | tf_op jit(solution)/shard_map/all_to_all | solution.py:276
  11.8 4.5 %own_stats.1 = (bf16[512,640]{1,0:T(8,128)(2,1)S(1)}, bf16[512,640]{1,0:T(8,128)(2,1)S(1)}, f32[5,1,512]{2,1,0:T(1,128)S(1)}, f32[5,1,512]{2,1,0:T(1,128)S(1)}, f32[5,1,512]{2,1,0:T(1,128)S(1)}) custom-call(s32[1]{0:T(128)S(6)} %copy.12.len_ref, bf16[512,640]{1,0:T(8,128)(2,1)} %q_ref.1, bf16[512,640]{1,0:T(8,128)(2,1)} %g_ref.1, bf16[512,128]{1,0:T(8,128)(2,1)} %k_ref.5, ...), custom_call_target="tpu_custom_call" | custom-call | flops 503316480 | bytes 2097152 | tf_op jit(solution)/shard_map/own_stats/pallas_call | solution.py:280
  16.3 6.8 %all-to-all-done = bf16[16,32,256]{2,1,0:T(8,128)(2,1)S(1)} async-done(((bf16[16,32,256]{2,1,0:T(8,128)(2,1)}), bf16[16,32,256]{2,1,0:T(8,128)(2,1)S(1)}, u32[]{:S(2)}, u32[]{:S(2)}) %all-to-all-start) | async-done | bytes 262176 | tf_op jit(solution)/shard_map/all_to_all | solution.py:276
  23.2 1.9 %collective-permute-start = (bf16[512,256]{1,0:T(8,128)(2,1)S(1)}, bf16[512,256]{1,0:T(8,128)(2,1)S(1)}, u32[]{:S(2)}, u32[]{:S(2)}) collective-permute-start(bf16[512,256]{1,0:T(8,128)(2,1)S(1)} %bitcast.2), channel_id=1, source_target_pairs={{0,4},{4,0},{8,12},{12,8},{16,20},{20,16},{24,28},{28,24},{32,36},... | collective-permute-start | bytes 786440 | tf_op jit(solution)/shard_map/ppermute | solution.py:295
  25.1 1.5 %collective-permute-done.other_ref = bf16[512,256]{1,0:T(8,128)(2,1)S(1)} collective-permute-done((bf16[512,256]{1,0:T(8,128)(2,1)S(1)}, bf16[512,256]{1,0:T(8,128)(2,1)S(1)}, u32[]{:S(2)}, u32[]{:S(2)}) %collective-permute-start) | collective-permute-done | bytes 262176 | tf_op jit(solution)/shard_map/ppermute | solution.py:295
  26.6 10.1 %prompt.1 = (bf16[5,1024,512]{2,1,0:T(8,128)(2,1)}, f32[512,256]{1,0:T(8,128)S(1)}, bf16[512,256]{1,0:T(8,128)(2,1)S(1)}, f32[5,1,512]{2,1,0:T(1,128)S(1)}, f32[5,1,512]{2,1,0:T(1,128)S(1)}) custom-call(bf16[512,640]{1,0:T(8,128)(2,1)S(1)} %get-tuple-element.20.q_ref, bf16[512,640]{1,0:T(8,128)(2,1)S(1)} %get-tuple-element.22.g_ref, ...), custom_call_target="tpu_custom_call" | custom-call | flops 2684354560 | bytes 8388608 | tf_op jit(solution)/shard_map/prompt/pallas_call | solution.py:297
  36.7 2.0 %collective-permute-start.1 = (bf16[512,256]{1,0:T(8,128)(2,1)S(1)}, bf16[512,256]{1,0:T(8,128)(2,1)S(1)}, u32[]{:S(2)}, u32[]{:S(2)}) collective-permute-start(bf16[512,256]{1,0:T(8,128)(2,1)S(1)} %get-tuple-element.32), channel_id=1, source_target_pairs={{0,4},{4,0},{8,12},{12,8},{16,20},{20,16},{24,28},{28,24},{32,36},... | collective-permute-start | bytes 786440 | tf_op jit(solution)/shard_map/ppermute | solution.py:324
  38.7 1.4 %collective-permute-done.1 = bf16[512,256]{1,0:T(8,128)(2,1)S(1)} collective-permute-done((bf16[512,256]{1,0:T(8,128)(2,1)S(1)}, bf16[512,256]{1,0:T(8,128)(2,1)S(1)}, u32[]{:S(2)}, u32[]{:S(2)}) %collective-permute-start.1) | collective-permute-done | bytes 262176 | tf_op jit(solution)/shard_map/ppermute | solution.py:324
  40.1 0.8 %add_convert_fusion = bf16[512,256]{1,0:T(8,128)(2,1)} fusion(f32[512,256]{1,0:T(8,128)S(1)} %get-tuple-element.31, bf16[512,256]{1,0:T(8,128)(2,1)S(1)} %collective-permute-done.1), kind=kLoop, calls=%fused_computation.1 | loop fusion | flops 393216 | bytes 1048576 | tf_op jit(solution)/shard_map/convert_element_type | solution.py:325
  40.9 3.5 %all-to-all-start.1 = ((bf16[16,32,256]{2,1,0:T(8,128)(2,1)}), bf16[16,32,256]{2,1,0:T(8,128)(2,1)S(1)}, u32[]{:S(2)}, u32[]{:S(2)}) async-start(bf16[16,32,256]{2,1,0:T(8,128)(2,1)} %bitcast.1), calls=%async_computation.1 | async-start | bytes 524288 | tf_op jit(solution)/shard_map/all_to_all | solution.py:326
  44.4 8.1 %grads.1 = (f32[512,640]{1,0:T(8,128)}, f32[512,128]{1,0:T(8,128)}, f32[512,128]{1,0:T(8,128)}) custom-call(bf16[512,640]{1,0:T(8,128)(2,1)S(1)} %get-tuple-element.20.q_ref, bf16[512,640]{1,0:T(8,128)(2,1)S(1)} %get-tuple-element.22.g_ref, bf16[512,128]{1,0:T(8,128)(2,1)} %k_ref.5, bf16[512,128]{1,0:T(8,128)(2,1)} %v_ref.5, ...), custom_call_target="tpu_custom_call" | custom-call | flops 1342177280 | bytes 8388608 | tf_op jit(solution)/shard_map/grads/pallas_call | solution.py:329
  52.5 4.9 %all-to-all-done.1 = bf16[16,32,256]{2,1,0:T(8,128)(2,1)S(1)} async-done(((bf16[16,32,256]{2,1,0:T(8,128)(2,1)}), bf16[16,32,256]{2,1,0:T(8,128)(2,1)S(1)}, u32[]{:S(2)}, u32[]{:S(2)}) %all-to-all-start.1) | async-done | bytes 262176 | tf_op jit(solution)/shard_map/all_to_all | solution.py:326
  57.5 0.6 %fusion = (f32[32,128]{1,0:T(8,128)}, f32[32,128]{1,0:T(8,128)}) fusion(f32[32,256]{1,0:T(8,128)S(1)} %convert_reduce_fusion), kind=kLoop, calls=%fused_computation.2 | loop fusion | bytes 65536 | tf_op jit(solution)/shard_map/slice | solution.py:352
  (1 shorter events, 0.0 us)
Async XLA Ops:
  2.1 21.1 %all-to-all-start = ((bf16[16,32,256]{2,1,0:T(8,128)(2,1)}), bf16[16,32,256]{2,1,0:T(8,128)(2,1)S(1)}, u32[]{:S(2)}, u32[]{:S(2)}) async-start(bf16[16,32,256]{2,1,0:T(8,128)(2,1)} %spread.1), calls=%async_computation | async-start | bytes 524288 | tf_op jit(solution)/shard_map/all_to_all | solution.py:276
  23.2 3.4 %collective-permute-start = (bf16[512,256]{1,0:T(8,128)(2,1)S(1)}, bf16[512,256]{1,0:T(8,128)(2,1)S(1)}, u32[]{:S(2)}, u32[]{:S(2)}) collective-permute-start(bf16[512,256]{1,0:T(8,128)(2,1)S(1)} %bitcast.2), channel_id=1, source_target_pairs={{0,4},{4,0},{8,12},{12,8},{16,20},{20,16},{24,28},{28,24},{32,36},... | collective-permute-start | bytes 786440 | tf_op jit(solution)/shard_map/ppermute | solution.py:295
  36.7 3.4 %collective-permute-start.1 = (bf16[512,256]{1,0:T(8,128)(2,1)S(1)}, bf16[512,256]{1,0:T(8,128)(2,1)S(1)}, u32[]{:S(2)}, u32[]{:S(2)}) collective-permute-start(bf16[512,256]{1,0:T(8,128)(2,1)S(1)} %get-tuple-element.32), channel_id=1, source_target_pairs={{0,4},{4,0},{8,12},{12,8},{16,20},{20,16},{24,28},{28,24},{32,36},... | collective-permute-start | bytes 786440 | tf_op jit(solution)/shard_map/ppermute | solution.py:324
  40.9 16.6 %all-to-all-start.1 = ((bf16[16,32,256]{2,1,0:T(8,128)(2,1)}), bf16[16,32,256]{2,1,0:T(8,128)(2,1)S(1)}, u32[]{:S(2)}, u32[]{:S(2)}) async-start(bf16[16,32,256]{2,1,0:T(8,128)(2,1)} %bitcast.1), calls=%async_computation.1 | async-start | bytes 524288 | tf_op jit(solution)/shard_map/all_to_all | solution.py:326

commit v6 on v5

--- a/solution.py
+++ b/solution.py
@@ -92,6 +92,7 @@
     half = mine_ref.shape[0]
     tokens = 2 * half
     tile = 64
+    chunk = tokens // 4
     blocks = MAXLEN // QB
     items = GROUP * blocks
 
@@ -102,77 +103,105 @@
     def buffers(item):
         return scratch[item % 2 * 3 : item % 2 * 3 + 3]
 
-    def scores(item):
-        _, rows, cols = place(item)
-        s_ref, dp_ref, top_ref = buffers(item)
-        q = q_ref[rows, cols]
-        s = dot_nt(ks_ref[...], jnp.concatenate([q, q], axis=1))
-        s_ref[...] = s
-        top_ref[...] = jnp.max(s.reshape(tokens // 8, 8, QB), axis=0)
-        dp_ref[...] = dot_nt(v_ref[...], g_ref[rows, cols])
-
-    def softmax(item):
-        head, rows, _ = place(item)
-        s_ref, dp_ref, top_ref = buffers(item)
-        own_top = max_ref[head, :, rows]
-        top = jnp.maximum(jnp.max(top_ref[...], axis=0, keepdims=True), own_top)
-        own = jnp.exp2(own_top - top)
-        total = jnp.zeros((8, QB), F32)
-        delta = jnp.zeros((8, QB), F32)
-        for t in range(0, tokens, tile):
-            e = jnp.exp2(s_ref[t : t + tile, :] - top)
-            total = total + jnp.sum(e.reshape(tile // 8, 8, QB), axis=0)
-            ed = e * dp_ref[t : t + tile, :]
-            delta = delta + jnp.sum(ed.reshape(tile // 8, 8, QB), axis=0)
-        total = jnp.sum(total, axis=0, keepdims=True) + own * sum_ref[head, :, rows]
-        delta = jnp.sum(delta, axis=0, keepdims=True) + own * del_ref[head, :, rows]
-        delta = delta * (1.0 / total)
-        lse = top + jnp.log2(total)
-        lse_ref[head, :, rows] = lse
-        delta_ref[head, :, rows] = delta
-        for t in range(0, tokens, tile):
-            p = jnp.exp2(s_ref[t : t + tile, :] - lse)
-            prob_ref[head % 2, t : t + tile, rows] = p.astype(BF16)
-            ds = p * (dp_ref[t : t + tile, :] - delta)
-            d_ref[head, t : t + tile, rows] = ds.astype(BF16)
+    def part(c):
+        return slice(c * chunk, (c + 1) * chunk)
+
+    def fold(x):
+        return x.reshape(x.shape[0] // 8, 8, QB)
+
+    def grad_product(head, c):
+        cols = slice(head * HD, (head + 1) * HD)
+        if c % 2:
+            return dot(prob_ref[head % 2, part(c // 2), :], g_ref[:, cols])
+        return dot(d_ref[head, part(c // 2), :], q_ref[:, cols])
+
+    def grad_add(head, c, product):
+        lane = slice(HD, 2 * HD) if c % 2 else slice(0, HD)
+        if head:
+            product = total_ref[part(c // 2), lane] + product
+        if head < GROUP - 1:
+            total_ref[part(c // 2), lane] = product
+            return
+        if c % 2 == 0:
+            product = product * SCALE
+        out = keep_ref if c < 4 else send_ref
+        row = c % 4 // 2 * chunk
+        out[row : row + chunk, lane] = product.astype(out.dtype)
 
     def save(head):
         return pltpu.make_async_copy(d_ref.at[head], ds_ref.at[head], sems.at[head])
 
-    def grads(head):
-        cols = slice(head * HD, (head + 1) * HD)
-        dv = dot(prob_ref[head % 2], g_ref[:, cols])
-        dk = dot(d_ref[head], q_ref[:, cols])
-        if head:
-            dv = total_ref[:, HD:] + dv
-            dk = total_ref[:, 0:HD] + dk
-        if head < GROUP - 1:
-            total_ref[:, HD:] = dv
-            total_ref[:, 0:HD] = dk
-            return
-        for part, out in ((slice(0, half), keep_ref), (slice(half, tokens), send_ref)):
-            out[:, 0:HD] = (dk[part] * SCALE).astype(out.dtype)
-            out[:, HD:] = dv[part].astype(out.dtype)
+    def step(item):
+        cur = 0 <= item
+        ahead = item + 1 < items
+        if ahead:
+            _, rows_n, cols_n = place(item + 1)
+            s_next, dp_next, top_next = buffers(item + 1)
+            q = q_ref[rows_n, cols_n]
+            q = jnp.concatenate([q, q], axis=1)
+            g = g_ref[rows_n, cols_n]
+            tops = None
+        if cur:
+            head, rows, _ = place(item)
+            block = item % blocks
+            s_ref, dp_ref, top_ref = buffers(item)
+            own_top = max_ref[head, :, rows]
+            top = jnp.maximum(jnp.max(top_ref[...], axis=0, keepdims=True), own_top)
+            own = jnp.exp2(own_top - top)
+            total = jnp.zeros((8, QB), F32)
+            delta = jnp.zeros((8, QB), F32)
+        for c in range(4):
+            if ahead:
+                s = dot_nt(ks_ref[part(c), :], q)
+            if cur:
+                for t in range(c * chunk, (c + 1) * chunk, tile):
+                    e = jnp.exp2(s_ref[t : t + tile, :] - top)
+                    s_ref[t : t + tile, :] = e
+                    total = total + jnp.sum(fold(e), axis=0)
+                    delta = delta + jnp.sum(fold(e * dp_ref[t : t + tile, :]), axis=0)
+            if ahead:
+                s_next[part(c), :] = s
+                high = jnp.max(fold(s), axis=0)
+                tops = high if tops is None else jnp.maximum(tops, high)
+        if ahead:
+            top_next[...] = tops
+        if cur:
+            total = jnp.sum(total, axis=0, keepdims=True) + own * sum_ref[head, :, rows]
+            delta = jnp.sum(delta, axis=0, keepdims=True) + own * del_ref[head, :, rows]
+            inverse = 1.0 / total
+            delta = delta * inverse
+            lse_ref[head, :, rows] = top + jnp.log2(total)
+            delta_ref[head, :, rows] = delta
+        for c in range(4):
+            if ahead:
+                dp = dot_nt(v_ref[part(c), :], g)
+            if cur and head:
+                product = grad_product(head - 1, 4 * block + c)
+            if cur:
+                for t in range(c * chunk, (c + 1) * chunk, tile):
+                    p = s_ref[t : t + tile, :] * inverse
+                    prob_ref[head % 2, t : t + tile, rows] = p.astype(BF16)
+                    ds = p * (dp_ref[t : t + tile, :] - delta)
+                    d_ref[head, t : t + tile, rows] = ds.astype(BF16)
+            if ahead:
+                dp_next[part(c), :] = dp
+            if cur and head:
+                grad_add(head - 1, 4 * block + c, product)
 
     for first, side_ref in ((0, mine_ref), (half, other_ref)):
-        part = slice(first, first + half)
-        v_ref[part, :] = side_ref[:, HD:]
+        side = slice(first, first + half)
+        v_ref[side, :] = side_ref[:, HD:]
         scaled = side_ref[:, 0:HD].astype(F32) * C2
         high = scaled.astype(BF16)
-        ks_ref[part, 0:HD] = high
-        ks_ref[part, HD:] = (scaled - high.astype(F32)).astype(BF16)
-
-    scores(0)
-    for item in range(items):
-        head, block = divmod(item, blocks)
-        if item + 1 < items:
-            scores(item + 1)
-        softmax(item)
-        if block == 0 and head:
-            grads(head - 1)
-        if block == blocks - 1:
-            save(head).start()
-    grads(GROUP - 1)
+        ks_ref[side, 0:HD] = high
+        ks_ref[side, HD:] = (scaled - high.astype(F32)).astype(BF16)
+
+    for item in range(-1, items):
+        step(item)
+        if item % blocks == blocks - 1 and item >= 0:
+            save(item // blocks).start()
+    for c in range(8):
+        grad_add(GROUP - 1, c, grad_product(GROUP - 1, c))
     for head in range(GROUP):
         save(head).wait()
 

time: 58.7 us -> 57.8 us (0.985)
  Pallas kernels: 24.2 us -> 23.3 us
    pallas_call x1, Pallas kernels: 10.1 us -> 9.23 us  [per_device(): pl.pallas_call(prompt_kernel, in_specs=[VMEM] * 7, out_specs=[pl.BlockSpe...]
where the time goes in v6:
time: 57.8 us; the launch traced here: 57.2 us
  Pallas kernels  23.3 us (40%)
  starting transfers between devices  16.5 us (29%)
  waiting for transfers between devices  14.6 us (25%)
  between operations  1.34 us (2%)
  other arithmetic  0.8 us (1%)
  local copies, waits for them, and re-layouts  0.61 us (1%)
    pallas_call x1, Pallas kernels, per_device(): pl.pallas_call(prompt_kernel, in_specs=[VMEM] * 7, out_specs=[pl.BlockSpe...  9.23 us
    all_to_all x1, starting transfers between devices, per_device(): lax.all_to_all(spread, 'comp', 0, 0, axis_index_groups=same_core, tiled=T...  9.03 us
    pallas_call x1, Pallas kernels, per_device(): pl.pallas_call(grads_kernel, grid=(GROUP,), in_specs=[VMEM, VMEM, whole((...  8.1 us
    all_to_all x1, waiting for transfers between devices, per_device(): lax.all_to_all(spread, 'comp', 0, 0, axis_index_groups=same_core, tiled=T...  6.83 us
    all_to_all x1, waiting for transfers between devices, per_device(): lax.all_to_all(total, 'comp', 0, 0, axis_index_groups=same_core, tiled=True)  4.92 us
    pallas_call x1, Pallas kernels, per_device(): pl.pallas_call(own_stats_kernel, grid=(GROUP,), in_specs=[SMEM, HEAD, HEA...  4.55 us
    all_to_all x1, starting transfers between devices, per_device(): lax.all_to_all(total, 'comp', 0, 0, axis_index_groups=same_core, tiled=True)  3.53 us
    ppermute x1, starting transfers between devices, per_device(): received = lax.ppermute(grad_send, 'comp', swap)  2.05 us
  transfers between devices with their start and end apart: 4, of which 4 were waited for; matrix products, arithmetic and copies ran while one was open for 0% of the time, Pallas kernels for 22%

profile of v6, /device:TPU:6, one launch (start us, length us, event | category | flops | bytes accessed | tf_op | source)
XLA Modules:
  0.0 57.2 jit_solution(10573023179067324327)
XLA Ops:
  0.6 1.5 %spread.1 = bf16[16,32,256]{2,1,0:T(8,128)(2,1)} custom-call(bf16[32,128]{1,0:T(8,128)(2,1)} %k_ref.4, bf16[32,128]{1,0:T(8,128)(2,1)} %v_ref.4), custom_call_target="tpu_custom_call" | custom-call | tf_op jit(solution)/shard_map/spread/pallas_call | solution.py:297
  2.1 9.0 %all-to-all-start = ((bf16[16,32,256]{2,1,0:T(8,128)(2,1)}), bf16[16,32,256]{2,1,0:T(8,128)(2,1)S(1)}, u32[]{:S(2)}, u32[]{:S(2)}) async-start(bf16[16,32,256]{2,1,0:T(8,128)(2,1)} %spread.1), calls=%async_computation | async-start | bytes 524288 | tf_op jit(solution)/shard_map/all_to_all | solution.py:305
  11.8 4.5 %own_stats.1 = (bf16[512,640]{1,0:T(8,128)(2,1)S(1)}, bf16[512,640]{1,0:T(8,128)(2,1)S(1)}, f32[5,1,512]{2,1,0:T(1,128)S(1)}, f32[5,1,512]{2,1,0:T(1,128)S(1)}, f32[5,1,512]{2,1,0:T(1,128)S(1)}) custom-call(s32[1]{0:T(128)S(6)} %copy.12.len_ref, bf16[512,640]{1,0:T(8,128)(2,1)} %q_ref.1, bf16[512,640]{1,0:T(8,128)(2,1)} %g_ref.1, bf16[512,128]{1,0:T(8,128)(2,1)} %k_ref.5, ...), custom_call_target="tpu_custom_call" | custom-call | flops 503316480 | bytes 2097152 | tf_op jit(solution)/shard_map/own_stats/pallas_call | solution.py:309
  16.3 6.8 %all-to-all-done = bf16[16,32,256]{2,1,0:T(8,128)(2,1)S(1)} async-done(((bf16[16,32,256]{2,1,0:T(8,128)(2,1)}), bf16[16,32,256]{2,1,0:T(8,128)(2,1)S(1)}, u32[]{:S(2)}, u32[]{:S(2)}) %all-to-all-start) | async-done | bytes 262176 | tf_op jit(solution)/shard_map/all_to_all | solution.py:305
  23.2 1.9 %collective-permute-start = (bf16[512,256]{1,0:T(8,128)(2,1)S(1)}, bf16[512,256]{1,0:T(8,128)(2,1)S(1)}, u32[]{:S(2)}, u32[]{:S(2)}) collective-permute-start(bf16[512,256]{1,0:T(8,128)(2,1)S(1)} %bitcast.2), channel_id=1, source_target_pairs={{0,4},{4,0},{8,12},{12,8},{16,20},{20,16},{24,28},{28,24},{32,36},... | collective-permute-start | bytes 786440 | tf_op jit(solution)/shard_map/ppermute | solution.py:324
  25.1 1.5 %collective-permute-done.other_ref = bf16[512,256]{1,0:T(8,128)(2,1)S(1)} collective-permute-done((bf16[512,256]{1,0:T(8,128)(2,1)S(1)}, bf16[512,256]{1,0:T(8,128)(2,1)S(1)}, u32[]{:S(2)}, u32[]{:S(2)}) %collective-permute-start) | collective-permute-done | bytes 262176 | tf_op jit(solution)/shard_map/ppermute | solution.py:324
  26.6 9.2 %prompt.1 = (bf16[5,1024,512]{2,1,0:T(8,128)(2,1)}, f32[512,256]{1,0:T(8,128)S(1)}, bf16[512,256]{1,0:T(8,128)(2,1)S(1)}, f32[5,1,512]{2,1,0:T(1,128)S(1)}, f32[5,1,512]{2,1,0:T(1,128)S(1)}) custom-call(bf16[512,640]{1,0:T(8,128)(2,1)S(1)} %get-tuple-element.20.q_ref, bf16[512,640]{1,0:T(8,128)(2,1)S(1)} %get-tuple-element.22.g_ref, ...), custom_call_target="tpu_custom_call" | custom-call | flops 2684354560 | bytes 8388608 | tf_op jit(solution)/shard_map/prompt/pallas_call | solution.py:326
  35.8 2.0 %collective-permute-start.1 = (bf16[512,256]{1,0:T(8,128)(2,1)S(1)}, bf16[512,256]{1,0:T(8,128)(2,1)S(1)}, u32[]{:S(2)}, u32[]{:S(2)}) collective-permute-start(bf16[512,256]{1,0:T(8,128)(2,1)S(1)} %get-tuple-element.32), channel_id=1, source_target_pairs={{0,4},{4,0},{8,12},{12,8},{16,20},{20,16},{24,28},{28,24},{32,36},... | collective-permute-start | bytes 786440 | tf_op jit(solution)/shard_map/ppermute | solution.py:353
  37.9 1.4 %collective-permute-done.1 = bf16[512,256]{1,0:T(8,128)(2,1)S(1)} collective-permute-done((bf16[512,256]{1,0:T(8,128)(2,1)S(1)}, bf16[512,256]{1,0:T(8,128)(2,1)S(1)}, u32[]{:S(2)}, u32[]{:S(2)}) %collective-permute-start.1) | collective-permute-done | bytes 262176 | tf_op jit(solution)/shard_map/ppermute | solution.py:353
  39.3 0.8 %add_convert_fusion = bf16[512,256]{1,0:T(8,128)(2,1)} fusion(f32[512,256]{1,0:T(8,128)S(1)} %get-tuple-element.31, bf16[512,256]{1,0:T(8,128)(2,1)S(1)} %collective-permute-done.1), kind=kLoop, calls=%fused_computation.1 | loop fusion | flops 393216 | bytes 1048576 | tf_op jit(solution)/shard_map/convert_element_type | solution.py:354
  40.0 3.5 %all-to-all-start.1 = ((bf16[16,32,256]{2,1,0:T(8,128)(2,1)}), bf16[16,32,256]{2,1,0:T(8,128)(2,1)S(1)}, u32[]{:S(2)}, u32[]{:S(2)}) async-start(bf16[16,32,256]{2,1,0:T(8,128)(2,1)} %bitcast.1), calls=%async_computation.1 | async-start | bytes 524288 | tf_op jit(solution)/shard_map/all_to_all | solution.py:355
  43.6 8.1 %grads.1 = (f32[512,640]{1,0:T(8,128)}, f32[512,128]{1,0:T(8,128)}, f32[512,128]{1,0:T(8,128)}) custom-call(bf16[512,640]{1,0:T(8,128)(2,1)S(1)} %get-tuple-element.20.q_ref, bf16[512,640]{1,0:T(8,128)(2,1)S(1)} %get-tuple-element.22.g_ref, bf16[512,128]{1,0:T(8,128)(2,1)} %k_ref.5, bf16[512,128]{1,0:T(8,128)(2,1)} %v_ref.5, ...), custom_call_target="tpu_custom_call" | custom-call | flops 1342177280 | bytes 8388608 | tf_op jit(solution)/shard_map/grads/pallas_call | solution.py:358
  51.7 4.9 %all-to-all-done.1 = bf16[16,32,256]{2,1,0:T(8,128)(2,1)S(1)} async-done(((bf16[16,32,256]{2,1,0:T(8,128)(2,1)}), bf16[16,32,256]{2,1,0:T(8,128)(2,1)S(1)}, u32[]{:S(2)}, u32[]{:S(2)}) %all-to-all-start.1) | async-done | bytes 262176 | tf_op jit(solution)/shard_map/all_to_all | solution.py:355
  56.6 0.6 %fusion = (f32[32,128]{1,0:T(8,128)}, f32[32,128]{1,0:T(8,128)}) fusion(f32[32,256]{1,0:T(8,128)S(1)} %convert_reduce_fusion), kind=kLoop, calls=%fused_computation.2 | loop fusion | bytes 65536 | tf_op jit(solution)/shard_map/slice | solution.py:381
  (1 shorter events, 0.0 us)
Async XLA Ops:
  2.1 21.1 %all-to-all-start = ((bf16[16,32,256]{2,1,0:T(8,128)(2,1)}), bf16[16,32,256]{2,1,0:T(8,128)(2,1)S(1)}, u32[]{:S(2)}, u32[]{:S(2)}) async-start(bf16[16,32,256]{2,1,0:T(8,128)(2,1)} %spread.1), calls=%async_computation | async-start | bytes 524288 | tf_op jit(solution)/shard_map/all_to_all | solution.py:305
  23.2 3.4 %collective-permute-start = (bf16[512,256]{1,0:T(8,128)(2,1)S(1)}, bf16[512,256]{1,0:T(8,128)(2,1)S(1)}, u32[]{:S(2)}, u32[]{:S(2)}) collective-permute-start(bf16[512,256]{1,0:T(8,128)(2,1)S(1)} %bitcast.2), channel_id=1, source_target_pairs={{0,4},{4,0},{8,12},{12,8},{16,20},{20,16},{24,28},{28,24},{32,36},... | collective-permute-start | bytes 786440 | tf_op jit(solution)/shard_map/ppermute | solution.py:324
  35.8 3.4 %collective-permute-start.1 = (bf16[512,256]{1,0:T(8,128)(2,1)S(1)}, bf16[512,256]{1,0:T(8,128)(2,1)S(1)}, u32[]{:S(2)}, u32[]{:S(2)}) collective-permute-start(bf16[512,256]{1,0:T(8,128)(2,1)S(1)} %get-tuple-element.32), channel_id=1, source_target_pairs={{0,4},{4,0},{8,12},{12,8},{16,20},{20,16},{24,28},{28,24},{32,36},... | collective-permute-start | bytes 786440 | tf_op jit(solution)/shard_map/ppermute | solution.py:353
  40.0 16.6 %all-to-all-start.1 = ((bf16[16,32,256]{2,1,0:T(8,128)(2,1)}), bf16[16,32,256]{2,1,0:T(8,128)(2,1)S(1)}, u32[]{:S(2)}, u32[]{:S(2)}) async-start(bf16[16,32,256]{2,1,0:T(8,128)(2,1)} %bitcast.1), calls=%async_computation.1 | async-start | bytes 524288 | tf_op jit(solution)/shard_map/all_to_all | solution.py:355

commit v7 on v6

--- a/solution.py
+++ b/solution.py
@@ -11,12 +11,13 @@
 GROUP = 5
 QB = 256
 SHARD = 32
+LATE = 3
 SCALE = HD ** (-0.5)
 LOG2E = 1.4426950408889634
 C2 = SCALE * LOG2E
 F32 = jnp.float32
 BF16 = jnp.bfloat16
-VMEM_LIMIT = 40 * 1024 * 1024
+VMEM_LIMIT = 32 * 1024 * 1024
 
 NT = (((1,), (1,)), ((), ()))
 
@@ -37,20 +38,6 @@
 
 def lanes(head):
     return pl.ds(pl.multiple_of(head * HD, HD), HD)
-
-
-def spread_kernel(k_ref, v_ref, out_ref, held_ref, sems):
-    copies = [
-        pltpu.make_async_copy(src, held_ref.at[i], sems.at[i])
-        for i, src in enumerate((k_ref, v_ref))
-    ]
-    for copy in copies:
-        copy.start()
-    for copy in copies:
-        copy.wait()
-    for chip in range(out_ref.shape[0]):
-        out_ref[chip, :, 0:HD] = held_ref[0]
-        out_ref[chip, :, HD:] = held_ref[1]
 
 
 def own_stats_kernel(
@@ -86,12 +73,13 @@
 
 def prompt_kernel(
     q_ref, g_ref, mine_ref, other_ref, max_ref, sum_ref, del_ref,
-    ds_ref, keep_ref, send_ref, lse_ref, delta_ref,
+    ds_ref, keep_ref, send_ref, lse_ref, delta_ref, late_p_ref, late_d_ref,
     total_ref, ks_ref, v_ref, d_ref, prob_ref, sems, *scratch,
 ):
     half = mine_ref.shape[0]
     tokens = 2 * half
     tile = 64
+    early = GROUP - LATE
     chunk = tokens // 4
     blocks = MAXLEN // QB
     items = GROUP * blocks
@@ -124,9 +112,8 @@
             return
         if c % 2 == 0:
             product = product * SCALE
-        out = keep_ref if c < 4 else send_ref
         row = c % 4 // 2 * chunk
-        out[row : row + chunk, lane] = product.astype(out.dtype)
+        send_ref[row : row + chunk, lane] = product.astype(send_ref.dtype)
 
     def save(head):
         return pltpu.make_async_copy(d_ref.at[head], ds_ref.at[head], sems.at[head])
@@ -175,17 +162,23 @@
         for c in range(4):
             if ahead:
                 dp = dot_nt(v_ref[part(c), :], g)
-            if cur and head:
+            due = cur and head and (block or head - 1 < early)
+            if due:
                 product = grad_product(head - 1, 4 * block + c)
             if cur:
                 for t in range(c * chunk, (c + 1) * chunk, tile):
                     p = s_ref[t : t + tile, :] * inverse
-                    prob_ref[head % 2, t : t + tile, rows] = p.astype(BF16)
-                    ds = p * (dp_ref[t : t + tile, :] - delta)
-                    d_ref[head, t : t + tile, rows] = ds.astype(BF16)
+                    ph = p.astype(BF16)
+                    ds = (p * (dp_ref[t : t + tile, :] - delta)).astype(BF16)
+                    d_ref[head, t : t + tile, rows] = ds
+                    if head >= early and t < half:
+                        late_p_ref[head - early, t : t + tile, rows] = ph
+                        late_d_ref[head - early, t : t + tile, rows] = ds
+                    else:
+                        prob_ref[head % 2, t : t + tile, rows] = ph
             if ahead:
                 dp_next[part(c), :] = dp
-            if cur and head:
+            if due:
                 grad_add(head - 1, 4 * block + c, product)
 
     for first, side_ref in ((0, mine_ref), (half, other_ref)):
@@ -200,10 +193,23 @@
         step(item)
         if item % blocks == blocks - 1 and item >= 0:
             save(item // blocks).start()
-    for c in range(8):
+    for c in range(4, 8):
         grad_add(GROUP - 1, c, grad_product(GROUP - 1, c))
+    keep_ref[...] = total_ref[0:half, :]
     for head in range(GROUP):
         save(head).wait()
+
+
+def keep_kernel(q_ref, g_ref, p_ref, d_ref, early_ref, out_ref):
+    dk = early_ref[:, 0:HD]
+    dv = early_ref[:, HD:]
+    for late in range(LATE):
+        head = GROUP - LATE + late
+        cols = slice(head * HD, (head + 1) * HD)
+        dk = dk + dot(d_ref[late], q_ref[:, cols])
+        dv = dv + dot(p_ref[late], g_ref[:, cols])
+    out_ref[:, 0:HD] = dk * SCALE
+    out_ref[:, HD:] = dv
 
 
 def grads_kernel(
@@ -294,14 +300,10 @@
     chips = devices // 2
     swap = [(d, d ^ 1) for d in range(devices)]
     same_core = [[2 * chip + core for chip in range(chips)] for core in range(2)]
-    spread = pl.pallas_call(
-        spread_kernel,
-        in_specs=[pl.BlockSpec(memory_space=pltpu.HBM)] * 2,
-        out_specs=VMEM,
-        out_shape=struct((chips, SHARD, 2 * HD), BF16),
-        scratch_shapes=[pltpu.VMEM((2, SHARD, HD), BF16), pltpu.SemaphoreType.DMA((2,))],
-        name="spread",
-    )(prompt_keys, prompt_values)
+    side_by_side = jnp.pad(prompt_keys, ((0, 0), (0, HD))) + jnp.pad(
+        prompt_values, ((0, 0), (HD, 0))
+    )
+    spread = jnp.broadcast_to(side_by_side[None], (chips, SHARD, 2 * HD))
     mine = lax.all_to_all(spread, "comp", 0, 0, axis_index_groups=same_core, tiled=True)
     mine = mine.reshape(half, 2 * HD)
 
@@ -323,13 +325,15 @@
     mine, masked = lax.optimization_barrier((mine, masked))
     other = lax.ppermute(mine, "comp", swap)
 
-    dscore, grad_keep, grad_send, lse, delta = pl.pallas_call(
+    late = (LATE, half, MAXLEN)
+    dscore, grad_early, grad_send, lse, delta, late_p, late_d = pl.pallas_call(
         prompt_kernel,
         in_specs=[VMEM] * 7,
-        out_specs=[pl.BlockSpec(memory_space=pltpu.HBM)] + [VMEM] * 4,
+        out_specs=[pl.BlockSpec(memory_space=pltpu.HBM)] + [VMEM] * 6,
         out_shape=[
             hbm_struct((GROUP, tokens, MAXLEN), BF16),
             struct((half, 2 * HD), F32), struct((half, 2 * HD), BF16), stat, stat,
+            vmem_struct(late, BF16), vmem_struct(late, BF16),
         ],
         scratch_shapes=[
             pltpu.VMEM((tokens, 2 * HD), F32),
@@ -351,6 +355,15 @@
     )(vmem(copied), vmem(masked), mine, other, own_max, own_sum, own_del)
 
     received = lax.ppermute(grad_send, "comp", swap)
+    grad_keep = pl.pallas_call(
+        keep_kernel,
+        in_specs=[VMEM] * 5,
+        out_specs=VMEM,
+        out_shape=struct((half, 2 * HD), F32),
+        compiler_params=pltpu.CompilerParams(vmem_limit_bytes=16 * 1024 * 1024),
+        cost_estimate=cost(LATE * 2 * 1024 * 512 * HD, 0, 2**22),
+        name="keep",
+    )(vmem(copied), vmem(masked), vmem(late_p), vmem(late_d), grad_early)
     total = (grad_keep + received.astype(F32)).astype(BF16).reshape(chips, SHARD, 2 * HD)
     arrived = lax.all_to_all(total, "comp", 0, 0, axis_index_groups=same_core, tiled=True)
     grad_prompt = jnp.sum(arrived.astype(F32), axis=0)

time: 57.8 us -> 57.5 us (level)
  waiting for transfers between devices: 14.6 us -> 13.6 us
  local copies, waits for them, and re-layouts: 0.61 us -> 1.34 us
  other arithmetic: 0.8 us -> 1.52 us
  Pallas kernels: 23.3 us -> 22.6 us
    ppermute x1, waiting for transfers between devices: 1.37 us -> 0.38 us  [per_device(): received = lax.ppermute(grad_send, 'comp', swap)]
    broadcast_in_dim x0 -> x1, local copies, waits for them, and re-layouts: none -> 0.73 us  [per_device(): spread = jnp.broadcast_to(side_by_side[None], (chips, SHARD, 2 * HD))]
    add x0 -> x1, other arithmetic: none -> 0.72 us  [per_device(): jnp.pad(prompt_keys, ((0, 0), (0, HD)))]
  transfers between devices with their start and end apart: 4 -> 4, of which waited for: 4 -> 4; matrix products, arithmetic and copies ran while one was open for 0% -> 0% of each run, Pallas kernels for 22% -> 24%
where the time goes in v7:
time: 57.5 us; the launch traced here: 57 us
  Pallas kernels  22.6 us (39%)
  starting transfers between devices  16.5 us (29%)
  waiting for transfers between devices  13.6 us (24%)
  other arithmetic  1.52 us (3%)
  local copies, waits for them, and re-layouts  1.34 us (2%)
  between operations  1.34 us (2%)
    all_to_all x1, starting transfers between devices, per_device(): lax.all_to_all(spread, 'comp', 0, 0, axis_index_groups=same_core, tiled=T...  9.01 us
    pallas_call x1, Pallas kernels, per_device(): pl.pallas_call(prompt_kernel, in_specs=[VMEM] * 7, out_specs=[pl.BlockSpe...  9 us
    pallas_call x1, Pallas kernels, per_device(): pl.pallas_call(grads_kernel, grid=(GROUP,), in_specs=[VMEM, VMEM, whole((...  8.1 us
    all_to_all x1, waiting for transfers between devices, per_device(): lax.all_to_all(spread, 'comp', 0, 0, axis_index_groups=same_core, tiled=T...  6.83 us
    all_to_all x1, waiting for transfers between devices, per_device(): lax.all_to_all(total, 'comp', 0, 0, axis_index_groups=same_core, tiled=True)  4.92 us
    pallas_call x1, Pallas kernels, per_device(): pl.pallas_call(own_stats_kernel, grid=(GROUP,), in_specs=[SMEM, HEAD, HEA...  4.55 us
    all_to_all x1, starting transfers between devices, per_device(): lax.all_to_all(total, 'comp', 0, 0, axis_index_groups=same_core, tiled=True)  3.53 us
    ppermute x1, starting transfers between devices, per_device(): received = lax.ppermute(grad_send, 'comp', swap)  2.05 us
  transfers between devices with their start and end apart: 4, of which 4 were waited for; matrix products, arithmetic and copies ran while one was open for 0% of the time, Pallas kernels for 24%

profile of v7, /device:TPU:6, one launch (start us, length us, event | category | flops | bytes accessed | tf_op | source)
XLA Modules:
  0.0 57.0 jit_solution(1028964295807923796)
XLA Ops:
  0.6 0.7 %pad_add_fusion = bf16[32,256]{1,0:T(8,128)(2,1)S(1)} fusion(bf16[32,128]{1,0:T(8,128)(2,1)} %param.12, bf16[32,128]{1,0:T(8,128)(2,1)} %param.11), kind=kLoop, calls=%fused_computation.2 | loop fusion | flops 32768 | bytes 32768 | tf_op jit(solution)/shard_map/add | solution.py:303
  1.4 0.7 %broadcast_in_dim.2 = bf16[16,32,256]{2,1,0:T(8,128)(2,1)} broadcast(bf16[32,256]{1,0:T(8,128)(2,1)S(1)} %pad_add_fusion), dimensions={1,2} | broadcast | bytes 278528 | tf_op jit(solution)/shard_map/broadcast_in_dim | solution.py:306
  2.1 9.0 %all-to-all-start = ((bf16[16,32,256]{2,1,0:T(8,128)(2,1)}), bf16[16,32,256]{2,1,0:T(8,128)(2,1)S(1)}, u32[]{:S(2)}, u32[]{:S(2)}) async-start(bf16[16,32,256]{2,1,0:T(8,128)(2,1)} %broadcast_in_dim.2), calls=%async_computation | async-start | bytes 524288 | tf_op jit(solution)/shard_map/all_to_all | solution.py:307
  11.7 4.6 %own_stats.1 = (bf16[512,640]{1,0:T(8,128)(2,1)S(1)}, bf16[512,640]{1,0:T(8,128)(2,1)S(1)}, f32[5,1,512]{2,1,0:T(1,128)S(1)}, f32[5,1,512]{2,1,0:T(1,128)S(1)}, f32[5,1,512]{2,1,0:T(1,128)S(1)}) custom-call(s32[1]{0:T(128)S(6)} %copy.12.len_ref, bf16[512,640]{1,0:T(8,128)(2,1)} %q_ref.1, bf16[512,640]{1,0:T(8,128)(2,1)} %g_ref.1, bf16[512,128]{1,0:T(8,128)(2,1)} %k_ref.3, ...), custom_call_target="tpu_custom_call" | custom-call | flops 503316480 | bytes 2097152 | tf_op jit(solution)/shard_map/own_stats/pallas_call | solution.py:311
  16.3 6.8 %all-to-all-done = bf16[16,32,256]{2,1,0:T(8,128)(2,1)S(1)} async-done(((bf16[16,32,256]{2,1,0:T(8,128)(2,1)}), bf16[16,32,256]{2,1,0:T(8,128)(2,1)S(1)}, u32[]{:S(2)}, u32[]{:S(2)}) %all-to-all-start) | async-done | bytes 262176 | tf_op jit(solution)/shard_map/all_to_all | solution.py:307
  23.1 1.9 %collective-permute-start = (bf16[512,256]{1,0:T(8,128)(2,1)S(1)}, bf16[512,256]{1,0:T(8,128)(2,1)S(1)}, u32[]{:S(2)}, u32[]{:S(2)}) collective-permute-start(bf16[512,256]{1,0:T(8,128)(2,1)S(1)} %bitcast.2), channel_id=1, source_target_pairs={{0,4},{4,0},{8,12},{12,8},{16,20},{20,16},{24,28},{28,24},{32,36},... | collective-permute-start | bytes 786440 | tf_op jit(solution)/shard_map/ppermute | solution.py:326
  25.1 1.5 %collective-permute-done.other_ref = bf16[512,256]{1,0:T(8,128)(2,1)S(1)} collective-permute-done((bf16[512,256]{1,0:T(8,128)(2,1)S(1)}, bf16[512,256]{1,0:T(8,128)(2,1)S(1)}, u32[]{:S(2)}, u32[]{:S(2)}) %collective-permute-start) | collective-permute-done | bytes 262176 | tf_op jit(solution)/shard_map/ppermute | solution.py:326
  26.6 9.0 %prompt.1 = (bf16[5,1024,512]{2,1,0:T(8,128)(2,1)}, f32[512,256]{1,0:T(8,128)S(1)}, bf16[512,256]{1,0:T(8,128)(2,1)S(1)}, f32[5,1,512]{2,1,0:T(1,128)S(1)}, f32[...) custom-call(bf16[512,640]{1,0:T(8,128)(2,1)S(1)} %get-tuple-element.22.q_ref, ...), custom_call_target="tpu_custom_call" | custom-call | flops 2684354560 | bytes 8388608 | tf_op jit(solution)/shard_map/prompt/pallas_call | solution.py:329
  35.6 2.0 %collective-permute-start.1 = (bf16[512,256]{1,0:T(8,128)(2,1)S(1)}, bf16[512,256]{1,0:T(8,128)(2,1)S(1)}, u32[]{:S(2)}, u32[]{:S(2)}) collective-permute-start(bf16[512,256]{1,0:T(8,128)(2,1)S(1)} %get-tuple-element.36), channel_id=1, source_target_pairs={{0,4},{4,0},{8,12},{12,8},{16,20},{20,16},{24,28},{28,24},{32,36},... | collective-permute-start | bytes 786440 | tf_op jit(solution)/shard_map/ppermute | solution.py:357
  37.6 1.0 %keep.1 = f32[512,256]{1,0:T(8,128)S(1)} custom-call(bf16[512,640]{1,0:T(8,128)(2,1)S(1)} %get-tuple-element.22.q_ref, bf16[512,640]{1,0:T(8,128)(2,1)S(1)} %get-tuple-element.24.g_ref, bf16[3,512,512]{2,1,0:T(8,128)(2,1)S(1)} %get-tuple-element.33.p_ref, bf16[3,512,512]{2,1,0:T(8,128)(2,1)S(1)} %get-tuple-element.34.d_ref, ...), custom_call_target="tpu_custom_call" | custom-call | flops 402653184 | bytes 4194304 | tf_op jit(solution)/shard_map/keep/pallas_call | solution.py:358
  38.6 0.4 collective-permute-done.1
  39.0 0.8 %add_convert_fusion = bf16[512,256]{1,0:T(8,128)(2,1)} fusion(f32[512,256]{1,0:T(8,128)S(1)} %keep.1, bf16[512,256]{1,0:T(8,128)(2,1)S(1)} %collective-permute-done.1), kind=kLoop, calls=%fused_computation.1 | loop fusion | flops 393216 | bytes 1048576 | tf_op jit(solution)/shard_map/convert_element_type | solution.py:367
  39.8 3.5 %all-to-all-start.1 = ((bf16[16,32,256]{2,1,0:T(8,128)(2,1)}), bf16[16,32,256]{2,1,0:T(8,128)(2,1)S(1)}, u32[]{:S(2)}, u32[]{:S(2)}) async-start(bf16[16,32,256]{2,1,0:T(8,128)(2,1)} %bitcast.1), calls=%async_computation.1 | async-start | bytes 524288 | tf_op jit(solution)/shard_map/all_to_all | solution.py:368
  43.3 8.1 %grads.1 = (f32[512,640]{1,0:T(8,128)}, f32[512,128]{1,0:T(8,128)}, f32[512,128]{1,0:T(8,128)}) custom-call(bf16[512,640]{1,0:T(8,128)(2,1)S(1)} %get-tuple-element.22.q_ref, bf16[512,640]{1,0:T(8,128)(2,1)S(1)} %get-tuple-element.24.g_ref, bf16[512,128]{1,0:T(8,128)(2,1)} %k_ref.3, bf16[512,128]{1,0:T(8,128)(2,1)} %v_ref.3, ...), custom_call_target="tpu_custom_call" | custom-call | flops 1342177280 | bytes 8388608 | tf_op jit(solution)/shard_map/grads/pallas_call | solution.py:371
  51.4 4.9 %all-to-all-done.1 = bf16[16,32,256]{2,1,0:T(8,128)(2,1)S(1)} async-done(((bf16[16,32,256]{2,1,0:T(8,128)(2,1)}), bf16[16,32,256]{2,1,0:T(8,128)(2,1)S(1)}, u32[]{:S(2)}, u32[]{:S(2)}) %all-to-all-start.1) | async-done | bytes 262176 | tf_op jit(solution)/shard_map/all_to_all | solution.py:368
  56.4 0.6 %fusion = (f32[32,128]{1,0:T(8,128)}, f32[32,128]{1,0:T(8,128)}) fusion(f32[32,256]{1,0:T(8,128)S(1)} %convert_reduce_fusion), kind=kLoop, calls=%fused_computation.3 | loop fusion | bytes 65536 | tf_op jit(solution)/shard_map/slice | solution.py:394
  (1 shorter events, 0.0 us)
Async XLA Ops:
  2.1 21.1 %all-to-all-start = ((bf16[16,32,256]{2,1,0:T(8,128)(2,1)}), bf16[16,32,256]{2,1,0:T(8,128)(2,1)S(1)}, u32[]{:S(2)}, u32[]{:S(2)}) async-start(bf16[16,32,256]{2,1,0:T(8,128)(2,1)} %broadcast_in_dim.2), calls=%async_computation | async-start | bytes 524288 | tf_op jit(solution)/shard_map/all_to_all | solution.py:307
  23.1 3.4 %collective-permute-start = (bf16[512,256]{1,0:T(8,128)(2,1)S(1)}, bf16[512,256]{1,0:T(8,128)(2,1)S(1)}, u32[]{:S(2)}, u32[]{:S(2)}) collective-permute-start(bf16[512,256]{1,0:T(8,128)(2,1)S(1)} %bitcast.2), channel_id=1, source_target_pairs={{0,4},{4,0},{8,12},{12,8},{16,20},{20,16},{24,28},{28,24},{32,36},... | collective-permute-start | bytes 786440 | tf_op jit(solution)/shard_map/ppermute | solution.py:326
  35.6 3.4 %collective-permute-start.1 = (bf16[512,256]{1,0:T(8,128)(2,1)S(1)}, bf16[512,256]{1,0:T(8,128)(2,1)S(1)}, u32[]{:S(2)}, u32[]{:S(2)}) collective-permute-start(bf16[512,256]{1,0:T(8,128)(2,1)S(1)} %get-tuple-element.36), channel_id=1, source_target_pairs={{0,4},{4,0},{8,12},{12,8},{16,20},{20,16},{24,28},{28,24},{32,36},... | collective-permute-start | bytes 786440 | tf_op jit(solution)/shard_map/ppermute | solution.py:357
  39.8 16.6 %all-to-all-start.1 = ((bf16[16,32,256]{2,1,0:T(8,128)(2,1)}), bf16[16,32,256]{2,1,0:T(8,128)(2,1)S(1)}, u32[]{:S(2)}, u32[]{:S(2)}) async-start(bf16[16,32,256]{2,1,0:T(8,128)(2,1)} %bitcast.1), calls=%async_computation.1 | async-start | bytes 524288 | tf_op jit(solution)/shard_map/all_to_all | solution.py:368

commit v8 on v7

--- a/solution.py
+++ b/solution.py
@@ -74,7 +74,7 @@
 def prompt_kernel(
     q_ref, g_ref, mine_ref, other_ref, max_ref, sum_ref, del_ref,
     ds_ref, keep_ref, send_ref, lse_ref, delta_ref, late_p_ref, late_d_ref,
-    total_ref, ks_ref, v_ref, d_ref, prob_ref, sems, *scratch,
+    total_ref, ks_ref, v_ref, vt_ref, d_ref, prob_ref, sems, *scratch,
 ):
     half = mine_ref.shape[0]
     tokens = 2 * half
@@ -89,7 +89,7 @@
         return head, slice(block * QB, (block + 1) * QB), slice(head * HD, (head + 1) * HD)
 
     def buffers(item):
-        return scratch[item % 2 * 3 : item % 2 * 3 + 3]
+        return scratch[item % 2 * 2 : item % 2 * 2 + 2]
 
     def part(c):
         return slice(c * chunk, (c + 1) * chunk)
@@ -123,20 +123,19 @@
         ahead = item + 1 < items
         if ahead:
             _, rows_n, cols_n = place(item + 1)
-            s_next, dp_next, top_next = buffers(item + 1)
+            s_next, top_next = buffers(item + 1)
             q = q_ref[rows_n, cols_n]
             q = jnp.concatenate([q, q], axis=1)
-            g = g_ref[rows_n, cols_n]
             tops = None
         if cur:
-            head, rows, _ = place(item)
+            head, rows, cols = place(item)
             block = item % blocks
-            s_ref, dp_ref, top_ref = buffers(item)
+            s_ref, top_ref = buffers(item)
+            g = g_ref[rows, cols]
             own_top = max_ref[head, :, rows]
             top = jnp.maximum(jnp.max(top_ref[...], axis=0, keepdims=True), own_top)
             own = jnp.exp2(own_top - top)
             total = jnp.zeros((8, QB), F32)
-            delta = jnp.zeros((8, QB), F32)
         for c in range(4):
             if ahead:
                 s = dot_nt(ks_ref[part(c), :], q)
@@ -145,45 +144,46 @@
                     e = jnp.exp2(s_ref[t : t + tile, :] - top)
                     s_ref[t : t + tile, :] = e
                     total = total + jnp.sum(fold(e), axis=0)
-                    delta = delta + jnp.sum(fold(e * dp_ref[t : t + tile, :]), axis=0)
             if ahead:
                 s_next[part(c), :] = s
                 high = jnp.max(fold(s), axis=0)
                 tops = high if tops is None else jnp.maximum(tops, high)
         if ahead:
             top_next[...] = tops
-        if cur:
-            total = jnp.sum(total, axis=0, keepdims=True) + own * sum_ref[head, :, rows]
-            delta = jnp.sum(delta, axis=0, keepdims=True) + own * del_ref[head, :, rows]
-            inverse = 1.0 / total
-            delta = delta * inverse
-            lse_ref[head, :, rows] = top + jnp.log2(total)
-            delta_ref[head, :, rows] = delta
+        if not cur:
+            return
+        total = jnp.sum(total, axis=0, keepdims=True) + own * sum_ref[head, :, rows]
+        inverse = 1.0 / total
+        lse_ref[head, :, rows] = top + jnp.log2(total)
+        due = head and (block or head - 1 < early)
+        attended = jnp.zeros((HD, QB), F32)
         for c in range(4):
-            if ahead:
-                dp = dot_nt(v_ref[part(c), :], g)
-            due = cur and head and (block or head - 1 < early)
             if due:
                 product = grad_product(head - 1, 4 * block + c)
-            if cur:
-                for t in range(c * chunk, (c + 1) * chunk, tile):
-                    p = s_ref[t : t + tile, :] * inverse
-                    ph = p.astype(BF16)
-                    ds = (p * (dp_ref[t : t + tile, :] - delta)).astype(BF16)
-                    d_ref[head, t : t + tile, rows] = ds
-                    if head >= early and t < half:
-                        late_p_ref[head - early, t : t + tile, rows] = ph
-                        late_d_ref[head - early, t : t + tile, rows] = ds
-                    else:
-                        prob_ref[head % 2, t : t + tile, rows] = ph
-            if ahead:
-                dp_next[part(c), :] = dp
+            late = head >= early and c < 2
+            prob, slot = (late_p_ref, head - early) if late else (prob_ref, head % 2)
+            for t in range(c * chunk, (c + 1) * chunk, tile):
+                p = s_ref[t : t + tile, :] * inverse
+                prob[slot, t : t + tile, rows] = p.astype(BF16)
+            attended = attended + dot(vt_ref[:, part(c)], prob[slot, part(c), rows])
             if due:
                 grad_add(head - 1, 4 * block + c, product)
+        delta = jnp.sum(attended * g.T.astype(F32), axis=0, keepdims=True)
+        delta = delta + own * inverse * del_ref[head, :, rows]
+        delta_ref[head, :, rows] = delta
+        for c in range(0, tokens, chunk // 2):
+            dp = dot_nt(v_ref[c : c + chunk // 2, :], g)
+            for t in range(c, c + chunk // 2, tile):
+                p = s_ref[t : t + tile, :] * inverse
+                ds = (p * (dp[t - c : t - c + tile] - delta)).astype(BF16)
+                d_ref[head, t : t + tile, rows] = ds
+                if head >= early and t < half:
+                    late_d_ref[head - early, t : t + tile, rows] = ds
 
     for first, side_ref in ((0, mine_ref), (half, other_ref)):
         side = slice(first, first + half)
         v_ref[side, :] = side_ref[:, HD:]
+        vt_ref[:, side] = side_ref[:, HD:].T
         scaled = side_ref[:, 0:HD].astype(F32) * C2
         high = scaled.astype(BF16)
         ks_ref[side, 0:HD] = high
@@ -339,12 +339,12 @@
             pltpu.VMEM((tokens, 2 * HD), F32),
             pltpu.VMEM((tokens, 2 * HD), BF16),
             pltpu.VMEM((tokens, HD), BF16),
+            pltpu.VMEM((HD, tokens), BF16),
             pltpu.VMEM((GROUP, tokens, MAXLEN), BF16),
             pltpu.VMEM((2, tokens, MAXLEN), BF16),
             pltpu.SemaphoreType.DMA((GROUP,)),
         ]
         + [
-            pltpu.VMEM((tokens, QB), F32),
             pltpu.VMEM((tokens, QB), F32),
             pltpu.VMEM((8, QB), F32),
         ]

time: 57.5 us -> 57.1 us (level)
  no operation moved by 1% of the time
where the time goes in v8:
time: 57.1 us; the launch traced here: 56.5 us
  Pallas kernels  22.1 us (39%)
  starting transfers between devices  16.5 us (29%)
  waiting for transfers between devices  13.6 us (24%)
  other arithmetic  1.52 us (3%)
  local copies, waits for them, and re-layouts  1.34 us (2%)
  between operations  1.34 us (2%)
    all_to_all x1, starting transfers between devices, per_device(): lax.all_to_all(spread, 'comp', 0, 0, axis_index_groups=same_core, tiled=T...  9.01 us
    pallas_call x1, Pallas kernels, per_device(): pl.pallas_call(prompt_kernel, in_specs=[VMEM] * 7, out_specs=[pl.BlockSpe...  8.52 us
    pallas_call x1, Pallas kernels, per_device(): pl.pallas_call(grads_kernel, grid=(GROUP,), in_specs=[VMEM, VMEM, whole((...  8.09 us
    all_to_all x1, waiting for transfers between devices, per_device(): lax.all_to_all(spread, 'comp', 0, 0, axis_index_groups=same_core, tiled=T...  6.83 us
    all_to_all x1, waiting for transfers between devices, per_device(): lax.all_to_all(total, 'comp', 0, 0, axis_index_groups=same_core, tiled=True)  4.92 us
    pallas_call x1, Pallas kernels, per_device(): pl.pallas_call(own_stats_kernel, grid=(GROUP,), in_specs=[SMEM, HEAD, HEA...  4.55 us
    all_to_all x1, starting transfers between devices, per_device(): lax.all_to_all(total, 'comp', 0, 0, axis_index_groups=same_core, tiled=True)  3.53 us
    ppermute x1, starting transfers between devices, per_device(): received = lax.ppermute(grad_send, 'comp', swap)  2.04 us
  transfers between devices with their start and end apart: 4, of which 4 were waited for; matrix products, arithmetic and copies ran while one was open for 0% of the time, Pallas kernels for 24%

profile of v8, /device:TPU:6, one launch (start us, length us, event | category | flops | bytes accessed | tf_op | source)
XLA Modules:
  0.0 56.5 jit_solution(7682660779628204537)
XLA Ops:
  0.6 0.7 %pad_add_fusion = bf16[32,256]{1,0:T(8,128)(2,1)S(1)} fusion(bf16[32,128]{1,0:T(8,128)(2,1)} %param.12, bf16[32,128]{1,0:T(8,128)(2,1)} %param.11), kind=kLoop, calls=%fused_computation.2 | loop fusion | flops 32768 | bytes 32768 | tf_op jit(solution)/shard_map/add | solution.py:303
  1.4 0.7 %broadcast_in_dim.2 = bf16[16,32,256]{2,1,0:T(8,128)(2,1)} broadcast(bf16[32,256]{1,0:T(8,128)(2,1)S(1)} %pad_add_fusion), dimensions={1,2} | broadcast | bytes 278528 | tf_op jit(solution)/shard_map/broadcast_in_dim | solution.py:306
  2.1 9.0 %all-to-all-start = ((bf16[16,32,256]{2,1,0:T(8,128)(2,1)}), bf16[16,32,256]{2,1,0:T(8,128)(2,1)S(1)}, u32[]{:S(2)}, u32[]{:S(2)}) async-start(bf16[16,32,256]{2,1,0:T(8,128)(2,1)} %broadcast_in_dim.2), calls=%async_computation | async-start | bytes 524288 | tf_op jit(solution)/shard_map/all_to_all | solution.py:307
  11.7 4.6 %own_stats.1 = (bf16[512,640]{1,0:T(8,128)(2,1)S(1)}, bf16[512,640]{1,0:T(8,128)(2,1)S(1)}, f32[5,1,512]{2,1,0:T(1,128)S(1)}, f32[5,1,512]{2,1,0:T(1,128)S(1)}, f32[5,1,512]{2,1,0:T(1,128)S(1)}) custom-call(s32[1]{0:T(128)S(6)} %copy.12.len_ref, bf16[512,640]{1,0:T(8,128)(2,1)} %q_ref.1, bf16[512,640]{1,0:T(8,128)(2,1)} %g_ref.1, bf16[512,128]{1,0:T(8,128)(2,1)} %k_ref.3, ...), custom_call_target="tpu_custom_call" | custom-call | flops 503316480 | bytes 2097152 | tf_op jit(solution)/shard_map/own_stats/pallas_call | solution.py:311
  16.3 6.8 %all-to-all-done = bf16[16,32,256]{2,1,0:T(8,128)(2,1)S(1)} async-done(((bf16[16,32,256]{2,1,0:T(8,128)(2,1)}), bf16[16,32,256]{2,1,0:T(8,128)(2,1)S(1)}, u32[]{:S(2)}, u32[]{:S(2)}) %all-to-all-start) | async-done | bytes 262176 | tf_op jit(solution)/shard_map/all_to_all | solution.py:307
  23.1 1.9 %collective-permute-start = (bf16[512,256]{1,0:T(8,128)(2,1)S(1)}, bf16[512,256]{1,0:T(8,128)(2,1)S(1)}, u32[]{:S(2)}, u32[]{:S(2)}) collective-permute-start(bf16[512,256]{1,0:T(8,128)(2,1)S(1)} %bitcast.2), channel_id=1, source_target_pairs={{0,4},{4,0},{8,12},{12,8},{16,20},{20,16},{24,28},{28,24},{32,36},... | collective-permute-start | bytes 786440 | tf_op jit(solution)/shard_map/ppermute | solution.py:326
  25.1 1.5 %collective-permute-done.other_ref = bf16[512,256]{1,0:T(8,128)(2,1)S(1)} collective-permute-done((bf16[512,256]{1,0:T(8,128)(2,1)S(1)}, bf16[512,256]{1,0:T(8,128)(2,1)S(1)}, u32[]{:S(2)}, u32[]{:S(2)}) %collective-permute-start) | collective-permute-done | bytes 262176 | tf_op jit(solution)/shard_map/ppermute | solution.py:326
  26.6 8.5 %prompt.1 = (bf16[5,1024,512]{2,1,0:T(8,128)(2,1)}, f32[512,256]{1,0:T(8,128)S(1)}, bf16[512,256]{1,0:T(8,128)(2,1)S(1)}, f32[5,1,512]{2,1,0:T(1,128)S(1)}, f32[...) custom-call(bf16[512,640]{1,0:T(8,128)(2,1)S(1)} %get-tuple-element.22.q_ref, ...), custom_call_target="tpu_custom_call" | custom-call | flops 2684354560 | bytes 8388608 | tf_op jit(solution)/shard_map/prompt/pallas_call | solution.py:329
  35.1 2.0 %collective-permute-start.1 = (bf16[512,256]{1,0:T(8,128)(2,1)S(1)}, bf16[512,256]{1,0:T(8,128)(2,1)S(1)}, u32[]{:S(2)}, u32[]{:S(2)}) collective-permute-start(bf16[512,256]{1,0:T(8,128)(2,1)S(1)} %get-tuple-element.36), channel_id=1, source_target_pairs={{0,4},{4,0},{8,12},{12,8},{16,20},{20,16},{24,28},{28,24},{32,36},... | collective-permute-start | bytes 786440 | tf_op jit(solution)/shard_map/ppermute | solution.py:357
  37.1 1.0 %keep.1 = f32[512,256]{1,0:T(8,128)S(1)} custom-call(bf16[512,640]{1,0:T(8,128)(2,1)S(1)} %get-tuple-element.22.q_ref, bf16[512,640]{1,0:T(8,128)(2,1)S(1)} %get-tuple-element.24.g_ref, bf16[3,512,512]{2,1,0:T(8,128)(2,1)S(1)} %get-tuple-element.33.p_ref, bf16[3,512,512]{2,1,0:T(8,128)(2,1)S(1)} %get-tuple-element.34.d_ref, ...), custom_call_target="tpu_custom_call" | custom-call | flops 402653184 | bytes 4194304 | tf_op jit(solution)/shard_map/keep/pallas_call | solution.py:358
  38.1 0.4 collective-permute-done.1
  38.5 0.8 %add_convert_fusion = bf16[512,256]{1,0:T(8,128)(2,1)} fusion(f32[512,256]{1,0:T(8,128)S(1)} %keep.1, bf16[512,256]{1,0:T(8,128)(2,1)S(1)} %collective-permute-done.1), kind=kLoop, calls=%fused_computation.1 | loop fusion | flops 393216 | bytes 1048576 | tf_op jit(solution)/shard_map/convert_element_type | solution.py:367
  39.3 3.5 %all-to-all-start.1 = ((bf16[16,32,256]{2,1,0:T(8,128)(2,1)}), bf16[16,32,256]{2,1,0:T(8,128)(2,1)S(1)}, u32[]{:S(2)}, u32[]{:S(2)}) async-start(bf16[16,32,256]{2,1,0:T(8,128)(2,1)} %bitcast.1), calls=%async_computation.1 | async-start | bytes 524288 | tf_op jit(solution)/shard_map/all_to_all | solution.py:368
  42.8 8.1 %grads.1 = (f32[512,640]{1,0:T(8,128)}, f32[512,128]{1,0:T(8,128)}, f32[512,128]{1,0:T(8,128)}) custom-call(bf16[512,640]{1,0:T(8,128)(2,1)S(1)} %get-tuple-element.22.q_ref, bf16[512,640]{1,0:T(8,128)(2,1)S(1)} %get-tuple-element.24.g_ref, bf16[512,128]{1,0:T(8,128)(2,1)} %k_ref.3, bf16[512,128]{1,0:T(8,128)(2,1)} %v_ref.3, ...), custom_call_target="tpu_custom_call" | custom-call | flops 1342177280 | bytes 8388608 | tf_op jit(solution)/shard_map/grads/pallas_call | solution.py:371
  50.9 4.9 %all-to-all-done.1 = bf16[16,32,256]{2,1,0:T(8,128)(2,1)S(1)} async-done(((bf16[16,32,256]{2,1,0:T(8,128)(2,1)}), bf16[16,32,256]{2,1,0:T(8,128)(2,1)S(1)}, u32[]{:S(2)}, u32[]{:S(2)}) %all-to-all-start.1) | async-done | bytes 262176 | tf_op jit(solution)/shard_map/all_to_all | solution.py:368
  55.9 0.6 %fusion = (f32[32,128]{1,0:T(8,128)}, f32[32,128]{1,0:T(8,128)}) fusion(f32[32,256]{1,0:T(8,128)S(1)} %convert_reduce_fusion), kind=kLoop, calls=%fused_computation.3 | loop fusion | bytes 65536 | tf_op jit(solution)/shard_map/slice | solution.py:394
  (1 shorter events, 0.0 us)
Async XLA Ops:
  2.1 21.1 %all-to-all-start = ((bf16[16,32,256]{2,1,0:T(8,128)(2,1)}), bf16[16,32,256]{2,1,0:T(8,128)(2,1)S(1)}, u32[]{:S(2)}, u32[]{:S(2)}) async-start(bf16[16,32,256]{2,1,0:T(8,128)(2,1)} %broadcast_in_dim.2), calls=%async_computation | async-start | bytes 524288 | tf_op jit(solution)/shard_map/all_to_all | solution.py:307
  23.1 3.4 %collective-permute-start = (bf16[512,256]{1,0:T(8,128)(2,1)S(1)}, bf16[512,256]{1,0:T(8,128)(2,1)S(1)}, u32[]{:S(2)}, u32[]{:S(2)}) collective-permute-start(bf16[512,256]{1,0:T(8,128)(2,1)S(1)} %bitcast.2), channel_id=1, source_target_pairs={{0,4},{4,0},{8,12},{12,8},{16,20},{20,16},{24,28},{28,24},{32,36},... | collective-permute-start | bytes 786440 | tf_op jit(solution)/shard_map/ppermute | solution.py:326
  35.1 3.4 %collective-permute-start.1 = (bf16[512,256]{1,0:T(8,128)(2,1)S(1)}, bf16[512,256]{1,0:T(8,128)(2,1)S(1)}, u32[]{:S(2)}, u32[]{:S(2)}) collective-permute-start(bf16[512,256]{1,0:T(8,128)(2,1)S(1)} %get-tuple-element.36), channel_id=1, source_target_pairs={{0,4},{4,0},{8,12},{12,8},{16,20},{20,16},{24,28},{28,24},{32,36},... | collective-permute-start | bytes 786440 | tf_op jit(solution)/shard_map/ppermute | solution.py:357
  39.3 16.6 %all-to-all-start.1 = ((bf16[16,32,256]{2,1,0:T(8,128)(2,1)}), bf16[16,32,256]{2,1,0:T(8,128)(2,1)S(1)}, u32[]{:S(2)}, u32[]{:S(2)}) async-start(bf16[16,32,256]{2,1,0:T(8,128)(2,1)} %bitcast.1), calls=%async_computation.1 | async-start | bytes 524288 | tf_op jit(solution)/shard_map/all_to_all | solution.py:368

commit v9 on v8

--- a/solution.py
+++ b/solution.py
@@ -38,6 +38,20 @@
 
 def lanes(head):
     return pl.ds(pl.multiple_of(head * HD, HD), HD)
+
+
+def spread_kernel(k_ref, v_ref, out_ref, sems):
+    copies = [
+        pltpu.make_async_copy(
+            src, out_ref.at[chip, :, pl.ds(i * HD, HD)], sems.at[2 * chip + i]
+        )
+        for chip in range(out_ref.shape[0])
+        for i, src in enumerate((k_ref, v_ref))
+    ]
+    for copy in copies:
+        copy.start()
+    for copy in copies:
+        copy.wait()
 
 
 def own_stats_kernel(
@@ -300,10 +314,14 @@
     chips = devices // 2
     swap = [(d, d ^ 1) for d in range(devices)]
     same_core = [[2 * chip + core for chip in range(chips)] for core in range(2)]
-    side_by_side = jnp.pad(prompt_keys, ((0, 0), (0, HD))) + jnp.pad(
-        prompt_values, ((0, 0), (HD, 0))
-    )
-    spread = jnp.broadcast_to(side_by_side[None], (chips, SHARD, 2 * HD))
+    spread = pl.pallas_call(
+        spread_kernel,
+        in_specs=[pl.BlockSpec(memory_space=pltpu.HBM)] * 2,
+        out_specs=pl.BlockSpec(memory_space=pltpu.HBM),
+        out_shape=hbm_struct((chips, SHARD, 2 * HD), BF16),
+        scratch_shapes=[pltpu.SemaphoreType.DMA((2 * chips,))],
+        name="spread",
+    )(hbm(prompt_keys), hbm(prompt_values))
     mine = lax.all_to_all(spread, "comp", 0, 0, axis_index_groups=same_core, tiled=True)
     mine = mine.reshape(half, 2 * HD)
 

time: 57.1 us -> 64.9 us (1.14)
  Pallas kernels: 22.1 us -> 31.4 us
  local copies, waits for them, and re-layouts: 1.34 us -> 0.61 us
  other arithmetic: 1.52 us -> 0.8 us
    pallas_call x0 -> x1, Pallas kernels: none -> 9.34 us  [per_device(): pl.pallas_call(spread_kernel, in_specs=[pl.BlockSpec(memory_space=pltpu.H...]
    broadcast_in_dim x1 -> x0, local copies, waits for them, and re-layouts: 0.73 us -> none  [per_device(): spread = jnp.broadcast_to(side_by_side[None], (chips, SHARD, 2 * HD))]
    add x1 -> x0, other arithmetic: 0.72 us -> none  [per_device(): jnp.pad(prompt_keys, ((0, 0), (0, HD)))]
  transfers between devices with their start and end apart: 4 -> 4, of which waited for: 4 -> 4; matrix products, arithmetic and copies ran while one was open for 0% -> 0% of each run, Pallas kernels for 24% -> 21%
where the time goes in v9:
time: 64.9 us; the launch traced here: 64.4 us
  Pallas kernels  31.4 us (48%)
  starting transfers between devices  16.5 us (25%)
  waiting for transfers between devices  13.6 us (21%)
  between operations  1.35 us (2%)
  other arithmetic  0.8 us (1%)
    pallas_call x1, Pallas kernels, per_device(): pl.pallas_call(spread_kernel, in_specs=[pl.BlockSpec(memory_space=pltpu.H...  9.34 us
    all_to_all x1, starting transfers between devices, per_device(): lax.all_to_all(spread, 'comp', 0, 0, axis_index_groups=same_core, tiled=T...  9.03 us
    pallas_call x1, Pallas kernels, per_device(): pl.pallas_call(prompt_kernel, in_specs=[VMEM] * 7, out_specs=[pl.BlockSpe...  8.48 us
    pallas_call x1, Pallas kernels, per_device(): pl.pallas_call(grads_kernel, grid=(GROUP,), in_specs=[VMEM, VMEM, whole((...  8.1 us
    all_to_all x1, waiting for transfers between devices, per_device(): lax.all_to_all(spread, 'comp', 0, 0, axis_index_groups=same_core, tiled=T...  6.82 us
    all_to_all x1, waiting for transfers between devices, per_device(): lax.all_to_all(total, 'comp', 0, 0, axis_index_groups=same_core, tiled=True)  4.92 us
    pallas_call x1, Pallas kernels, per_device(): pl.pallas_call(own_stats_kernel, grid=(GROUP,), in_specs=[SMEM, HEAD, HEA...  4.56 us
    all_to_all x1, starting transfers between devices, per_device(): lax.all_to_all(total, 'comp', 0, 0, axis_index_groups=same_core, tiled=True)  3.53 us
  transfers between devices with their start and end apart: 4, of which 4 were waited for; matrix products, arithmetic and copies ran while one was open for 0% of the time, Pallas kernels for 21%

profile of v9, /device:TPU:6, one launch (start us, length us, event | category | flops | bytes accessed | tf_op | source)
XLA Modules:
  0.0 64.4 jit_solution(16662840941933825789)
XLA Ops:
  0.6 9.3 %spread.1 = bf16[16,32,256]{2,1,0:T(8,128)(2,1)} custom-call(bf16[32,128]{1,0:T(8,128)(2,1)} %k_ref.4, bf16[32,128]{1,0:T(8,128)(2,1)} %v_ref.4), custom_call_target="tpu_custom_call" | custom-call | tf_op jit(solution)/shard_map/spread/pallas_call | solution.py:317
  10.0 9.0 %all-to-all-start = ((bf16[16,32,256]{2,1,0:T(8,128)(2,1)}), bf16[16,32,256]{2,1,0:T(8,128)(2,1)S(1)}, u32[]{:S(2)}, u32[]{:S(2)}) async-start(bf16[16,32,256]{2,1,0:T(8,128)(2,1)} %spread.1), calls=%async_computation | async-start | bytes 524288 | tf_op jit(solution)/shard_map/all_to_all | solution.py:325
  19.7 4.6 %own_stats.1 = (bf16[512,640]{1,0:T(8,128)(2,1)S(1)}, bf16[512,640]{1,0:T(8,128)(2,1)S(1)}, f32[5,1,512]{2,1,0:T(1,128)S(1)}, f32[5,1,512]{2,1,0:T(1,128)S(1)}, f32[5,1,512]{2,1,0:T(1,128)S(1)}) custom-call(s32[1]{0:T(128)S(6)} %copy.12.len_ref, bf16[512,640]{1,0:T(8,128)(2,1)} %q_ref.1, bf16[512,640]{1,0:T(8,128)(2,1)} %g_ref.1, bf16[512,128]{1,0:T(8,128)(2,1)} %k_ref.5, ...), custom_call_target="tpu_custom_call" | custom-call | flops 503316480 | bytes 2097152 | tf_op jit(solution)/shard_map/own_stats/pallas_call | solution.py:329
  24.2 6.8 %all-to-all-done = bf16[16,32,256]{2,1,0:T(8,128)(2,1)S(1)} async-done(((bf16[16,32,256]{2,1,0:T(8,128)(2,1)}), bf16[16,32,256]{2,1,0:T(8,128)(2,1)S(1)}, u32[]{:S(2)}, u32[]{:S(2)}) %all-to-all-start) | async-done | bytes 262176 | tf_op jit(solution)/shard_map/all_to_all | solution.py:325
  31.0 1.9 %collective-permute-start = (bf16[512,256]{1,0:T(8,128)(2,1)S(1)}, bf16[512,256]{1,0:T(8,128)(2,1)S(1)}, u32[]{:S(2)}, u32[]{:S(2)}) collective-permute-start(bf16[512,256]{1,0:T(8,128)(2,1)S(1)} %bitcast.2), channel_id=1, source_target_pairs={{0,4},{4,0},{8,12},{12,8},{16,20},{20,16},{24,28},{28,24},{32,36},... | collective-permute-start | bytes 786440 | tf_op jit(solution)/shard_map/ppermute | solution.py:344
  33.0 1.5 %collective-permute-done.other_ref = bf16[512,256]{1,0:T(8,128)(2,1)S(1)} collective-permute-done((bf16[512,256]{1,0:T(8,128)(2,1)S(1)}, bf16[512,256]{1,0:T(8,128)(2,1)S(1)}, u32[]{:S(2)}, u32[]{:S(2)}) %collective-permute-start) | collective-permute-done | bytes 262176 | tf_op jit(solution)/shard_map/ppermute | solution.py:344
  34.5 8.5 %prompt.1 = (bf16[5,1024,512]{2,1,0:T(8,128)(2,1)}, f32[512,256]{1,0:T(8,128)S(1)}, bf16[512,256]{1,0:T(8,128)(2,1)S(1)}, f32[5,1,512]{2,1,0:T(1,128)S(1)}, f32[...) custom-call(bf16[512,640]{1,0:T(8,128)(2,1)S(1)} %get-tuple-element.22.q_ref, ...), custom_call_target="tpu_custom_call" | custom-call | flops 2684354560 | bytes 8388608 | tf_op jit(solution)/shard_map/prompt/pallas_call | solution.py:347
  43.0 2.0 %collective-permute-start.1 = (bf16[512,256]{1,0:T(8,128)(2,1)S(1)}, bf16[512,256]{1,0:T(8,128)(2,1)S(1)}, u32[]{:S(2)}, u32[]{:S(2)}) collective-permute-start(bf16[512,256]{1,0:T(8,128)(2,1)S(1)} %get-tuple-element.36), channel_id=1, source_target_pairs={{0,4},{4,0},{8,12},{12,8},{16,20},{20,16},{24,28},{28,24},{32,36},... | collective-permute-start | bytes 786440 | tf_op jit(solution)/shard_map/ppermute | solution.py:375
  45.0 1.0 %keep.1 = f32[512,256]{1,0:T(8,128)S(1)} custom-call(bf16[512,640]{1,0:T(8,128)(2,1)S(1)} %get-tuple-element.22.q_ref, bf16[512,640]{1,0:T(8,128)(2,1)S(1)} %get-tuple-element.24.g_ref, bf16[3,512,512]{2,1,0:T(8,128)(2,1)S(1)} %get-tuple-element.33.p_ref, bf16[3,512,512]{2,1,0:T(8,128)(2,1)S(1)} %get-tuple-element.34.d_ref, ...), custom_call_target="tpu_custom_call" | custom-call | flops 402653184 | bytes 4194304 | tf_op jit(solution)/shard_map/keep/pallas_call | solution.py:376
  46.0 0.4 collective-permute-done.1
  46.4 0.8 %add_convert_fusion = bf16[512,256]{1,0:T(8,128)(2,1)} fusion(f32[512,256]{1,0:T(8,128)S(1)} %keep.1, bf16[512,256]{1,0:T(8,128)(2,1)S(1)} %collective-permute-done.1), kind=kLoop, calls=%fused_computation.1 | loop fusion | flops 393216 | bytes 1048576 | tf_op jit(solution)/shard_map/convert_element_type | solution.py:385
  47.1 3.5 %all-to-all-start.1 = ((bf16[16,32,256]{2,1,0:T(8,128)(2,1)}), bf16[16,32,256]{2,1,0:T(8,128)(2,1)S(1)}, u32[]{:S(2)}, u32[]{:S(2)}) async-start(bf16[16,32,256]{2,1,0:T(8,128)(2,1)} %bitcast.1), calls=%async_computation.1 | async-start | bytes 524288 | tf_op jit(solution)/shard_map/all_to_all | solution.py:386
  50.7 8.1 %grads.1 = (f32[512,640]{1,0:T(8,128)}, f32[512,128]{1,0:T(8,128)}, f32[512,128]{1,0:T(8,128)}) custom-call(bf16[512,640]{1,0:T(8,128)(2,1)S(1)} %get-tuple-element.22.q_ref, bf16[512,640]{1,0:T(8,128)(2,1)S(1)} %get-tuple-element.24.g_ref, bf16[512,128]{1,0:T(8,128)(2,1)} %k_ref.5, bf16[512,128]{1,0:T(8,128)(2,1)} %v_ref.5, ...), custom_call_target="tpu_custom_call" | custom-call | flops 1342177280 | bytes 8388608 | tf_op jit(solution)/shard_map/grads/pallas_call | solution.py:389
  58.8 4.9 %all-to-all-done.1 = bf16[16,32,256]{2,1,0:T(8,128)(2,1)S(1)} async-done(((bf16[16,32,256]{2,1,0:T(8,128)(2,1)}), bf16[16,32,256]{2,1,0:T(8,128)(2,1)S(1)}, u32[]{:S(2)}, u32[]{:S(2)}) %all-to-all-start.1) | async-done | bytes 262176 | tf_op jit(solution)/shard_map/all_to_all | solution.py:386
  63.7 0.6 fusion
  (1 shorter events, 0.0 us)
Async XLA Ops:
  10.0 21.1 %all-to-all-start = ((bf16[16,32,256]{2,1,0:T(8,128)(2,1)}), bf16[16,32,256]{2,1,0:T(8,128)(2,1)S(1)}, u32[]{:S(2)}, u32[]{:S(2)}) async-start(bf16[16,32,256]{2,1,0:T(8,128)(2,1)} %spread.1), calls=%async_computation | async-start | bytes 524288 | tf_op jit(solution)/shard_map/all_to_all | solution.py:325
  31.0 3.4 %collective-permute-start = (bf16[512,256]{1,0:T(8,128)(2,1)S(1)}, bf16[512,256]{1,0:T(8,128)(2,1)S(1)}, u32[]{:S(2)}, u32[]{:S(2)}) collective-permute-start(bf16[512,256]{1,0:T(8,128)(2,1)S(1)} %bitcast.2), channel_id=1, source_target_pairs={{0,4},{4,0},{8,12},{12,8},{16,20},{20,16},{24,28},{28,24},{32,36},... | collective-permute-start | bytes 786440 | tf_op jit(solution)/shard_map/ppermute | solution.py:344
  43.0 3.4 %collective-permute-start.1 = (bf16[512,256]{1,0:T(8,128)(2,1)S(1)}, bf16[512,256]{1,0:T(8,128)(2,1)S(1)}, u32[]{:S(2)}, u32[]{:S(2)}) collective-permute-start(bf16[512,256]{1,0:T(8,128)(2,1)S(1)} %get-tuple-element.36), channel_id=1, source_target_pairs={{0,4},{4,0},{8,12},{12,8},{16,20},{20,16},{24,28},{28,24},{32,36},... | collective-permute-start | bytes 786440 | tf_op jit(solution)/shard_map/ppermute | solution.py:375
  47.1 16.6 %all-to-all-start.1 = ((bf16[16,32,256]{2,1,0:T(8,128)(2,1)}), bf16[16,32,256]{2,1,0:T(8,128)(2,1)S(1)}, u32[]{:S(2)}, u32[]{:S(2)}) async-start(bf16[16,32,256]{2,1,0:T(8,128)(2,1)} %bitcast.1), calls=%async_computation.1 | async-start | bytes 524288 | tf_op jit(solution)/shard_map/all_to_all | solution.py:386
